TPU v7x, 32 devices: a whole 2x2x4 slice. The times are simulated.
32 devices in a mesh: dp: 16 (over z, x, core), tensor: 2 (over y).
Axes of the slice: x: 2, y: 2, z: 4, core: 2. Of those that a mesh axis runs over, the one named last changes fastest.
Arguments:
- queries: bfloat16 [16384, 4096], P('dp', 'tensor'), may hold values from -6 to 6
- out_grad: bfloat16 [16384, 4096], P('dp', 'tensor'), may hold values from -6 to 6
- target_len: int32 [16], P('dp'), may hold values from 1 to 1024, 12288 in all
- encoded: bfloat16 [2048, 4096], P('dp', 'tensor'), may hold values from -6 to 6
- row_owner: int32 [2048, 1], P('dp'), may hold values from 0 to 15; in each aligned block of 128 rows (0 to 127, 128 to 255, ...) at most 16 rows name the same one
- projections: bfloat16 [2, 4096, 4096], P(None, 'dp', 'tensor'), may hold values from -0.09375 to 0.09375
- velocity: float32 [2, 4096, 4096], P(None, 'dp', 'tensor'), may hold values from -0.046875 to 0.046875
Outputs:
- query_grad: bfloat16 [16384, 4096], P('dp', 'tensor')
- encoded_grad: bfloat16 [2048, 4096], P('dp', 'tensor')
Inputs may be any that keep to these rules, and one draw needn't show every extreme that they name: row_owner[r, 0] names the sample whose decoder positions attend to encoder row r; sample s has its 1024 query rows on index s of dp. Among the 128 rows of one index of dp at most 16 name the same sample, exactly 16 do for some sample, and every sample is named by some row. `target_len`: some sample has all 1024 positions live.
All inputs are finite; a program needn't handle non-finite values. No bound on the sum of `target_len` on one device may be relied on, other than what follows from the above.
Results may differ from a plain program's by a relative error of at most 0.014.
Values may be sent and summed in bfloat16 or wider, within the bound.
No kernel may reach another device: no remote copies, remote signals or barrier semaphores. Data moves between devices by JAX's collectives and lax.ppermute only.
A program may use at most 128 MiB of HBM per device.

v0:
```python
import math

import jax
import jax.numpy as jnp
from jax import lax
from jax.sharding import PartitionSpec as P

HD = 256


cap_limit = 10.0


def slot_table(labels, capacity, peer_count):
    targets = (labels[:, None] == jnp.arange(peer_count, dtype=jnp.int32)[None, :]).astype(
        jnp.int32
    )
    before = jnp.cumsum(targets, axis=0) - targets
    rank_in = jnp.sum(before * targets, axis=1)
    slot_index = labels * capacity + rank_in
    placement = jnp.arange(peer_count * capacity, dtype=jnp.int32)[:, None] == slot_index[None, :]
    return placement.astype(jnp.bfloat16)


def to_home(placement, incoming):
    return lax.dot_general(
        placement, incoming, (((0,), (0,)), ((), ())), preferred_element_type=jnp.float32
    )


def attend_back(query_rows, grad_rows, key_rows, value_rows, usable):
    block_rows = query_rows.shape[0]
    slot_count = key_rows.shape[0]
    head_count = query_rows.shape[1] // HD
    score_scale = 1.0 / math.sqrt(HD)
    query_heads = query_rows.reshape(block_rows, head_count, HD)
    grad_heads = grad_rows.reshape(block_rows, head_count, HD)
    key_heads = key_rows.reshape(slot_count, head_count, HD)
    value_heads = value_rows.reshape(slot_count, head_count, HD)
    raw_scores = (
        jnp.einsum("qhd,khd->hqk", query_heads, key_heads, preferred_element_type=jnp.float32)
        * score_scale
    )
    capped = cap_limit * jnp.tanh(raw_scores / cap_limit)
    exp_terms = jnp.exp(capped) * usable[None, None, :]
    attention = exp_terms / jnp.sum(exp_terms, axis=-1, keepdims=True)
    prob_grad = jnp.einsum(
        "qhd,khd->hqk", grad_heads, value_heads, preferred_element_type=jnp.float32
    )
    row_term = jnp.sum(attention * prob_grad, axis=-1, keepdims=True)
    score_grad = (
        attention * (prob_grad - row_term) * (1.0 - (capped / cap_limit) ** 2) * score_scale
    ).astype(jnp.bfloat16)
    rounded_attention = attention.astype(jnp.bfloat16)
    query_block = jnp.einsum(
        "hqk,khd->qhd", score_grad, key_heads, preferred_element_type=jnp.float32
    )
    key_block = jnp.einsum(
        "hqk,qhd->khd", score_grad, query_heads, preferred_element_type=jnp.float32
    )
    value_block = jnp.einsum(
        "hqk,qhd->khd", rounded_attention, grad_heads, preferred_element_type=jnp.float32
    )
    width_all = head_count * HD
    return (
        query_block.reshape(block_rows, width_all).astype(jnp.bfloat16),
        key_block.reshape(slot_count, width_all),
        value_block.reshape(slot_count, width_all),
    )


def attend_all(queries, live_grad, key_rows, value_rows, usable):
    query_count = queries.shape[0]
    block_rows = min(512, query_count)
    key_total = jnp.zeros(key_rows.shape, jnp.float32)
    value_total = jnp.zeros(value_rows.shape, jnp.float32)
    query_parts = []
    for first_row in range(0, query_count, block_rows):
        query_block, key_block, value_block = attend_back(
            queries[first_row : first_row + block_rows],
            live_grad[first_row : first_row + block_rows],
            key_rows,
            value_rows,
            usable,
        )
        query_parts.append(query_block)
        key_total = key_total + key_block
        value_total = value_total + value_block
    query_grad = jnp.concatenate(query_parts, axis=0)
    pair_grad = jnp.stack((key_total, value_total), axis=1).astype(jnp.bfloat16)
    return (query_grad, pair_grad)


def on_device(queries, out_grad, target_len, encoded, row_owner, projections, velocity):
    peer_count = lax.axis_size("dp")
    stored_rows = encoded.shape[0]
    capacity = max(2, 2 * stored_rows // peer_count)
    predicted = (projections.astype(jnp.float32) - velocity).astype(jnp.bfloat16)
    gathered = lax.all_gather(predicted, "dp", axis=1, tiled=True)
    alive_rows = jnp.arange(queries.shape[0], dtype=jnp.int32) < target_len[0]
    live_grad = jnp.where(alive_rows[:, None], out_grad, jnp.zeros_like(out_grad))
    placement = slot_table(row_owner[:, 0], capacity, peer_count)
    filled = jnp.sum(placement.astype(jnp.float32), axis=1).astype(jnp.bfloat16)
    outgoing = jnp.dot(placement, encoded, preferred_element_type=jnp.float32).astype(jnp.bfloat16)
    incoming, incoming_flag = (
        lax.all_to_all(outgoing, "dp", split_axis=0, concat_axis=0, tiled=True),
        lax.all_to_all(filled, "dp", split_axis=0, concat_axis=0, tiled=True),
    )
    full_rows = lax.all_gather(incoming, "tensor", axis=1, tiled=True)
    key_value = jnp.einsum(
        "rd,kdg->rkg", full_rows, gathered, preferred_element_type=jnp.float32
    ).astype(jnp.bfloat16)
    usable = (incoming_flag.astype(jnp.float32) > 0.5).astype(jnp.float32)
    query_grad, pair_grad = attend_all(queries, live_grad, key_value[:, 0], key_value[:, 1], usable)
    partial_value = jnp.einsum(
        "rkg,kdg->rd", pair_grad, gathered, preferred_element_type=jnp.float32
    )
    summed = lax.psum_scatter(
        partial_value.astype(jnp.bfloat16), "tensor", scatter_dimension=1, tiled=True
    )
    returned = lax.all_to_all(summed, "dp", split_axis=0, concat_axis=0, tiled=True)
    encoded_grad = to_home(placement, returned).astype(jnp.bfloat16)
    return (query_grad, encoded_grad)


def solution(mesh):
    in_specs = (
        P("dp", "tensor"),
        P("dp", "tensor"),
        P("dp"),
        P("dp", "tensor"),
        P("dp", None),
        P(None, "dp", "tensor"),
        P(None, "dp", "tensor"),
    )
    out_specs = (P("dp", "tensor"), P("dp", "tensor"))
    return jax.shard_map(
        on_device, mesh=mesh, in_specs=in_specs, out_specs=out_specs, check_vma=False
    )
```

profile of v0, /device:TPU:0, one launch (start us, length us, event | category | flops | bytes accessed | tf_op | source)
XLA Modules:
  0.0 400.9 jit_solution(8685719519346796365)
XLA Ops:
  7.2 0.0 all-gather.3.cloned.1.call-start
  7.2 0.9 fusion.55
  8.1 0.2 reduce_window_sum.11
  8.3 0.8 select_reduce_fusion
  9.1 0.7 multiply_add_fusion
  9.8 0.4 convolution_convert_fusion.1
  10.2 32.1 %all_to_all.34 = bf16[16,16,2048]{2,1,0:T(8,128)(2,1)} all-to-all(bf16[16,16,2048]{2,1,0:T(8,128)(2,1)S(1)} %bitcast.135), channel_id=1, replica_groups=mesh['dp'=16,'tensor'=2] {'dp'}, dimensions={0} | all-to-all | bytes 2097152 | tf_op jit(solution)/shard_map/all_to_all | solution.py:106
  42.4 0.0 all-gather.5.cloned.1.call-start
  42.4 4.2 %subtract_convert_fusion = bf16[2,256,2048]{2,1,0:T(8,128)(2,1)} fusion(f32[2,256,2048]{2,1,0:T(8,128)} %param.13, bf16[2,256,2048]{2,1,0:T(8,128)(2,1)S(1)} %copy-done.7), kind=kLoop, calls=%fused_computation.23 | loop fusion | flops 3145728 | bytes 8388608 | tf_op jit(solution)/shard_map/convert_element_type | solution.py:98
  46.7 0.1 fusion.52
  46.8 0.7 all_to_all.30
  47.5 5.0 %all-to-all-start.1 = ((bf16[16,16,1]{1,2,0:T(2,128)(2,1)}), bf16[16,16,1]{1,2,0:T(2,128)(2,1)S(1)}, u32[]{:S(2)}, u32[]{:S(2)}) async-start(bf16[16,16,1]{1,2,0:T(2,128)(2,1)} %all_to_all.30), calls=%async_computation.1 | async-start | bytes 16384 | tf_op jit(solution)/shard_map/all_to_all | solution.py:107
  52.5 0.0 reduce-scatter.2.cloned.1.call-start
  52.5 6.4 %copy.80 = bf16[1024,2048]{0,1:T(8,128)(2,1)} copy(bf16[1024,2048]{1,0:T(8,128)(2,1)} %param.8) | data formatting | bytes 8388608 | tf_op args[1]
  59.6 4.9 %fusion.75 = (bf16[512,2048]{1,0:T(8,128)(2,1)}, bf16[512,2048]{1,0:T(8,128)(2,1)}) fusion(bf16[1024,2048]{1,0:T(8,128)(2,1)} %param.7), kind=kLoop, calls=%fused_computation.82 | loop fusion | bytes 8388608 | tf_op jit(solution)/shard_map/slice | solution.py:80
  64.5 0.3 broadcast_select_fusion
  64.8 2.3 fusion.74
  67.2 2.9 copy.111
  70.0 3.9 copy.110
  74.0 0.1 reshape.100
  74.1 1.9 all-gather.3.cloned.1.call-done
  76.0 169.7 %all-gather.5.cloned.1.call-done = bf16[2,4096,2048]{2,1,0:T(8,128)(2,1)} async-done(((bf16[2,256,2048]{2,1,0:T(8,128)(2,1)}), bf16[2,4096,2048]{2,1,0:T(8,128)(2,1)}) %all-gather.5.cloned.1.call-update) | async-done | bytes 33554448 | tf_op jit(solution)/shard_map/all_gather | solution.py:99
  245.6 15.6 %convolution_convert_fusion = bf16[256,2,2048]{2,0,1:T(8,128)(2,1)S(1)} fusion(bf16[2,4096,2048]{2,1,0:T(8,128)(2,1)} %all-gather.5.cloned.1.call-done, bf16[256,4096]{1,0:T(8,128)(2,1)} %all-gather.3.cloned.1.call-done), kind=kOutput, calls=%fused_computation.25 | convolution fusion | flops 8590983168 | bytes 37748736 | tf_op jit(solution)/shard_map/rd,kdg->rkg/dot_general | solution.py:110
  261.3 0.1 fusion.76
  261.4 0.3 copy.112
  261.8 0.3 copy.113
  262.1 0.8 copy-done.3
  262.9 2.7 fusion.43
  265.6 2.8 fusion.45
  268.3 0.7 fusion.47
  269.1 0.9 copy-done.6
  269.9 4.2 %bitcast_reduce_fusion.1 = (f32[8,512]{1,0:T(8,128)S(1)}, f32[8,512]{1,0:T(8,128)S(1)}, f32[8,256,512]{2,1,0:T(8,128)}) fusion(f32[256]{0:T(256)S(1)} %reshape.100, f32[8,256,512]{2,1,0:T(8,128)S(1)} %fusion.47, bf16[512,8,256]{0,2,1:T(8,128)(2,1)S(1)} %bitcast.139, bf16[256,8,256]{2,1,0:T(8,128)(2,1)S(1)} %bitcast.126), kind=kOutput, calls=%fused_computation.14 | convolution fusion | flops 545251328 | bytes 11568128 | tf_op jit(solution)/shard_map/qhd,khd->hqk/dot_general | solution.py:41
  274.2 2.8 fusion.17
  277.0 11.5 %fusion.22 = f32[8,256,256]{1,2,0:T(8,128)} fusion(bf16[512,8,256]{0,2,1:T(8,128)(2,1)} %bitcast.138, f32[8,512,256]{1,2,0:T(8,128)} %fusion.43, f32[8,256,512]{2,1,0:T(8,128)} %get-tuple-element.10, f32[256]{0:T(256)S(1)} %reshape.100, f32[8,512]{1,0:T(8,128)S(1)} %get-tuple-element.2), kind=kOutput, calls=%fused_computation.38 | convolution fusion | flops 553652480 | bytes 12600320 | tf_op jit(solution)/shard_map/hqk,qhd->khd/dot_general | solution.py:58
  288.5 10.6 %add_convert_fusion.1 = bf16[8,256,256]{1,2,0:T(8,128)(2,1)} fusion(f32[8,256,256]{1,2,0:T(8,128)} %fusion.22, bf16[512,8,256]{0,2,1:T(8,128)(2,1)S(1)} %bitcast.129, f32[8,512,256]{1,2,0:T(8,128)} %fusion.45, f32[8,256,512]{2,1,0:T(8,128)} %copy-done.5, f32[256]{0:T(256)S(1)} %reshape.100, f32[8,512]{1,0:T(8,128)S(1)} %get-tuple-element.3), kind=kOutput, calls=%fused_computation.37 | convolution fusion | flops 554701056 | bytes 13648896 | tf_op jit(solution)/shard_map/hqk,qhd->khd/dot_general | solution.py:58
  299.0 1.5 copy.98
  300.5 6.1 %add_convert_fusion = bf16[8,256,256]{2,1,0:T(8,128)(2,1)} fusion(f32[8,256,256]{2,1,0:T(8,128)} %fusion.17, bf16[512,8,256]{0,2,1:T(8,128)(2,1)} %bitcast.130, f32[8,256,512]{2,1,0:T(8,128)} %get-tuple-element.10, f32[256]{0:T(256)S(1)} %reshape.100, f32[8,512]{1,0:T(8,128)S(1)} %get-tuple-element.2), kind=kOutput, calls=%fused_computation.32 | convolution fusion | flops 543162368 | bytes 9454592 | tf_op jit(solution)/shard_map/hqk,qhd->khd/dot_general | solution.py:61
  306.6 1.5 copy.99
  308.1 15.8 %fusion.2 = bf16[256,4096]{1,0:T(8,128)(2,1)} fusion(bf16[2,4096,2048]{2,1,0:T(8,128)(2,1)} %all-gather.5.cloned.1.call-done, bf16[256,1,2048]{2,0,1:T(8,128)(2,1)S(1)} %copy.99, bf16[256,1,2048]{2,0,1:T(8,128)(2,1)S(1)} %copy.98), kind=kOutput, calls=%fused_computation.3 | convolution fusion | flops 8592031744 | bytes 37748736 | tf_op jit(solution)/shard_map/rkg,kdg->rd/dot_general | solution.py:115
  323.9 31.9 %reduce-scatter.2.cloned.1.call-done = bf16[256,2048]{1,0:T(8,128)(2,1)} async-done(((bf16[256,4096]{1,0:T(8,128)(2,1)}), bf16[256,2048]{1,0:T(8,128)(2,1)}) %reduce-scatter.2.cloned.1.call-update) | async-done | bytes 1048592 | tf_op jit(solution)/shard_map/reduce_scatter | solution.py:118
  355.8 5.7 %all-to-all-start.2 = ((bf16[16,16,2048]{2,1,0:T(8,128)(2,1)}), bf16[16,16,2048]{2,1,0:T(8,128)(2,1)}, u32[]{:S(2)}, u32[]{:S(2)}) async-start(bf16[16,16,2048]{2,1,0:T(8,128)(2,1)} %bitcast.142), calls=%async_computation.3 | async-start | bytes 2097152 | tf_op jit(solution)/shard_map/all_to_all | solution.py:121
  361.5 0.8 copy.83
  362.3 9.2 %fusion.36 = bf16[8,256,512]{2,1,0:T(8,128)(2,1)} fusion(bf16[256,8,256]{0,2,1:T(8,128)(2,1)S(1)} %copy.83, f32[8,512,256]{1,2,0:T(8,128)} %fusion.43, f32[8,256,512]{2,1,0:T(8,128)} %get-tuple-element.10, f32[256]{0:T(256)S(1)} %reshape.100, f32[8,512]{1,0:T(8,128)S(1)} %get-tuple-element.2), kind=kOutput, calls=%fused_computation.43 | convolution fusion | flops 554701056 | bytes 11551744 | tf_op jit(solution)/shard_map/hqk,khd->qhd/dot_general | solution.py:55
  371.6 2.9 copy.92
  374.5 9.3 %fusion.33 = bf16[8,256,512]{2,1,0:T(8,128)(2,1)} fusion(bf16[256,8,256]{0,2,1:T(8,128)(2,1)} %copy-done.8, f32[8,512,256]{1,2,0:T(8,128)} %fusion.45, f32[8,256,512]{2,1,0:T(8,128)} %copy-done.5, f32[256]{0:T(256)S(1)} %reshape.100, f32[8,512]{1,0:T(8,128)S(1)} %get-tuple-element.3), kind=kOutput, calls=%fused_computation.42 | convolution fusion | flops 554701056 | bytes 11551744 | tf_op jit(solution)/shard_map/hqk,khd->qhd/dot_general | solution.py:55
  383.8 4.0 %copy.93 = bf16[512,2048]{1,0:T(8,128)(2,1)} copy(bf16[512,2048]{0,1:T(8,128)(2,1)} %bitcast.140) | data formatting | bytes 4194304 | tf_op jit(solution)/shard_map/convert_element_type | solution.py:66
  387.8 4.2 %pad_maximum_fusion = bf16[1024,2048]{1,0:T(8,128)(2,1)} fusion(bf16[512,2048]{1,0:T(8,128)(2,1)} %copy.93, bf16[512,2048]{1,0:T(8,128)(2,1)S(1)} %copy.92), kind=kLoop, calls=%fused_computation.4 | loop fusion | flops 8388608 | bytes 8388608 | tf_op jit(solution)/shard_map/concatenate | solution.py:89
  392.0 2.4 convolution_convert_fusion.2
  (23 shorter events, 0.1 us)
Async XLA Ops:
  7.2 2.6 copy-start
  7.2 35.2 %copy-start.7 = (bf16[2,256,2048]{2,1,0:T(8,128)(2,1)S(1)}, bf16[2,256,2048]{2,1,0:T(8,128)(2,1)}, u32[]{:S(2)}) copy-start(bf16[2,256,2048]{2,1,0:T(8,128)(2,1)} %param.12) | copy-start | bytes 6291460
  7.2 68.8 %all-gather.3.cloned.1.call-start = ((), (), s32[]{:S(2)}) async-start(), calls=%async_computation.4 | async-start | bytes 3145728 | tf_op jit(solution)/shard_map/all_gather | solution.py:109
  42.4 203.3 %all-gather.5.cloned.1.call-start = ((), (), s32[]{:S(2)}) async-start(), calls=%async_computation.5 | async-start | bytes 35651584 | tf_op jit(solution)/shard_map/all_gather | solution.py:99
  47.5 26.5 %all-to-all-start.1 = ((bf16[16,16,1]{1,2,0:T(2,128)(2,1)}), bf16[16,16,1]{1,2,0:T(2,128)(2,1)S(1)}, u32[]{:S(2)}, u32[]{:S(2)}) async-start(bf16[16,16,1]{1,2,0:T(2,128)(2,1)} %all_to_all.30), calls=%async_computation.1 | async-start | bytes 16384 | tf_op jit(solution)/shard_map/all_to_all | solution.py:107
  52.5 303.3 %reduce-scatter.2.cloned.1.call-start = ((), (), s32[]{:S(2)}) async-start(), calls=%async_computation.6 | async-start | bytes 3145728 | tf_op jit(solution)/shard_map/reduce_scatter | solution.py:118
  59.6 4.9 %copy-start.2 = (bf16[1024,2048]{0,1:T(8,128)(2,1)S(1)}, bf16[1024,2048]{0,1:T(8,128)(2,1)}, u32[]{:S(2)}) copy-start(bf16[1024,2048]{0,1:T(8,128)(2,1)} %copy.80) | copy-start | bytes 12582916
  261.3 1.6 copy-start.3
  262.1 3.5 copy-start.4
  268.3 1.6 copy-start.6
  269.0 5.1 %copy-start.5 = (f32[8,256,512]{2,1,0:T(8,128)}, f32[8,256,512]{2,1,0:T(8,128)S(1)}, u32[]{:S(2)}) copy-start(f32[8,256,512]{2,1,0:T(8,128)S(1)} %fusion.47) | copy-start | bytes 12582916
  355.8 36.1 %all-to-all-start.2 = ((bf16[16,16,2048]{2,1,0:T(8,128)(2,1)}), bf16[16,16,2048]{2,1,0:T(8,128)(2,1)}, u32[]{:S(2)}, u32[]{:S(2)}) async-start(bf16[16,16,2048]{2,1,0:T(8,128)(2,1)} %bitcast.142), calls=%async_computation.3 | async-start | bytes 2097152 | tf_op jit(solution)/shard_map/all_to_all | solution.py:121
  362.3 9.2 %copy-start.8 = (bf16[256,8,256]{0,2,1:T(8,128)(2,1)}, bf16[256,8,256]{0,2,1:T(8,128)(2,1)S(1)}, u32[]{:S(2)}) copy-start(bf16[256,8,256]{0,2,1:T(8,128)(2,1)S(1)} %copy.83) | copy-start | bytes 3145732
  383.8 10.6 %copy-start.1 = (bf16[128,2048]{1,0:T(8,128)(2,1)S(1)}, bf16[128,2048]{1,0:T(8,128)(2,1)}, u32[]{:S(2)}) copy-start(bf16[128,2048]{1,0:T(8,128)(2,1)} %param.10) | copy-start | bytes 1572868
Sparse Core Ops, SparseCore 0:
  42.5 33.4 all-gather.2
  77.5 168.0 all-gather.4
  324.0 31.7 reduce-scatter.1
where the time goes:
time: 402 us; the launch traced here: 401 us
  waiting for transfers between devices  204 us (51%)
  matrix products  94.1 us (23%)
  local copies, waits for them, and re-layouts  34.4 us (9%)
  blocking collectives  32.1 us (8%)
  between operations  14.6 us (4%)
  other arithmetic  11.4 us (3%)
  starting transfers between devices  10.8 us (3%)
    all_gather x1, waiting for transfers between devices, on_device(): gathered = lax.all_gather(predicted, 'dp', axis=1, tiled=True)  170 us
    all_to_all x1, blocking collectives, on_device(): lax.all_to_all(outgoing, 'dp', split_axis=0, concat_axis=0, tiled=True)  32.1 us
    reduce_scatter x1, waiting for transfers between devices, on_device(): lax.psum_scatter(partial_value.astype(jnp.bfloat16), 'tensor', scatter_di...  31.9 us
    dot_general x2, matrix products, attend_back(): jnp.einsum('hqk,qhd->khd', score_grad, query_heads, preferred_element_typ...  22 us
    dot_general x2, matrix products, attend_back(): jnp.einsum('hqk,khd->qhd', score_grad, key_heads, preferred_element_type=...  18.5 us
    dot_general x1, matrix products, on_device(): jnp.einsum('rkg,kdg->rd', pair_grad, gathered, preferred_element_type=jnp...  15.8 us
    dot_general x1, matrix products, on_device(): jnp.einsum('rd,kdg->rkg', full_rows, gathered, preferred_element_type=jnp...  15.6 us
    unnamed x23, local copies, waits for them, and re-layouts  15.5 us
  transfers between devices with their start and end apart: 5, of which 3 were waited for; matrix products, arithmetic and copies ran while one was open for 14% of the time, Pallas kernels for 0%

commit v1 on v0

v1 whole, which is shorter than its diff:
```python
import functools
import math

import jax
import jax.numpy as jnp
from jax import lax
from jax.experimental import pallas as pl
from jax.experimental.pallas import tpu as pltpu
from jax.sharding import PartitionSpec as P

HD = 256
CAP_LIMIT = 10.0
VMEM_LIMIT = 48 * 1024 * 1024


def slot_table(labels, capacity, peer_count):
    targets = (labels[:, None] == jnp.arange(peer_count, dtype=jnp.int32)[None, :]).astype(
        jnp.int32
    )
    before = jnp.cumsum(targets, axis=0) - targets
    rank_in = jnp.sum(before * targets, axis=1)
    slot_index = labels * capacity + rank_in
    placement = jnp.arange(peer_count * capacity, dtype=jnp.int32)[:, None] == slot_index[None, :]
    return placement.astype(jnp.bfloat16)


def split_heads(head_count):
    if head_count < 4:
        return [1] * head_count
    sizes = [2] * (head_count // 2)
    if head_count % 2:
        sizes.append(1)
    return sizes


def line_index(step, pos, line):
    return lax.rem(pos[0] - step + line, line)


def project_kernel(pos, rows, own, sibling, mine, other, total):
    step = pl.program_id(0)
    x, core = pos[1], pos[2]

    @pl.when(step == 0)
    def _():
        mine[...] = jnp.zeros_like(mine)
        total[...] = jnp.zeros_like(total)

    for x_at, result in ((1 - x, total), (x, mine)):
        from_own, from_sibling = rows[0, core, x_at], rows[0, 1 - core, x_at]
        for side in range(2):
            result[side] += jnp.dot(
                from_own, own[0, side], preferred_element_type=jnp.float32
            ) + jnp.dot(from_sibling, sibling[0, side], preferred_element_type=jnp.float32)

    @pl.when(step == pl.num_programs(0) - 1)
    def _():
        other[...] = total[...].astype(other.dtype)


def project(pos, rows, own, sibling, tensor_count):
    line, _, depth, width = own.shape
    slots = rows.shape[3]
    per_tensor = line // tensor_count

    def rows_at(step, pos):
        z = line_index(step, pos, line)
        shift = lax.rem(pos[3] - z // per_tensor + tensor_count, tensor_count)
        return (shift * per_tensor + lax.rem(z, per_tensor), 0, 0, 0, 0)

    weight_spec = pl.BlockSpec((1, 2, depth, width), lambda step, pos: (step, 0, 0, 0))
    whole = pl.BlockSpec((2, slots, width), lambda step, pos: (0, 0, 0))
    return pl.pallas_call(
        project_kernel,
        grid_spec=pltpu.PrefetchScalarGridSpec(
            num_scalar_prefetch=1,
            grid=(line,),
            in_specs=[
                pl.BlockSpec((1, 2, 2, slots, depth), rows_at),
                weight_spec,
                weight_spec,
            ],
            out_specs=[whole, whole],
            scratch_shapes=[pltpu.VMEM((2, slots, width), jnp.float32)],
        ),
        out_shape=(
            jax.ShapeDtypeStruct((2, slots, width), jnp.float32),
            jax.ShapeDtypeStruct((2, slots, width), jnp.bfloat16),
        ),
        compiler_params=pltpu.CompilerParams(vmem_limit_bytes=VMEM_LIMIT),
        cost_estimate=pl.CostEstimate(
            flops=2 * 2 * slots * 2 * line * depth * 2 * width,
            bytes_accessed=2 * own.size * 2 + rows.size * 2 + 6 * 2 * slots * width,
            transcendentals=0,
        ),
        name="project",
    )(pos, rows, own, sibling)


def attend_kernel(block, live, usable, queries, grads, mine, received, *rest):
    query_grad, pair_grad, key_total, value_total = rest[-4:]
    keys = (mine[0] + received[0].astype(jnp.float32)).astype(jnp.bfloat16)
    values = (mine[1] + received[1].astype(jnp.float32)).astype(jnp.bfloat16)
    scale = 1.0 / math.sqrt(HD)
    mask = usable[...]
    last_dims = (((1,), (1,)), ((), ()))
    query_count = queries.shape[0]
    for first in range(0, query_count, block):
        at = pl.ds(first, block)
        q = queries[at, :]
        position = first + lax.broadcasted_iota(jnp.int32, (block, 1), 0)
        g = grads[at, :]
        g = jnp.where(position < live[0], g, jnp.zeros_like(g))
        raw = lax.dot_general(keys, q, last_dims, preferred_element_type=jnp.float32)
        bent = jnp.tanh(raw * (scale / CAP_LIMIT))
        terms = jnp.exp(bent * CAP_LIMIT) * mask
        attention = terms * (1.0 / jnp.sum(terms, axis=0, keepdims=True))
        prob_grad = lax.dot_general(values, g, last_dims, preferred_element_type=jnp.float32)
        row_term = jnp.sum(attention * prob_grad, axis=0, keepdims=True)
        score_grad = (
            attention * (prob_grad - row_term) * ((1.0 - bent * bent) * scale)
        ).astype(jnp.bfloat16)
        rounded = attention.astype(jnp.bfloat16)
        query_grad[at, :] = lax.dot_general(
            score_grad, keys, (((0,), (0,)), ((), ())), preferred_element_type=jnp.float32
        ).astype(jnp.bfloat16)
        key_block = jnp.dot(score_grad, q, preferred_element_type=jnp.float32)
        value_block = jnp.dot(rounded, g, preferred_element_type=jnp.float32)
        if first == 0:
            key_total[...] = key_block
            value_total[...] = value_block
        else:
            key_total[...] += key_block
            value_total[...] += value_block
    pair_grad[0] = key_total[...].astype(jnp.bfloat16)
    pair_grad[1] = value_total[...].astype(jnp.bfloat16)


def attend(live, usable, queries, grads, mine, received, first_head, earlier):
    query_count, width = queries.shape
    _, slots, chunk = mine.shape
    heads = chunk // HD
    block = min(256, query_count)
    columns = pl.BlockSpec((query_count, HD), lambda head: (0, first_head + head))
    pair = pl.BlockSpec((2, slots, HD), lambda head: (0, 0, head))
    operands = [live, usable, queries, grads, mine, received]
    in_specs = [
        pl.BlockSpec(memory_space=pltpu.SMEM),
        pl.BlockSpec((slots, 1), lambda head: (0, 0)),
        columns,
        columns,
        pair,
        pair,
    ]
    aliases = {}
    if earlier is not None:
        aliases = {len(operands): 0}
        operands.append(earlier)
        in_specs.append(pl.BlockSpec(memory_space=pl.ANY))
    return pl.pallas_call(
        functools.partial(attend_kernel, block),
        grid=(heads,),
        in_specs=in_specs,
        out_specs=[columns, pair],
        out_shape=(
            jax.ShapeDtypeStruct((query_count, width), jnp.bfloat16),
            jax.ShapeDtypeStruct((2, slots, chunk), jnp.bfloat16),
        ),
        scratch_shapes=[pltpu.VMEM((slots, HD), jnp.float32)] * 2,
        input_output_aliases=aliases,
        compiler_params=pltpu.CompilerParams(vmem_limit_bytes=VMEM_LIMIT),
        cost_estimate=pl.CostEstimate(
            flops=10 * query_count * slots * chunk,
            bytes_accessed=6 * query_count * chunk + 10 * 2 * slots * chunk,
            transcendentals=2 * query_count * slots * heads,
        ),
        name="attend",
    )(*operands)


def spread_kernel(pos, mine, received, own, sibling, *rest):
    result = rest[-1]
    x, core = pos[1], pos[2]
    last_dims = (((1,), (1,)), ((), ()))
    for core_at, weights in ((core, own), (1 - core, sibling)):
        for x_at, grads in ((x, mine), (1 - x, received)):
            total = lax.dot_general(
                grads[0], weights[0, 0], last_dims, preferred_element_type=jnp.float32
            ) + lax.dot_general(
                grads[1], weights[0, 1], last_dims, preferred_element_type=jnp.float32
            )
            if len(rest) > 1:
                total = total + rest[0][0, core_at, x_at]
            result[0, core_at, x_at] = total.astype(result.dtype)


def spread(pos, mine, received, own, sibling, earlier, tensor_count, final):
    line, _, depth, width = own.shape
    slots = mine.shape[1]
    per_tensor = line // tensor_count

    def result_at(step, pos):
        z = line_index(step, pos, line)
        shift = lax.rem(z // per_tensor - pos[3] + tensor_count, tensor_count)
        return (shift * per_tensor + lax.rem(z, per_tensor), 0, 0, 0, 0)

    weight_spec = pl.BlockSpec((1, 2, depth, width), lambda step, pos: (step, 0, 0, 0))
    grad_spec = pl.BlockSpec((2, slots, width), lambda step, pos: (0, 0, 0))
    result_spec = pl.BlockSpec((1, 2, 2, slots, depth), result_at)
    operands = [pos, mine, received, own, sibling]
    in_specs = [grad_spec, grad_spec, weight_spec, weight_spec]
    aliases = {}
    if earlier is not None:
        if not final:
            aliases = {len(operands): 0}
        operands.append(earlier)
        in_specs.append(result_spec)
    shape = (line, 2, 2, slots, depth)
    return pl.pallas_call(
        spread_kernel,
        grid_spec=pltpu.PrefetchScalarGridSpec(
            num_scalar_prefetch=1, grid=(line,), in_specs=in_specs, out_specs=result_spec
        ),
        out_shape=jax.ShapeDtypeStruct(shape, jnp.bfloat16 if final else jnp.float32),
        input_output_aliases=aliases,
        compiler_params=pltpu.CompilerParams(vmem_limit_bytes=VMEM_LIMIT),
        cost_estimate=pl.CostEstimate(
            flops=2 * 2 * slots * 2 * line * depth * 2 * width,
            bytes_accessed=2 * own.size * 2 + 8 * math.prod(shape) + 8 * slots * width,
            transcendentals=0,
        ),
        name="spread",
    )(*operands)


def gather_line(block, z, line, up, down):
    rising, falling = [block], [block]
    for _ in range(line - 1):
        rising.append(lax.ppermute(rising[-1], "dp", up))
        falling.append(lax.ppermute(falling[-1], "dp", down))
    parts = [block]
    for step in range(1, line):
        parts.append(jnp.where(z >= step, rising[step], falling[line - step]))
    return jnp.stack(parts)


def on_device(queries, out_grad, target_len, encoded, row_owner, projections, velocity):
    peers = lax.axis_size("dp")
    tensor_count = lax.axis_size("tensor")
    line = peers // 4
    per_tensor = line // tensor_count
    stored_rows = encoded.shape[0]
    depth = projections.shape[1]
    capacity = max(2, 2 * stored_rows // peers)
    slots = peers * capacity
    place = lax.axis_index("dp")
    tensor_at = lax.axis_index("tensor")
    z, x, core = place // 4, (place // 2) % 2, place % 2
    pos = jnp.stack([z, x, core, tensor_at]).astype(jnp.int32)
    up = [(i, i + 4) for i in range(peers - 4)]
    down = [(i + 4, i) for i in range(peers - 4)]
    x_swap = [(i, i ^ 2) for i in range(peers)]
    core_swap = [(i, i ^ 1) for i in range(peers)]

    def tensor_shift(value, shift):
        pairs = [(i, (i + shift) % tensor_count) for i in range(tensor_count)]
        return lax.ppermute(value, "tensor", pairs)

    sizes = split_heads(queries.shape[1] // HD)
    firsts = [sum(sizes[:i]) for i in range(len(sizes))]

    own_parts, sibling_parts = [], []
    for first, size in zip(firsts, sizes):
        at = slice(first * HD, (first + size) * HD)
        predicted = (projections[:, :, at].astype(jnp.float32) - velocity[:, :, at]).astype(
            jnp.bfloat16
        )
        gathered = gather_line(predicted, z, line, up, down)
        own_parts.append(gathered)
        sibling_parts.append(lax.ppermute(gathered, "dp", core_swap))

    placement = slot_table(row_owner[:, 0], capacity, peers)
    filled = jnp.sum(placement.astype(jnp.float32), axis=1).astype(jnp.bfloat16)
    outgoing = jnp.dot(placement, encoded, preferred_element_type=jnp.float32).astype(jnp.bfloat16)
    outgoing = outgoing.reshape(line, 2, 2, capacity, per_tensor, 2, 2, depth)
    outgoing = outgoing.transpose(0, 5, 2, 4, 6, 1, 3, 7).reshape(peers, -1, depth)
    incoming = lax.all_to_all(outgoing, "dp", split_axis=0, concat_axis=0, tiled=True)
    incoming_flag = lax.all_to_all(filled, "dp", split_axis=0, concat_axis=0, tiled=True)
    usable = (incoming_flag.astype(jnp.float32) > 0.5).astype(jnp.float32)[:, None]
    incoming = incoming.reshape(peers, per_tensor, 2, 2, capacity, depth)
    incoming = incoming.transpose(1, 2, 3, 0, 4, 5).reshape(per_tensor, 2, 2, slots, depth)
    rows = jnp.concatenate(
        [incoming] + [tensor_shift(incoming, shift) for shift in range(1, tensor_count)]
    )

    query_grad = None
    spread_total = None
    for index, (first, size) in enumerate(zip(firsts, sizes)):
        own, sibling = own_parts[index], sibling_parts[index]
        mine, other = project(pos, rows, own, sibling, tensor_count)
        received = lax.ppermute(other, "dp", x_swap)
        query_grad, pair_grad = attend(
            target_len, usable, queries, out_grad, mine, received, first, query_grad
        )
        pair_received = lax.ppermute(pair_grad, "dp", x_swap)
        spread_total = spread(
            pos,
            pair_grad,
            pair_received,
            own,
            sibling,
            spread_total,
            tensor_count,
            index == len(sizes) - 1,
        )

    summed = spread_total[:per_tensor].astype(jnp.float32)
    for shift in range(1, tensor_count):
        part = spread_total[shift * per_tensor : (shift + 1) * per_tensor]
        summed = summed + tensor_shift(part, shift).astype(jnp.float32)
    summed = summed.astype(jnp.bfloat16).reshape(per_tensor, 2, 2, peers, capacity, depth)
    summed = summed.transpose(3, 0, 1, 2, 4, 5).reshape(peers, -1, depth)
    returned = lax.all_to_all(summed, "dp", split_axis=0, concat_axis=0, tiled=True)
    returned = returned.reshape(line, 2, 2, per_tensor, 2, 2, capacity, depth)
    returned = returned.transpose(0, 5, 2, 6, 3, 1, 4, 7).reshape(slots, -1)
    encoded_grad = lax.dot_general(
        placement, returned, (((0,), (0,)), ((), ())), preferred_element_type=jnp.float32
    ).astype(jnp.bfloat16)
    return (query_grad, encoded_grad)


def solution(mesh):
    in_specs = (
        P("dp", "tensor"),
        P("dp", "tensor"),
        P("dp"),
        P("dp", "tensor"),
        P("dp", None),
        P(None, "dp", "tensor"),
        P(None, "dp", "tensor"),
    )
    out_specs = (P("dp", "tensor"), P("dp", "tensor"))
    return jax.shard_map(
        on_device, mesh=mesh, in_specs=in_specs, out_specs=out_specs, check_vma=False
    )
```

time: 402 us -> 364 us (0.905)
  starting transfers between devices: 10.8 us -> 119 us
  waiting for transfers between devices: 204 us -> 104 us
  matrix products: 94.1 us -> 1.57 us
  Pallas kernels: 0 us -> 73.2 us
  local copies, waits for them, and re-layouts: 34.4 us -> 7.42 us
  between operations: 14.6 us -> 1.89 us
  other arithmetic: 11.4 us -> 19 us
    all_gather x2 -> x0, waiting for transfers between devices: 172 us -> none  [the longest x1 170 us: on_device(): gathered = lax.all_gather(predicted, 'dp', axis=1, tiled=True)]
    ppermute x0 -> x38, starting transfers between devices: none -> 104 us  [the longest x12 74.8 us: gather_line(): rising.append(lax.ppermute(rising[-1], 'dp', up))]
    ppermute x0 -> x38, waiting for transfers between devices: none -> 98.2 us  [the longest x12 37.8 us: gather_line(): falling.append(lax.ppermute(falling[-1], 'dp', down))]
    dot_general x13 -> x1, matrix products: 93.6 us -> 1.15 us  [on_device(): lax.dot_general(placement, returned, (((0,), (0,)), ((), ())), preferred_...]
    pallas_call x0 -> x12, Pallas kernels: none -> 73.2 us  [the longest x4 28.7 us: spread(): pl.pallas_call(spread_kernel, grid_spec=pltpu.PrefetchScalarGridSpec(num_...]
    reduce_scatter x1 -> x0, waiting for transfers between devices: 31.9 us -> none  [on_device(): lax.psum_scatter(partial_value.astype(jnp.bfloat16), 'tensor', scatter_di...]
    unnamed x23 -> x24, local copies, waits for them, and re-layouts: 15.5 us -> 1.43 us
    another operation x0 -> x17, other arithmetic: none -> 12.4 us  [the longest x16 12.3 us: gather_line(): return jnp.stack(parts)]
  transfers between devices with their start and end apart: 5 -> 40, of which waited for: 3 -> 21; matrix products, arithmetic and copies ran while one was open for 14% -> 5% of each run, Pallas kernels for 0% -> 19%
where the time goes in v1:
time: 364 us; the launch traced here: 362 us
  starting transfers between devices  119 us (33%)
  waiting for transfers between devices  104 us (29%)
  Pallas kernels  73.2 us (20%)
  blocking collectives  36.1 us (10%)
  other arithmetic  19 us (5%)
  local copies, waits for them, and re-layouts  7.42 us (2%)
    ppermute x12, starting transfers between devices, gather_line(): rising.append(lax.ppermute(rising[-1], 'dp', up))  74.8 us
    ppermute x12, waiting for transfers between devices, gather_line(): falling.append(lax.ppermute(falling[-1], 'dp', down))  37.8 us
    all_to_all x1, blocking collectives, on_device(): lax.all_to_all(summed, 'dp', split_axis=0, concat_axis=0, tiled=True)  36.1 us
    pallas_call x4, Pallas kernels, spread(): pl.pallas_call(spread_kernel, grid_spec=pltpu.PrefetchScalarGridSpec(num_...  28.7 us
    ppermute x2, waiting for transfers between devices, tensor_shift(): return lax.ppermute(value, 'tensor', pairs)  27.7 us
    pallas_call x4, Pallas kernels, attend(): pl.pallas_call(functools.partial(attend_kernel, block), grid=(heads,), in...  23.3 us
    pallas_call x4, Pallas kernels, project(): pl.pallas_call(project_kernel, grid_spec=pltpu.PrefetchScalarGridSpec(num...  21.3 us
    ppermute x12, starting transfers between devices, gather_line(): falling.append(lax.ppermute(falling[-1], 'dp', down))  15.4 us
  transfers between devices with their start and end apart: 40, of which 21 were waited for; matrix products, arithmetic and copies ran while one was open for 5% of the time, Pallas kernels for 19%

profile of v1, /device:TPU:0, one launch (start us, length us, event | category | flops | bytes accessed | tf_op | source)
XLA Modules:
  0.0 361.9 jit_solution(5556286445713946860)
XLA Ops:
  0.7 4.4 %subtract_convert_fusion = (bf16[2,256,512]{2,1,0:T(8,128)(2,1)S(1)}, bf16[2,256,512]{2,1,0:T(8,128)(2,1)S(1)}, bf16[2,256,512]{2,1,0:T(8,128)(2,1)}, bf16[2,256,512]{2,1,0:T(8,128)(2,1)S(1)}) fusion(f32[2,256,2048]{2,1,0:T(8,128)} %param.13, bf16[2,256,2048]{2,1,0:T(8,128)(2,1)} %param.12), kind=kLoop, calls=%fused_computation.9 | loop fusion | flops 3145728 | bytes 8388608 | tf_op jit(solution)/shard_map/convert_element_type | solution.py:275
  6.4 6.4 %collective-permute-start.25 = (bf16[2,256,512]{2,1,0:T(8,128)(2,1)S(1)}, bf16[2,256,512]{2,1,0:T(8,128)(2,1)}, u32[]{:S(2)}, u32[]{:S(2)}) collective-permute-start(bf16[2,256,512]{2,1,0:T(8,128)(2,1)S(1)} %get-tuple-element.34), channel_id=1, source_target_pairs={{0,8},{2,10},{4,12},{6,14},{8,16},{10,18},{12,20},{14,22},{16,24},... | collective-permute-start | bytes 1572872 | tf_op jit(solution)/shard_map/ppermute | solution.py:239
  14.0 5.3 %collective-permute-start.17 = (bf16[2,256,512]{2,1,0:T(8,128)(2,1)S(1)}, bf16[2,256,512]{2,1,0:T(8,128)(2,1)}, u32[]{:S(2)}, u32[]{:S(2)}) collective-permute-start(bf16[2,256,512]{2,1,0:T(8,128)(2,1)S(1)} %get-tuple-element.37), channel_id=1, source_target_pairs={{0,8},{2,10},{4,12},{6,14},{8,16},{10,18},{12,20},{14,22},{16,24},... | collective-permute-start | bytes 1572872 | tf_op jit(solution)/shard_map/ppermute | solution.py:239
  20.7 2.2 collective-permute-done.26
  22.8 4.7 %collective-permute-start.9 = (bf16[2,256,512]{2,1,0:T(8,128)(2,1)S(1)}, bf16[2,256,512]{2,1,0:T(8,128)(2,1)}, u32[]{:S(2)}, u32[]{:S(2)}) collective-permute-start(bf16[2,256,512]{2,1,0:T(8,128)(2,1)S(1)} %get-tuple-element.35), channel_id=1, source_target_pairs={{0,8},{2,10},{4,12},{6,14},{8,16},{10,18},{12,20},{14,22},{16,24},... | collective-permute-start | bytes 1572872 | tf_op jit(solution)/shard_map/ppermute | solution.py:239
  29.1 4.9 %collective-permute-done.18 = bf16[2,256,512]{2,1,0:T(8,128)(2,1)} collective-permute-done((bf16[2,256,512]{2,1,0:T(8,128)(2,1)S(1)}, bf16[2,256,512]{2,1,0:T(8,128)(2,1)}, u32[]{:S(2)}, u32[]{:S(2)}) %collective-permute-start.18) | collective-permute-done | bytes 524320 | tf_op jit(solution)/shard_map/ppermute | solution.py:240
  35.5 5.3 %collective-permute-start.29 = (bf16[2,256,512]{2,1,0:T(8,128)(2,1)}, bf16[2,256,512]{2,1,0:T(8,128)(2,1)}, u32[]{:S(2)}, u32[]{:S(2)}) collective-permute-start(bf16[2,256,512]{2,1,0:T(8,128)(2,1)} %collective-permute-done.25), channel_id=1, source_target_pairs={{0,8},{2,10},{4,12},{6,14},{8,16},{10,18},{12,20},{14,22},{16,24},... | collective-permute-start | bytes 1572872 | tf_op jit(solution)/shard_map/ppermute | solution.py:239
  40.9 4.4 %collective-permute-done.10 = bf16[2,256,512]{2,1,0:T(8,128)(2,1)} collective-permute-done((bf16[2,256,512]{2,1,0:T(8,128)(2,1)S(1)}, bf16[2,256,512]{2,1,0:T(8,128)(2,1)}, u32[]{:S(2)}, u32[]{:S(2)}) %collective-permute-start.10) | collective-permute-done | bytes 524320 | tf_op jit(solution)/shard_map/ppermute | solution.py:240
  45.3 4.8 %collective-permute-start.1 = (bf16[2,256,512]{2,1,0:T(8,128)(2,1)}, bf16[2,256,512]{2,1,0:T(8,128)(2,1)}, u32[]{:S(2)}, u32[]{:S(2)}) collective-permute-start(bf16[2,256,512]{2,1,0:T(8,128)(2,1)} %get-tuple-element.36), channel_id=1, source_target_pairs={{0,8},{2,10},{4,12},{6,14},{8,16},{10,18},{12,20},{14,22},{16,24},... | collective-permute-start | bytes 1572872 | tf_op jit(solution)/shard_map/ppermute | solution.py:239
  51.4 5.1 %collective-permute-done.2 = bf16[2,256,512]{2,1,0:T(8,128)(2,1)S(1)} collective-permute-done((bf16[2,256,512]{2,1,0:T(8,128)(2,1)}, bf16[2,256,512]{2,1,0:T(8,128)(2,1)S(1)}, u32[]{:S(2)}, u32[]{:S(2)}) %collective-permute-start.2) | collective-permute-done | bytes 524320 | tf_op jit(solution)/shard_map/ppermute | solution.py:240
  57.2 4.8 %collective-permute-start.21 = (bf16[2,256,512]{2,1,0:T(8,128)(2,1)}, bf16[2,256,512]{2,1,0:T(8,128)(2,1)}, u32[]{:S(2)}, u32[]{:S(2)}) collective-permute-start(bf16[2,256,512]{2,1,0:T(8,128)(2,1)} %collective-permute-done.17), channel_id=1, source_target_pairs={{0,8},{2,10},{4,12},{6,14},{8,16},{10,18},{12,20},{14,22},{16,24},... | collective-permute-start | bytes 1572872 | tf_op jit(solution)/shard_map/ppermute | solution.py:239
  64.5 3.8 %all-to-all-start.1 = ((bf16[16,128,256]{2,1,0:T(8,128)(2,1)}), bf16[16,128,256]{2,1,0:T(8,128)(2,1)S(1)}, u32[]{:S(2)}, u32[]{:S(2)}) async-start(bf16[16,128,256]{2,1,0:T(8,128)(2,1)} %bitcast.6), calls=%async_computation.1 | async-start | bytes 2097152 | tf_op jit(solution)/shard_map/all_to_all | solution.py:287
  69.7 4.6 %collective-permute-start.13 = (bf16[2,256,512]{2,1,0:T(8,128)(2,1)}, bf16[2,256,512]{2,1,0:T(8,128)(2,1)S(1)}, u32[]{:S(2)}, u32[]{:S(2)}) collective-permute-start(bf16[2,256,512]{2,1,0:T(8,128)(2,1)} %collective-permute-done.9), channel_id=1, source_target_pairs={{0,8},{2,10},{4,12},{6,14},{8,16},{10,18},{12,20},{14,22},{16,24},... | collective-permute-start | bytes 1572872 | tf_op jit(solution)/shard_map/ppermute | solution.py:239
  76.7 3.7 %collective-permute-done.19 = bf16[2,256,512]{2,1,0:T(8,128)(2,1)} collective-permute-done((bf16[2,256,512]{2,1,0:T(8,128)(2,1)}, bf16[2,256,512]{2,1,0:T(8,128)(2,1)}, u32[]{:S(2)}, u32[]{:S(2)}) %collective-permute-start.19) | collective-permute-done | bytes 524320 | tf_op jit(solution)/shard_map/ppermute | solution.py:240
  80.4 7.1 %collective-permute-start.5 = (bf16[2,256,512]{2,1,0:T(8,128)(2,1)}, bf16[2,256,512]{2,1,0:T(8,128)(2,1)S(1)}, u32[]{:S(2)}, u32[]{:S(2)}) collective-permute-start(bf16[2,256,512]{2,1,0:T(8,128)(2,1)} %collective-permute-done.1), channel_id=1, source_target_pairs={{0,8},{2,10},{4,12},{6,14},{8,16},{10,18},{12,20},{14,22},{16,24},... | collective-permute-start | bytes 1572872 | tf_op jit(solution)/shard_map/ppermute | solution.py:239
  87.6 1.9 collective-permute-start.30
  90.6 16.4 %collective-permute-done.11 = bf16[2,256,512]{2,1,0:T(8,128)(2,1)S(1)} collective-permute-done((bf16[2,256,512]{2,1,0:T(8,128)(2,1)}, bf16[2,256,512]{2,1,0:T(8,128)(2,1)S(1)}, u32[]{:S(2)}, u32[]{:S(2)}) %collective-permute-start.11) | collective-permute-done | bytes 524320 | tf_op jit(solution)/shard_map/ppermute | solution.py:240
  108.7 9.8 %collective-permute-start.22 = (bf16[2,256,512]{2,1,0:T(8,128)(2,1)}, bf16[2,256,512]{2,1,0:T(8,128)(2,1)S(1)}, u32[]{:S(2)}, u32[]{:S(2)}) collective-permute-start(bf16[2,256,512]{2,1,0:T(8,128)(2,1)} %collective-permute-done.21), channel_id=1, source_target_pairs={{0,8},{2,10},{4,12},{6,14},{8,16},{10,18},{12,20},{14,22},{16,24},... | collective-permute-start | bytes 1572872 | tf_op jit(solution)/shard_map/ppermute | solution.py:239
  119.9 9.8 %collective-permute-start.14 = (bf16[2,256,512]{2,1,0:T(8,128)(2,1)S(1)}, bf16[2,256,512]{2,1,0:T(8,128)(2,1)S(1)}, u32[]{:S(2)}, u32[]{:S(2)}) collective-permute-start(bf16[2,256,512]{2,1,0:T(8,128)(2,1)S(1)} %collective-permute-done.13), channel_id=1, source_target_pairs={{0,8},{2,10},{4,12},{6,14},{8,16},{10,18},{12,20},{14,22},{16,24},... | collective-permute-start | bytes 1572872 | tf_op jit(solution)/shard_map/ppermute | solution.py:239
  133.6 8.8 %collective-permute-done.22 = bf16[2,256,512]{2,1,0:T(8,128)(2,1)S(1)} collective-permute-done((bf16[2,256,512]{2,1,0:T(8,128)(2,1)}, bf16[2,256,512]{2,1,0:T(8,128)(2,1)S(1)}, u32[]{:S(2)}, u32[]{:S(2)}) %collective-permute-start.22) | collective-permute-done | bytes 524320 | tf_op jit(solution)/shard_map/ppermute | solution.py:239
  144.8 10.1 %collective-permute-start.6 = (bf16[2,256,512]{2,1,0:T(8,128)(2,1)S(1)}, bf16[2,256,512]{2,1,0:T(8,128)(2,1)S(1)}, u32[]{:S(2)}, u32[]{:S(2)}) collective-permute-start(bf16[2,256,512]{2,1,0:T(8,128)(2,1)S(1)} %collective-permute-done.5), channel_id=1, source_target_pairs={{0,8},{2,10},{4,12},{6,14},{8,16},{10,18},{12,20},{14,22},{16,24},... | collective-permute-start | bytes 1572872 | tf_op jit(solution)/shard_map/ppermute | solution.py:239
  159.1 1.7 pad_maximum_fusion.2.own
  163.7 2.6 pad_maximum_fusion.1.own
  169.8 11.4 %all-to-all-start = ((bf16[16,16,1]{1,2,0:T(2,128)(2,1)}), bf16[16,16,1]{1,2,0:T(2,128)(2,1)S(1)}, u32[]{:S(2)}, u32[]{:S(2)}) async-start(bf16[16,16,1]{1,2,0:T(2,128)(2,1)} %all_to_all.16), calls=%async_computation | async-start | bytes 16384 | tf_op jit(solution)/shard_map/all_to_all | solution.py:288
  182.0 5.6 %all-to-all-done = bf16[16,16,1]{1,2,0:T(2,128)(2,1)S(1)} async-done(((bf16[16,16,1]{1,2,0:T(2,128)(2,1)}), bf16[16,16,1]{1,2,0:T(2,128)(2,1)S(1)}, u32[]{:S(2)}, u32[]{:S(2)}) %all-to-all-start) | async-done | bytes 544 | tf_op jit(solution)/shard_map/all_to_all | solution.py:288
  187.7 5.5 %collective-permute-done = bf16[2,2,2,256,256]{4,3,2,1,0:T(8,128)(2,1)S(1)} collective-permute-done((bf16[2,2,2,256,256]{4,3,2,1,0:T(8,128)(2,1)}, bf16[2,2,2,256,256]{4,3,2,1,0:T(8,128)(2,1)S(1)}, u32[]{:S(2)}, u32[]{:S(2)}) %collective-permute-start) | collective-permute-done | bytes 1048608 | tf_op jit(solution)/shard_map/ppermute | solution.py:267
  194.6 5.1 %project.7 = (f32[2,256,512]{2,1,0:T(8,128)S(1)}, bf16[2,256,512]{2,1,0:T(8,128)(2,1)S(1)}) custom-call(s32[4]{0:T(128)S(1)} %pad_add_fusion.pos, bf16[4,2,2,256,256]{4,3,2,1,0:T(8,128)(2,1)S(1)} %pad_maximum_fusion.rows, bf16[4,2,256,512]{3,2,1,0:T(8,128)(2,1)S(1)} %pad_maximum_fusion.4.own, bf16[4,2,256,512]{3,2,1,0:T(8,128)(2,1)} %collective-permute-done.31.sibling), custom_call_target="tpu_custom_call" | custom-call | flops 2147483648 | bytes 7864320 | tf_op jit(solution)/shard_map/project/pallas_call | solution.py:73
  199.6 1.7 collective-permute-start.32
  201.3 5.4 %project.6 = (f32[2,256,512]{2,1,0:T(8,128)S(1)}, bf16[2,256,512]{2,1,0:T(8,128)(2,1)S(1)}) custom-call(s32[4]{0:T(128)S(1)} %pad_add_fusion.pos, bf16[4,2,2,256,256]{4,3,2,1,0:T(8,128)(2,1)S(1)} %pad_maximum_fusion.rows, bf16[4,2,256,512]{3,2,1,0:T(8,128)(2,1)} %pad_maximum_fusion.3.own, bf16[4,2,256,512]{3,2,1,0:T(8,128)(2,1)} %collective-permute-done.23.sibling), custom_call_target="tpu_custom_call" | custom-call | flops 2147483648 | bytes 7864320 | tf_op jit(solution)/shard_map/project/pallas_call | solution.py:73
  207.2 5.4 %project.5 = (f32[2,256,512]{2,1,0:T(8,128)S(1)}, bf16[2,256,512]{2,1,0:T(8,128)(2,1)S(1)}) custom-call(s32[4]{0:T(128)S(1)} %pad_add_fusion.pos, bf16[4,2,2,256,256]{4,3,2,1,0:T(8,128)(2,1)S(1)} %pad_maximum_fusion.rows, bf16[4,2,256,512]{3,2,1,0:T(8,128)(2,1)} %pad_maximum_fusion.2.own, bf16[4,2,256,512]{3,2,1,0:T(8,128)(2,1)} %collective-permute-done.15.sibling), custom_call_target="tpu_custom_call" | custom-call | flops 2147483648 | bytes 7864320 | tf_op jit(solution)/shard_map/project/pallas_call | solution.py:73
  214.3 5.4 %project.4 = (f32[2,256,512]{2,1,0:T(8,128)S(1)}, bf16[2,256,512]{2,1,0:T(8,128)(2,1)S(1)}) custom-call(s32[4]{0:T(128)S(1)} %pad_add_fusion.pos, bf16[4,2,2,256,256]{4,3,2,1,0:T(8,128)(2,1)S(1)} %pad_maximum_fusion.rows, bf16[4,2,256,512]{3,2,1,0:T(8,128)(2,1)} %pad_maximum_fusion.1.own, bf16[4,2,256,512]{3,2,1,0:T(8,128)(2,1)} %collective-permute-done.7.sibling), custom_call_target="tpu_custom_call" | custom-call | flops 2147483648 | bytes 7864320 | tf_op jit(solution)/shard_map/project/pallas_call | solution.py:73
  220.2 5.8 %attend.4 = (bf16[1024,2048]{1,0:T(8,128)(2,1)}, bf16[2,256,512]{2,1,0:T(8,128)(2,1)S(1)}) custom-call(s32[1]{0:T(128)S(6)} %copy.55.live, f32[256,1]{1,0:T(8,128)S(1)} %reshape.68.usable, bf16[1024,2048]{1,0:T(8,128)(2,1)} %queries.7, bf16[1024,2048]{1,0:T(8,128)(2,1)} %grads.7, f32[2,256,512]{2,1,0:T(8,128)S(1)} %get-tuple-element.24.mine, ...), custom_call_target="tpu_custom_call" | custom-call | flops 1342177280 | bytes 5767168 | tf_op jit(solution)/shard_map/attend/pallas_call | solution.py:160
  227.7 5.8 %attend.5 = (bf16[1024,2048]{1,0:T(8,128)(2,1)}, bf16[2,256,512]{2,1,0:T(8,128)(2,1)S(1)}) custom-call(s32[1]{0:T(128)S(6)} %copy.55.live, f32[256,1]{1,0:T(8,128)S(1)} %reshape.68.usable, bf16[1024,2048]{1,0:T(8,128)(2,1)} %queries.7, bf16[1024,2048]{1,0:T(8,128)(2,1)} %grads.7, ...), custom_call_target="tpu_custom_call", output_to_operand_aliasing={{0}: (6, {})} | custom-call | flops 1342177280 | bytes 5767168 | tf_op jit(solution)/shard_map/attend/pallas_call | solution.py:160
  233.9 3.1 collective-permute-done.16.received
  237.0 5.8 %attend.6 = (bf16[1024,2048]{1,0:T(8,128)(2,1)}, bf16[2,256,512]{2,1,0:T(8,128)(2,1)S(1)}) custom-call(s32[1]{0:T(128)S(6)} %copy.55.live, f32[256,1]{1,0:T(8,128)S(1)} %reshape.68.usable, bf16[1024,2048]{1,0:T(8,128)(2,1)} %queries.7, bf16[1024,2048]{1,0:T(8,128)(2,1)} %grads.7, ...), custom_call_target="tpu_custom_call", output_to_operand_aliasing={{0}: (6, {})} | custom-call | flops 1342177280 | bytes 5767168 | tf_op jit(solution)/shard_map/attend/pallas_call | solution.py:160
  244.4 3.8 %collective-permute-done.8.received = bf16[2,256,512]{2,1,0:T(8,128)(2,1)S(1)} collective-permute-done((bf16[2,256,512]{2,1,0:T(8,128)(2,1)S(1)}, bf16[2,256,512]{2,1,0:T(8,128)(2,1)S(1)}, u32[]{:S(2)}, u32[]{:S(2)}) %collective-permute-start.8) | collective-permute-done | bytes 524320 | tf_op jit(solution)/shard_map/ppermute | solution.py:301
  248.2 5.8 %attend.7 = (bf16[1024,2048]{1,0:T(8,128)(2,1)}, bf16[2,256,512]{2,1,0:T(8,128)(2,1)S(1)}) custom-call(s32[1]{0:T(128)S(6)} %copy.55.live, f32[256,1]{1,0:T(8,128)S(1)} %reshape.68.usable, bf16[1024,2048]{1,0:T(8,128)(2,1)} %queries.7, bf16[1024,2048]{1,0:T(8,128)(2,1)} %grads.7, ...), custom_call_target="tpu_custom_call", output_to_operand_aliasing={{0}: (6, {})} | custom-call | flops 1342177280 | bytes 5767168 | tf_op jit(solution)/shard_map/attend/pallas_call | solution.py:160
  255.6 3.8 %collective-permute-done.36.received = bf16[2,256,512]{2,1,0:T(8,128)(2,1)S(1)} collective-permute-done((bf16[2,256,512]{2,1,0:T(8,128)(2,1)S(1)}, bf16[2,256,512]{2,1,0:T(8,128)(2,1)S(1)}, u32[]{:S(2)}, u32[]{:S(2)}) %collective-permute-start.36) | collective-permute-done | bytes 524320 | tf_op jit(solution)/shard_map/ppermute | solution.py:305
  259.5 6.5 %spread.4.rest_0_ = f32[4,2,2,256,256]{4,3,2,1,0:T(8,128)} custom-call(s32[4]{0:T(128)S(1)} %pad_add_fusion.pos, bf16[2,256,512]{2,1,0:T(8,128)(2,1)S(1)} %get-tuple-element.33.mine, bf16[2,256,512]{2,1,0:T(8,128)(2,1)S(1)} %collective-permute-done.36.received, bf16[4,2,256,512]{3,2,1,0:T(8,128)(2,1)S(1)} %pad_maximum_fusion.4.own, ...), custom_call_target="tpu_custom_call" | custom-call | flops 2147483648 | bytes 13631488 | tf_op jit(solution)/shard_map/spread/pallas_call | solution.py:219
  265.9 4.8 %collective-permute-done.35.received = bf16[2,256,512]{2,1,0:T(8,128)(2,1)S(1)} collective-permute-done((bf16[2,256,512]{2,1,0:T(8,128)(2,1)S(1)}, bf16[2,256,512]{2,1,0:T(8,128)(2,1)S(1)}, u32[]{:S(2)}, u32[]{:S(2)}) %collective-permute-start.35) | collective-permute-done | bytes 524320 | tf_op jit(solution)/shard_map/ppermute | solution.py:305
  270.7 7.9 %spread.5.rest_0_ = f32[4,2,2,256,256]{4,3,2,1,0:T(8,128)} custom-call(s32[4]{0:T(128)S(1)} %pad_add_fusion.pos, bf16[2,256,512]{2,1,0:T(8,128)(2,1)S(1)} %get-tuple-element.32.mine, bf16[2,256,512]{2,1,0:T(8,128)(2,1)S(1)} %collective-permute-done.35.received, bf16[4,2,256,512]{3,2,1,0:T(8,128)(2,1)} %pad_maximum_fusion.3.own, ...), custom_call_target="tpu_custom_call", output_to_operand_aliasing={{}: (5, {})} | custom-call | flops 2147483648 | bytes 13631488 | tf_op jit(solution)/shard_map/spread/pallas_call | solution.py:219
  278.5 3.4 collective-permute-done.34.received
  281.9 8.1 %spread.6.rest_0_ = f32[4,2,2,256,256]{4,3,2,1,0:T(8,128)} custom-call(s32[4]{0:T(128)S(1)} %pad_add_fusion.pos, bf16[2,256,512]{2,1,0:T(8,128)(2,1)S(1)} %get-tuple-element.31.mine, bf16[2,256,512]{2,1,0:T(8,128)(2,1)S(1)} %collective-permute-done.34.received, bf16[4,2,256,512]{3,2,1,0:T(8,128)(2,1)} %pad_maximum_fusion.2.own, ...), custom_call_target="tpu_custom_call", output_to_operand_aliasing={{}: (5, {})} | custom-call | flops 2147483648 | bytes 13631488 | tf_op jit(solution)/shard_map/spread/pallas_call | solution.py:219
  290.0 1.9 collective-permute-done.33.received
  291.9 6.3 %spread.7 = bf16[4,2,2,256,256]{4,3,2,1,0:T(8,128)(2,1)S(1)} custom-call(s32[4]{0:T(128)S(1)} %pad_add_fusion.pos, bf16[2,256,512]{2,1,0:T(8,128)(2,1)S(1)} %get-tuple-element.30.mine, bf16[2,256,512]{2,1,0:T(8,128)(2,1)S(1)} %collective-permute-done.33.received, bf16[4,2,256,512]{3,2,1,0:T(8,128)(2,1)} %pad_maximum_fusion.1.own, ...), custom_call_target="tpu_custom_call" | custom-call | flops 2147483648 | bytes 13631488 | tf_op jit(solution)/shard_map/spread/pallas_call | solution.py:219
  298.3 1.7 collective-permute-start.37
  300.0 22.3 %collective-permute-done.37 = bf16[2,2,2,256,256]{4,3,2,1,0:T(8,128)(2,1)S(1)} collective-permute-done((bf16[2,2,2,256,256]{4,3,2,1,0:T(8,128)(2,1)S(1)}, bf16[2,2,2,256,256]{4,3,2,1,0:T(8,128)(2,1)S(1)}, u32[]{:S(2)}, u32[]{:S(2)}) %collective-permute-start.37) | collective-permute-done | bytes 1048608 | tf_op jit(solution)/shard_map/ppermute | solution.py:267
  322.6 36.1 %all_to_all.20 = bf16[16,128,256]{2,1,0:T(8,128)(2,1)S(1)} all-to-all(bf16[16,128,256]{2,1,0:T(8,128)(2,1)S(1)} %bitcast.53), channel_id=1, replica_groups=mesh['dp'=16,'tensor'=2] {'dp'}, dimensions={0} | all-to-all | bytes 2097152 | tf_op jit(solution)/shard_map/all_to_all | solution.py:323
  (106 shorter events, 49.1 us)
Async XLA Ops:
  0.6 61.4 %copy-start = (bf16[128,2048]{1,0:T(8,128)(2,1)S(1)}, bf16[128,2048]{1,0:T(8,128)(2,1)}, u32[]{:S(2)}) copy-start(bf16[128,2048]{1,0:T(8,128)(2,1)} %param.10) | copy-start | bytes 1572868
  0.6 28.2 %copy-start.11 = (s32[128,1]{0,1:T(1,128)S(1)}, s32[128,1]{0,1:T(1,128)}, u32[]{:S(2)}) copy-start(s32[128,1]{0,1:T(1,128)} %param.11) | copy-start | bytes 1540
  5.0 15.6 %copy-start.6 = (bf16[2,256,512]{2,1,0:T(8,128)(2,1)}, bf16[2,256,512]{2,1,0:T(8,128)(2,1)S(1)}, u32[]{:S(2)}) copy-start(bf16[2,256,512]{2,1,0:T(8,128)(2,1)S(1)} %get-tuple-element.34) | copy-start | bytes 1572868
  5.0 51.4 %copy-start.4 = (bf16[2,256,512]{2,1,0:T(8,128)(2,1)}, bf16[2,256,512]{2,1,0:T(8,128)(2,1)S(1)}, u32[]{:S(2)}) copy-start(bf16[2,256,512]{2,1,0:T(8,128)(2,1)S(1)} %get-tuple-element.37) | copy-start | bytes 1572868
  5.0 57.0 %copy-start.2 = (bf16[2,256,512]{2,1,0:T(8,128)(2,1)}, bf16[2,256,512]{2,1,0:T(8,128)(2,1)S(1)}, u32[]{:S(2)}) copy-start(bf16[2,256,512]{2,1,0:T(8,128)(2,1)S(1)} %get-tuple-element.35) | copy-start | bytes 1572868
  5.1 17.8 %collective-permute-start.26 = (bf16[2,256,512]{2,1,0:T(8,128)(2,1)S(1)}, bf16[2,256,512]{2,1,0:T(8,128)(2,1)}, u32[]{:S(2)}, u32[]{:S(2)}) collective-permute-start(bf16[2,256,512]{2,1,0:T(8,128)(2,1)S(1)} %get-tuple-element.34), channel_id=1, source_target_pairs={{8,0},{10,2},{12,4},{14,6},{16,8},{18,10},{20,12},{22,14},{24,16},... | collective-permute-start | bytes 1572872 | tf_op jit(solution)/shard_map/ppermute | solution.py:240
  6.4 21.2 %collective-permute-start.25 = (bf16[2,256,512]{2,1,0:T(8,128)(2,1)S(1)}, bf16[2,256,512]{2,1,0:T(8,128)(2,1)}, u32[]{:S(2)}, u32[]{:S(2)}) collective-permute-start(bf16[2,256,512]{2,1,0:T(8,128)(2,1)S(1)} %get-tuple-element.34), channel_id=1, source_target_pairs={{0,8},{2,10},{4,12},{6,14},{8,16},{10,18},{12,20},{14,22},{16,24},... | collective-permute-start | bytes 1572872 | tf_op jit(solution)/shard_map/ppermute | solution.py:239
  12.7 21.3 %collective-permute-start.18 = (bf16[2,256,512]{2,1,0:T(8,128)(2,1)S(1)}, bf16[2,256,512]{2,1,0:T(8,128)(2,1)}, u32[]{:S(2)}, u32[]{:S(2)}) collective-permute-start(bf16[2,256,512]{2,1,0:T(8,128)(2,1)S(1)} %get-tuple-element.37), channel_id=1, source_target_pairs={{8,0},{10,2},{12,4},{14,6},{16,8},{18,10},{20,12},{22,14},{24,16},... | collective-permute-start | bytes 1572872 | tf_op jit(solution)/shard_map/ppermute | solution.py:240
  14.0 21.5 %collective-permute-start.17 = (bf16[2,256,512]{2,1,0:T(8,128)(2,1)S(1)}, bf16[2,256,512]{2,1,0:T(8,128)(2,1)}, u32[]{:S(2)}, u32[]{:S(2)}) collective-permute-start(bf16[2,256,512]{2,1,0:T(8,128)(2,1)S(1)} %get-tuple-element.37), channel_id=1, source_target_pairs={{0,8},{2,10},{4,12},{6,14},{8,16},{10,18},{12,20},{14,22},{16,24},... | collective-permute-start | bytes 1572872 | tf_op jit(solution)/shard_map/ppermute | solution.py:239
  19.4 25.9 %collective-permute-start.10 = (bf16[2,256,512]{2,1,0:T(8,128)(2,1)S(1)}, bf16[2,256,512]{2,1,0:T(8,128)(2,1)}, u32[]{:S(2)}, u32[]{:S(2)}) collective-permute-start(bf16[2,256,512]{2,1,0:T(8,128)(2,1)S(1)} %get-tuple-element.35), channel_id=1, source_target_pairs={{8,0},{10,2},{12,4},{14,6},{16,8},{18,10},{20,12},{22,14},{24,16},... | collective-permute-start | bytes 1572872 | tf_op jit(solution)/shard_map/ppermute | solution.py:240
  22.8 27.3 %collective-permute-start.9 = (bf16[2,256,512]{2,1,0:T(8,128)(2,1)S(1)}, bf16[2,256,512]{2,1,0:T(8,128)(2,1)}, u32[]{:S(2)}, u32[]{:S(2)}) collective-permute-start(bf16[2,256,512]{2,1,0:T(8,128)(2,1)S(1)} %get-tuple-element.35), channel_id=1, source_target_pairs={{0,8},{2,10},{4,12},{6,14},{8,16},{10,18},{12,20},{14,22},{16,24},... | collective-permute-start | bytes 1572872 | tf_op jit(solution)/shard_map/ppermute | solution.py:239
  27.6 28.8 %collective-permute-start.2 = (bf16[2,256,512]{2,1,0:T(8,128)(2,1)}, bf16[2,256,512]{2,1,0:T(8,128)(2,1)S(1)}, u32[]{:S(2)}, u32[]{:S(2)}) collective-permute-start(bf16[2,256,512]{2,1,0:T(8,128)(2,1)} %get-tuple-element.36), channel_id=1, source_target_pairs={{8,0},{10,2},{12,4},{14,6},{16,8},{18,10},{20,12},{22,14},{24,16},... | collective-permute-start | bytes 1572872 | tf_op jit(solution)/shard_map/ppermute | solution.py:240
  34.1 34.3 %collective-permute-start.27 = (bf16[2,256,512]{2,1,0:T(8,128)(2,1)}, bf16[2,256,512]{2,1,0:T(8,128)(2,1)}, u32[]{:S(2)}, u32[]{:S(2)}) collective-permute-start(bf16[2,256,512]{2,1,0:T(8,128)(2,1)} %collective-permute-done.26), channel_id=1, source_target_pairs={{8,0},{10,2},{12,4},{14,6},{16,8},{18,10},{20,12},{22,14},{24,16},... | collective-permute-start | bytes 1572872 | tf_op jit(solution)/shard_map/ppermute | solution.py:240
  35.5 34.2 %collective-permute-start.29 = (bf16[2,256,512]{2,1,0:T(8,128)(2,1)}, bf16[2,256,512]{2,1,0:T(8,128)(2,1)}, u32[]{:S(2)}, u32[]{:S(2)}) collective-permute-start(bf16[2,256,512]{2,1,0:T(8,128)(2,1)} %collective-permute-done.25), channel_id=1, source_target_pairs={{0,8},{2,10},{4,12},{6,14},{8,16},{10,18},{12,20},{14,22},{16,24},... | collective-permute-start | bytes 1572872 | tf_op jit(solution)/shard_map/ppermute | solution.py:239
  45.3 30.1 %collective-permute-start.1 = (bf16[2,256,512]{2,1,0:T(8,128)(2,1)}, bf16[2,256,512]{2,1,0:T(8,128)(2,1)}, u32[]{:S(2)}, u32[]{:S(2)}) collective-permute-start(bf16[2,256,512]{2,1,0:T(8,128)(2,1)} %get-tuple-element.36), channel_id=1, source_target_pairs={{0,8},{2,10},{4,12},{6,14},{8,16},{10,18},{12,20},{14,22},{16,24},... | collective-permute-start | bytes 1572872 | tf_op jit(solution)/shard_map/ppermute | solution.py:239
  50.1 30.3 %collective-permute-start.19 = (bf16[2,256,512]{2,1,0:T(8,128)(2,1)}, bf16[2,256,512]{2,1,0:T(8,128)(2,1)}, u32[]{:S(2)}, u32[]{:S(2)}) collective-permute-start(bf16[2,256,512]{2,1,0:T(8,128)(2,1)} %collective-permute-done.18), channel_id=1, source_target_pairs={{8,0},{10,2},{12,4},{14,6},{16,8},{18,10},{20,12},{22,14},{24,16},... | collective-permute-start | bytes 1572872 | tf_op jit(solution)/shard_map/ppermute | solution.py:240
  57.2 30.3 %collective-permute-start.21 = (bf16[2,256,512]{2,1,0:T(8,128)(2,1)}, bf16[2,256,512]{2,1,0:T(8,128)(2,1)}, u32[]{:S(2)}, u32[]{:S(2)}) collective-permute-start(bf16[2,256,512]{2,1,0:T(8,128)(2,1)} %collective-permute-done.17), channel_id=1, source_target_pairs={{0,8},{2,10},{4,12},{6,14},{8,16},{10,18},{12,20},{14,22},{16,24},... | collective-permute-start | bytes 1572872 | tf_op jit(solution)/shard_map/ppermute | solution.py:239
  64.5 10.9 %copy-start.9 = (bf16[2,256,512]{2,1,0:T(8,128)(2,1)S(1)}, bf16[2,256,512]{2,1,0:T(8,128)(2,1)}, u32[]{:S(2)}) copy-start(bf16[2,256,512]{2,1,0:T(8,128)(2,1)} %copy-done.8) | copy-start | bytes 1572868
  64.5 101.8 %all-to-all-start.1 = ((bf16[16,128,256]{2,1,0:T(8,128)(2,1)}), bf16[16,128,256]{2,1,0:T(8,128)(2,1)S(1)}, u32[]{:S(2)}, u32[]{:S(2)}) async-start(bf16[16,128,256]{2,1,0:T(8,128)(2,1)} %bitcast.6), calls=%async_computation.1 | async-start | bytes 2097152 | tf_op jit(solution)/shard_map/all_to_all | solution.py:287
  68.3 38.7 %collective-permute-start.11 = (bf16[2,256,512]{2,1,0:T(8,128)(2,1)}, bf16[2,256,512]{2,1,0:T(8,128)(2,1)S(1)}, u32[]{:S(2)}, u32[]{:S(2)}) collective-permute-start(bf16[2,256,512]{2,1,0:T(8,128)(2,1)} %collective-permute-done.10), channel_id=1, source_target_pairs={{8,0},{10,2},{12,4},{14,6},{16,8},{18,10},{20,12},{22,14},{24,16},... | collective-permute-start | bytes 1572872 | tf_op jit(solution)/shard_map/ppermute | solution.py:240
  69.7 39.0 %collective-permute-start.13 = (bf16[2,256,512]{2,1,0:T(8,128)(2,1)}, bf16[2,256,512]{2,1,0:T(8,128)(2,1)S(1)}, u32[]{:S(2)}, u32[]{:S(2)}) collective-permute-start(bf16[2,256,512]{2,1,0:T(8,128)(2,1)} %collective-permute-done.9), channel_id=1, source_target_pairs={{0,8},{2,10},{4,12},{6,14},{8,16},{10,18},{12,20},{14,22},{16,24},... | collective-permute-start | bytes 1572872 | tf_op jit(solution)/shard_map/ppermute | solution.py:239
  75.4 43.2 %collective-permute-start.3 = (bf16[2,256,512]{2,1,0:T(8,128)(2,1)S(1)}, bf16[2,256,512]{2,1,0:T(8,128)(2,1)S(1)}, u32[]{:S(2)}, u32[]{:S(2)}) collective-permute-start(bf16[2,256,512]{2,1,0:T(8,128)(2,1)S(1)} %copy-done.9), channel_id=1, source_target_pairs={{8,0},{10,2},{12,4},{14,6},{16,8},{18,10},{20,12},{22,14},{24,16},... | collective-permute-start | bytes 1572872 | tf_op jit(solution)/shard_map/ppermute | solution.py:240
  80.4 39.5 %collective-permute-start.5 = (bf16[2,256,512]{2,1,0:T(8,128)(2,1)}, bf16[2,256,512]{2,1,0:T(8,128)(2,1)S(1)}, u32[]{:S(2)}, u32[]{:S(2)}) collective-permute-start(bf16[2,256,512]{2,1,0:T(8,128)(2,1)} %collective-permute-done.1), channel_id=1, source_target_pairs={{0,8},{2,10},{4,12},{6,14},{8,16},{10,18},{12,20},{14,22},{16,24},... | collective-permute-start | bytes 1572872 | tf_op jit(solution)/shard_map/ppermute | solution.py:239
  87.6 43.6 %collective-permute-start.30 = (bf16[2,256,512]{2,1,0:T(8,128)(2,1)}, bf16[2,256,512]{2,1,0:T(8,128)(2,1)S(1)}, u32[]{:S(2)}, u32[]{:S(2)}) collective-permute-start(bf16[2,256,512]{2,1,0:T(8,128)(2,1)} %collective-permute-done.29), channel_id=1, source_target_pairs={{0,8},{2,10},{4,12},{6,14},{8,16},{10,18},{12,20},{14,22},{16,24},... | collective-permute-start | bytes 1572872 | tf_op jit(solution)/shard_map/ppermute | solution.py:239
  107.0 37.8 %collective-permute-start.28 = (bf16[2,256,512]{2,1,0:T(8,128)(2,1)}, bf16[2,256,512]{2,1,0:T(8,128)(2,1)S(1)}, u32[]{:S(2)}, u32[]{:S(2)}) collective-permute-start(bf16[2,256,512]{2,1,0:T(8,128)(2,1)} %collective-permute-done.27), channel_id=1, source_target_pairs={{8,0},{10,2},{12,4},{14,6},{16,8},{18,10},{20,12},{22,14},{24,16},... | collective-permute-start | bytes 1572872 | tf_op jit(solution)/shard_map/ppermute | solution.py:240
  108.7 33.7 %collective-permute-start.22 = (bf16[2,256,512]{2,1,0:T(8,128)(2,1)}, bf16[2,256,512]{2,1,0:T(8,128)(2,1)S(1)}, u32[]{:S(2)}, u32[]{:S(2)}) collective-permute-start(bf16[2,256,512]{2,1,0:T(8,128)(2,1)} %collective-permute-done.21), channel_id=1, source_target_pairs={{0,8},{2,10},{4,12},{6,14},{8,16},{10,18},{12,20},{14,22},{16,24},... | collective-permute-start | bytes 1572872 | tf_op jit(solution)/shard_map/ppermute | solution.py:239
  118.6 36.7 %collective-permute-start.20 = (bf16[2,256,512]{2,1,0:T(8,128)(2,1)}, bf16[2,256,512]{2,1,0:T(8,128)(2,1)S(1)}, u32[]{:S(2)}, u32[]{:S(2)}) collective-permute-start(bf16[2,256,512]{2,1,0:T(8,128)(2,1)} %collective-permute-done.19), channel_id=1, source_target_pairs={{8,0},{10,2},{12,4},{14,6},{16,8},{18,10},{20,12},{22,14},{24,16},... | collective-permute-start | bytes 1572872 | tf_op jit(solution)/shard_map/ppermute | solution.py:240
  119.9 37.8 %collective-permute-start.14 = (bf16[2,256,512]{2,1,0:T(8,128)(2,1)S(1)}, bf16[2,256,512]{2,1,0:T(8,128)(2,1)S(1)}, u32[]{:S(2)}, u32[]{:S(2)}) collective-permute-start(bf16[2,256,512]{2,1,0:T(8,128)(2,1)S(1)} %collective-permute-done.13), channel_id=1, source_target_pairs={{0,8},{2,10},{4,12},{6,14},{8,16},{10,18},{12,20},{14,22},{16,24},... | collective-permute-start | bytes 1572872 | tf_op jit(solution)/shard_map/ppermute | solution.py:239
  129.8 25.2 %copy-start.7 = (bf16[2,256,512]{2,1,0:T(8,128)(2,1)S(1)}, bf16[2,256,512]{2,1,0:T(8,128)(2,1)}, u32[]{:S(2)}) copy-start(bf16[2,256,512]{2,1,0:T(8,128)(2,1)} %copy-done.6) | copy-start | bytes 1572868
  131.2 27.8 %collective-permute-start.12 = (bf16[2,256,512]{2,1,0:T(8,128)(2,1)S(1)}, bf16[2,256,512]{2,1,0:T(8,128)(2,1)S(1)}, u32[]{:S(2)}, u32[]{:S(2)}) collective-permute-start(bf16[2,256,512]{2,1,0:T(8,128)(2,1)S(1)} %collective-permute-done.11), channel_id=1, source_target_pairs={{8,0},{10,2},{12,4},{14,6},{16,8},{18,10},{20,12},{22,14},{24,16},... | collective-permute-start | bytes 1572872 | tf_op jit(solution)/shard_map/ppermute | solution.py:240
  142.4 19.9 %collective-permute-start.4 = (bf16[2,256,512]{2,1,0:T(8,128)(2,1)S(1)}, bf16[2,256,512]{2,1,0:T(8,128)(2,1)S(1)}, u32[]{:S(2)}, u32[]{:S(2)}) collective-permute-start(bf16[2,256,512]{2,1,0:T(8,128)(2,1)S(1)} %collective-permute-done.3), channel_id=1, source_target_pairs={{8,0},{10,2},{12,4},{14,6},{16,8},{18,10},{20,12},{22,14},{24,16},... | collective-permute-start | bytes 1572872 | tf_op jit(solution)/shard_map/ppermute | solution.py:240
  144.8 18.8 %collective-permute-start.6 = (bf16[2,256,512]{2,1,0:T(8,128)(2,1)S(1)}, bf16[2,256,512]{2,1,0:T(8,128)(2,1)S(1)}, u32[]{:S(2)}, u32[]{:S(2)}) collective-permute-start(bf16[2,256,512]{2,1,0:T(8,128)(2,1)S(1)} %collective-permute-done.5), channel_id=1, source_target_pairs={{0,8},{2,10},{4,12},{6,14},{8,16},{10,18},{12,20},{14,22},{16,24},... | collective-permute-start | bytes 1572872 | tf_op jit(solution)/shard_map/ppermute | solution.py:239
  155.3 39.2 %collective-permute-start.31 = (bf16[4,2,256,512]{3,2,1,0:T(8,128)(2,1)S(1)}, bf16[4,2,256,512]{3,2,1,0:T(8,128)(2,1)}, u32[]{:S(2)}, u32[]{:S(2)}) collective-permute-start(bf16[4,2,256,512]{3,2,1,0:T(8,128)(2,1)S(1)} %pad_maximum_fusion.4.own), channel_id=1, source_target_pairs={{0,2},{2,0},{4,6},{6,4},{8,10},{10,8},{12,14},{14,12},{16,18},{18,... | collective-permute-start | bytes 6291464 | tf_op jit(solution)/shard_map/ppermute | solution.py:280
  157.7 43.5 %collective-permute-start.23 = (bf16[4,2,256,512]{3,2,1,0:T(8,128)(2,1)}, bf16[4,2,256,512]{3,2,1,0:T(8,128)(2,1)}, u32[]{:S(2)}, u32[]{:S(2)}) collective-permute-start(bf16[4,2,256,512]{3,2,1,0:T(8,128)(2,1)} %pad_maximum_fusion.3.own), channel_id=1, source_target_pairs={{0,2},{2,0},{4,6},{6,4},{8,10},{10,8},{12,14},{14,12},{16,18},{18,... | collective-permute-start | bytes 6291464 | tf_op jit(solution)/shard_map/ppermute | solution.py:280
  159.0 4.6 %copy-start.10 = (bf16[2,256,512]{2,1,0:T(8,128)(2,1)S(1)}, bf16[2,256,512]{2,1,0:T(8,128)(2,1)}, u32[]{:S(2)}) copy-start(bf16[2,256,512]{2,1,0:T(8,128)(2,1)} %copy-done.8) | copy-start | bytes 1572868
  160.7 46.5 %collective-permute-start.15 = (bf16[4,2,256,512]{3,2,1,0:T(8,128)(2,1)}, bf16[4,2,256,512]{3,2,1,0:T(8,128)(2,1)}, u32[]{:S(2)}, u32[]{:S(2)}) collective-permute-start(bf16[4,2,256,512]{3,2,1,0:T(8,128)(2,1)} %pad_maximum_fusion.2.own), channel_id=1, source_target_pairs={{0,2},{2,0},{4,6},{6,4},{8,10},{10,8},{12,14},{14,12},{16,18},{18,... | collective-permute-start | bytes 6291464 | tf_op jit(solution)/shard_map/ppermute | solution.py:280
  166.3 48.0 %collective-permute-start.7 = (bf16[4,2,256,512]{3,2,1,0:T(8,128)(2,1)}, bf16[4,2,256,512]{3,2,1,0:T(8,128)(2,1)}, u32[]{:S(2)}, u32[]{:S(2)}) collective-permute-start(bf16[4,2,256,512]{3,2,1,0:T(8,128)(2,1)} %pad_maximum_fusion.1.own), channel_id=1, source_target_pairs={{0,2},{2,0},{4,6},{6,4},{8,10},{10,8},{12,14},{14,12},{16,18},{18,... | collective-permute-start | bytes 6291464 | tf_op jit(solution)/shard_map/ppermute | solution.py:280
  167.4 25.8 %collective-permute-start = (bf16[2,2,2,256,256]{4,3,2,1,0:T(8,128)(2,1)}, bf16[2,2,2,256,256]{4,3,2,1,0:T(8,128)(2,1)S(1)}, u32[]{:S(2)}, u32[]{:S(2)}) collective-permute-start(bf16[2,2,2,256,256]{4,3,2,1,0:T(8,128)(2,1)} %bitcast.9), channel_id=1, source_target_pairs={{0,1},{1,0},{2,3},{3,2},{4,5},{5,4},{6,7},{7,6},{8,9},{9,8},{10,11... | collective-permute-start | bytes 3145736 | tf_op jit(solution)/shard_map/ppermute | solution.py:267
  169.8 17.7 %all-to-all-start = ((bf16[16,16,1]{1,2,0:T(2,128)(2,1)}), bf16[16,16,1]{1,2,0:T(2,128)(2,1)S(1)}, u32[]{:S(2)}, u32[]{:S(2)}) async-start(bf16[16,16,1]{1,2,0:T(2,128)(2,1)} %all_to_all.16), calls=%async_computation | async-start | bytes 16384 | tf_op jit(solution)/shard_map/all_to_all | solution.py:288
  199.6 20.6 %collective-permute-start.32 = (bf16[2,256,512]{2,1,0:T(8,128)(2,1)S(1)}, bf16[2,256,512]{2,1,0:T(8,128)(2,1)S(1)}, u32[]{:S(2)}, u32[]{:S(2)}) collective-permute-start(bf16[2,256,512]{2,1,0:T(8,128)(2,1)S(1)} %get-tuple-element.25), channel_id=1, source_target_pairs={{0,4},{2,6},{4,0},{6,2},{8,12},{10,14},{12,8},{14,10},{16,20},{18,... | collective-permute-start | bytes 1572872 | tf_op jit(solution)/shard_map/ppermute | solution.py:301
  206.7 20.9 %collective-permute-start.24 = (bf16[2,256,512]{2,1,0:T(8,128)(2,1)S(1)}, bf16[2,256,512]{2,1,0:T(8,128)(2,1)S(1)}, u32[]{:S(2)}, u32[]{:S(2)}) collective-permute-start(bf16[2,256,512]{2,1,0:T(8,128)(2,1)S(1)} %get-tuple-element.23), channel_id=1, source_target_pairs={{0,4},{2,6},{4,0},{6,2},{8,12},{10,14},{12,8},{14,10},{16,20},{18,... | collective-permute-start | bytes 1572872 | tf_op jit(solution)/shard_map/ppermute | solution.py:301
  212.6 24.3 %collective-permute-start.16 = (bf16[2,256,512]{2,1,0:T(8,128)(2,1)S(1)}, bf16[2,256,512]{2,1,0:T(8,128)(2,1)S(1)}, u32[]{:S(2)}, u32[]{:S(2)}) collective-permute-start(bf16[2,256,512]{2,1,0:T(8,128)(2,1)S(1)} %get-tuple-element.21), channel_id=1, source_target_pairs={{0,4},{2,6},{4,0},{6,2},{8,12},{10,14},{12,8},{14,10},{16,20},{18,... | collective-permute-start | bytes 1572872 | tf_op jit(solution)/shard_map/ppermute | solution.py:301
  219.7 28.5 %collective-permute-start.8 = (bf16[2,256,512]{2,1,0:T(8,128)(2,1)S(1)}, bf16[2,256,512]{2,1,0:T(8,128)(2,1)S(1)}, u32[]{:S(2)}, u32[]{:S(2)}) collective-permute-start(bf16[2,256,512]{2,1,0:T(8,128)(2,1)S(1)} %get-tuple-element.19), channel_id=1, source_target_pairs={{0,4},{2,6},{4,0},{6,2},{8,12},{10,14},{12,8},{14,10},{16,20},{18,... | collective-permute-start | bytes 1572872 | tf_op jit(solution)/shard_map/ppermute | solution.py:301
  226.0 33.4 %collective-permute-start.36 = (bf16[2,256,512]{2,1,0:T(8,128)(2,1)S(1)}, bf16[2,256,512]{2,1,0:T(8,128)(2,1)S(1)}, u32[]{:S(2)}, u32[]{:S(2)}) collective-permute-start(bf16[2,256,512]{2,1,0:T(8,128)(2,1)S(1)} %get-tuple-element.33.mine), channel_id=1, source_target_pairs={{0,4},{2,6},{4,0},{6,2},{8,12},{10,14},{12,8},{14,10},{16,20},{18,... | collective-permute-start | bytes 1572872 | tf_op jit(solution)/shard_map/ppermute | solution.py:305
  233.5 37.2 %collective-permute-start.35 = (bf16[2,256,512]{2,1,0:T(8,128)(2,1)S(1)}, bf16[2,256,512]{2,1,0:T(8,128)(2,1)S(1)}, u32[]{:S(2)}, u32[]{:S(2)}) collective-permute-start(bf16[2,256,512]{2,1,0:T(8,128)(2,1)S(1)} %get-tuple-element.32.mine), channel_id=1, source_target_pairs={{0,4},{2,6},{4,0},{6,2},{8,12},{10,14},{12,8},{14,10},{16,20},{18,... | collective-permute-start | bytes 1572872 | tf_op jit(solution)/shard_map/ppermute | solution.py:305
  242.8 39.1 %collective-permute-start.34 = (bf16[2,256,512]{2,1,0:T(8,128)(2,1)S(1)}, bf16[2,256,512]{2,1,0:T(8,128)(2,1)S(1)}, u32[]{:S(2)}, u32[]{:S(2)}) collective-permute-start(bf16[2,256,512]{2,1,0:T(8,128)(2,1)S(1)} %get-tuple-element.31.mine), channel_id=1, source_target_pairs={{0,4},{2,6},{4,0},{6,2},{8,12},{10,14},{12,8},{14,10},{16,20},{18,... | collective-permute-start | bytes 1572872 | tf_op jit(solution)/shard_map/ppermute | solution.py:305
  254.0 37.9 %collective-permute-start.33 = (bf16[2,256,512]{2,1,0:T(8,128)(2,1)S(1)}, bf16[2,256,512]{2,1,0:T(8,128)(2,1)S(1)}, u32[]{:S(2)}, u32[]{:S(2)}) collective-permute-start(bf16[2,256,512]{2,1,0:T(8,128)(2,1)S(1)} %get-tuple-element.30.mine), channel_id=1, source_target_pairs={{0,4},{2,6},{4,0},{6,2},{8,12},{10,14},{12,8},{14,10},{16,20},{18,... | collective-permute-start | bytes 1572872 | tf_op jit(solution)/shard_map/ppermute | solution.py:305
  298.3 24.0 %collective-permute-start.37 = (bf16[2,2,2,256,256]{4,3,2,1,0:T(8,128)(2,1)S(1)}, bf16[2,2,2,256,256]{4,3,2,1,0:T(8,128)(2,1)S(1)}, u32[]{:S(2)}, u32[]{:S(2)}) collective-permute-start(bf16[2,2,2,256,256]{4,3,2,1,0:T(8,128)(2,1)S(1)} %slice.41), channel_id=1, source_target_pairs={{0,1},{1,0},{2,3},{3,2},{4,5},{5,4},{6,7},{7,6},{8,9},{9,8},{10,11... | collective-permute-start | bytes 3145736 | tf_op jit(solution)/shard_map/ppermute | solution.py:267
  (4 other events, 6.2 us)

commit v2 on v1

v2 whole, which is shorter than its diff:
```python
import functools
import math

import jax
import jax.numpy as jnp
from jax import lax
from jax.experimental import pallas as pl
from jax.experimental.pallas import tpu as pltpu
from jax.sharding import PartitionSpec as P

HD = 256
CAP_LIMIT = 10.0
VMEM_LIMIT = 48 * 1024 * 1024


def slot_table(labels, capacity, peer_count):
    targets = (labels[:, None] == jnp.arange(peer_count, dtype=jnp.int32)[None, :]).astype(
        jnp.int32
    )
    before = jnp.cumsum(targets, axis=0) - targets
    rank_in = jnp.sum(before * targets, axis=1)
    slot_index = labels * capacity + rank_in
    placement = jnp.arange(peer_count * capacity, dtype=jnp.int32)[:, None] == slot_index[None, :]
    return placement.astype(jnp.bfloat16)


def split_heads(head_count):
    if head_count < 4:
        return [1] * head_count
    part = (3 * head_count) // 8
    return [head_count - part, part]


def split_units(size):
    return [2] * (size // 2) + [1] * (size % 2)


ANYWHERE = pl.BlockSpec(memory_space=pl.ANY)


def predict_kernel(weights, velocity, *rest):
    result = rest[-1]
    for side in range(2):
        result[:, side * HD : (side + 1) * HD] = (
            weights[side].astype(jnp.float32) - velocity[side]
        ).astype(jnp.bfloat16)


def predict(projections, velocity, first, size, *tokens):
    depth = projections.shape[1]
    spec = pl.BlockSpec((2, depth, HD), lambda head: (0, 0, first + head))
    return pl.pallas_call(
        predict_kernel,
        grid=(size,),
        in_specs=[spec, spec] + [ANYWHERE] * len(tokens),
        out_specs=pl.BlockSpec((depth, 2 * HD), lambda head: (0, head)),
        out_shape=jax.ShapeDtypeStruct((depth, 2 * HD * size), jnp.bfloat16),
        cost_estimate=pl.CostEstimate(
            flops=2 * depth * HD * size, bytes_accessed=16 * depth * HD * size, transcendentals=0
        ),
        name="predict",
    )(projections, velocity, *tokens)


def arrange_kernel(pos, rows, result, *, line, tensor_count):
    per_tensor = line // tensor_count
    slots, depth = rows.shape[3:]
    for x_at in range(2):
        for z in range(line):
            shift = lax.rem(pos[3] - z // per_tensor + tensor_count, tensor_count)
            for core in range(2):
                first = (2 * z + core) * depth
                result[x_at * slots : (x_at + 1) * slots, first : first + depth] = rows[
                    shift * per_tensor + z % per_tensor, core, lax.rem(pos[1] + x_at, 2)
                ]


def arrange(pos, rows, line, tensor_count):
    slots, depth = rows.shape[3:]
    return pl.pallas_call(
        functools.partial(arrange_kernel, line=line, tensor_count=tensor_count),
        in_specs=[
            pl.BlockSpec(memory_space=pltpu.SMEM),
            pl.BlockSpec(memory_space=pltpu.VMEM),
        ],
        out_specs=pl.BlockSpec(memory_space=pltpu.VMEM),
        out_shape=jax.ShapeDtypeStruct((2 * slots, 2 * line * depth), jnp.bfloat16),
        compiler_params=pltpu.CompilerParams(vmem_limit_bytes=VMEM_LIMIT),
        cost_estimate=pl.CostEstimate(
            flops=0, bytes_accessed=4 * rows.size, transcendentals=0
        ),
        name="arrange",
    )(pos, rows)


def project_kernel(rows, weights, *rest):
    mine, other = rest[-2:]
    slots = mine.shape[0]
    total = jnp.dot(rows[...], weights[...], preferred_element_type=jnp.float32)
    mine[...] = total[:slots]
    other[...] = total[slots:].astype(other.dtype)


def project(rows, weights, first, width, *tokens):
    features = weights.shape[0]
    first_block = first // HD
    slots = rows.shape[0] // 2
    result_spec = pl.BlockSpec((slots, HD), lambda at: (0, at))
    return pl.pallas_call(
        project_kernel,
        grid=(width // HD,),
        in_specs=[
            pl.BlockSpec(rows.shape, lambda at: (0, 0)),
            pl.BlockSpec((features, HD), lambda at: (0, first_block + at)),
        ]
        + [ANYWHERE] * len(tokens),
        out_specs=[result_spec, result_spec],
        out_shape=(
            jax.ShapeDtypeStruct((slots, width), jnp.float32),
            jax.ShapeDtypeStruct((slots, width), jnp.bfloat16),
        ),
        compiler_params=pltpu.CompilerParams(vmem_limit_bytes=VMEM_LIMIT),
        cost_estimate=pl.CostEstimate(
            flops=2 * 2 * slots * features * width,
            bytes_accessed=2 * features * width + rows.size * 2 + 6 * slots * width,
            transcendentals=0,
        ),
        name="project",
    )(rows, weights, *tokens)


def attend_kernel(block, live, usable, queries, grads, mine, received, *rest):
    query_grad, pair_grad, key_total, value_total = rest[-4:]
    both = (mine[...] + received[...].astype(jnp.float32)).astype(jnp.bfloat16)
    keys, values = both[:, :HD], both[:, HD:]
    scale = 1.0 / math.sqrt(HD)
    mask = usable[...]
    last_dims = (((1,), (1,)), ((), ()))
    query_count = queries.shape[0]
    for first in range(0, query_count, block):
        at = pl.ds(first, block)
        q = queries[at, :]
        position = first + lax.broadcasted_iota(jnp.int32, (block, 1), 0)
        g = grads[at, :]
        g = jnp.where(position < live[0], g, jnp.zeros_like(g))
        raw = lax.dot_general(keys, q, last_dims, preferred_element_type=jnp.float32)
        bent = jnp.tanh(raw * (scale / CAP_LIMIT))
        terms = jnp.exp(bent * CAP_LIMIT) * mask
        attention = terms * (1.0 / jnp.sum(terms, axis=0, keepdims=True))
        prob_grad = lax.dot_general(values, g, last_dims, preferred_element_type=jnp.float32)
        row_term = jnp.sum(attention * prob_grad, axis=0, keepdims=True)
        score_grad = (
            attention * (prob_grad - row_term) * ((1.0 - bent * bent) * scale)
        ).astype(jnp.bfloat16)
        rounded = attention.astype(jnp.bfloat16)
        query_grad[at, :] = lax.dot_general(
            score_grad, keys, (((0,), (0,)), ((), ())), preferred_element_type=jnp.float32
        ).astype(jnp.bfloat16)
        key_block = jnp.dot(score_grad, q, preferred_element_type=jnp.float32)
        value_block = jnp.dot(rounded, g, preferred_element_type=jnp.float32)
        if first == 0:
            key_total[...] = key_block
            value_total[...] = value_block
        else:
            key_total[...] += key_block
            value_total[...] += value_block
    pair_grad[:, :HD] = key_total[...].astype(jnp.bfloat16)
    pair_grad[:, HD:] = value_total[...].astype(jnp.bfloat16)


def attend(live, usable, queries, grads, mine, received, first_head, earlier, *tokens):
    query_count, width = queries.shape
    slots, chunk = mine.shape
    heads = chunk // (2 * HD)
    block = min(256, query_count)
    columns = pl.BlockSpec((query_count, HD), lambda head: (0, first_head + head))
    pair = pl.BlockSpec((slots, 2 * HD), lambda head: (0, head))
    operands = [live, usable, queries, grads, mine, received]
    in_specs = [
        pl.BlockSpec(memory_space=pltpu.SMEM),
        pl.BlockSpec((slots, 1), lambda head: (0, 0)),
        columns,
        columns,
        pair,
        pair,
    ]
    aliases = {}
    if earlier is not None:
        aliases = {len(operands): 0}
        operands.append(earlier)
        in_specs.append(ANYWHERE)
    operands += tokens
    in_specs += [ANYWHERE] * len(tokens)
    return pl.pallas_call(
        functools.partial(attend_kernel, block),
        grid=(heads,),
        in_specs=in_specs,
        out_specs=[columns, pair],
        out_shape=(
            jax.ShapeDtypeStruct((query_count, width), jnp.bfloat16),
            jax.ShapeDtypeStruct((slots, chunk), jnp.bfloat16),
        ),
        scratch_shapes=[pltpu.VMEM((slots, HD), jnp.float32)] * 2,
        input_output_aliases=aliases,
        compiler_params=pltpu.CompilerParams(vmem_limit_bytes=VMEM_LIMIT),
        cost_estimate=pl.CostEstimate(
            flops=5 * query_count * slots * chunk,
            bytes_accessed=3 * query_count * chunk + 10 * slots * chunk,
            transcendentals=2 * query_count * slots * heads,
        ),
        name="attend",
    )(*operands)


def spread_kernel(pos, *refs, parts, sides, earlier):
    scratch = parts if len(sides) > 1 else 0
    result, joined = refs[len(refs) - 1 - scratch], refs[len(refs) - scratch :]
    stride = len(sides) + 1
    depth = result.shape[-1]
    slots = refs[0].shape[0]

    if scratch:

        @pl.when(pl.program_id(0) == 0)
        def _():
            for part in range(parts):
                for at in range(len(sides)):
                    joined[part][at * slots : (at + 1) * slots] = refs[stride * part + at][...]

    total = None
    for part in range(parts):
        grads = joined[part] if scratch else refs[stride * part]
        term = lax.dot_general(
            grads[...],
            refs[stride * part + stride - 1][...],
            (((1,), (1,)), ((), ())),
            preferred_element_type=jnp.float32,
        )
        total = term if total is None else total + term
    for core in range(2):
        for at in range(len(sides)):
            share = total[at * slots : (at + 1) * slots, core * depth : (core + 1) * depth]
            if earlier:
                share = share + refs[stride * parts][0, core, at]
            result[0, core, at] = share.astype(result.dtype)


def spread(pos, depth, units, earlier, sides, first, count, tensor_count, dtype, *tokens):
    line = units[0][2].shape[0] // (2 * depth)
    slots = units[0][0].shape[0]
    per_tensor = line // tensor_count

    def weight_at(column):
        def index(step, pos):
            block = first + step
            return (
                lax.rem(pos[3] + block // per_tensor, tensor_count) * per_tensor
                + lax.rem(block, per_tensor),
                column,
            )

        return index

    operands, in_specs, scratch, widths = [pos], [], [], 0
    for unit in units:
        width = unit[0].shape[1]
        for side in sides:
            operands.append(unit[side])
            in_specs.append(pl.BlockSpec((slots, width), lambda step, pos: (0, 0)))
        operands.append(unit[2])
        in_specs.append(pl.BlockSpec((2 * depth, width), weight_at(unit[3] // width)))
        if len(sides) > 1:
            scratch.append(pltpu.VMEM((len(sides) * slots, width), jnp.bfloat16))
        widths += width
    block = (1, 2, len(sides), slots, depth)
    if earlier is not None:
        operands.append(earlier)
        side = sides[0] if len(sides) == 1 else 0
        in_specs.append(pl.BlockSpec(block, lambda step, pos: (first + step, 0, side, 0, 0)))
    operands += tokens
    in_specs += [ANYWHERE] * len(tokens)
    return pl.pallas_call(
        functools.partial(
            spread_kernel, parts=len(units), sides=sides, earlier=earlier is not None
        ),
        grid_spec=pltpu.PrefetchScalarGridSpec(
            num_scalar_prefetch=1,
            grid=(count,),
            in_specs=in_specs,
            out_specs=pl.BlockSpec(block, lambda step, pos: (step, 0, 0, 0, 0)),
            scratch_shapes=scratch,
        ),
        out_shape=jax.ShapeDtypeStruct((count,) + block[1:], dtype),
        compiler_params=pltpu.CompilerParams(vmem_limit_bytes=VMEM_LIMIT),
        cost_estimate=pl.CostEstimate(
            flops=2 * len(sides) * slots * 2 * count * depth * widths,
            bytes_accessed=4 * count * depth * widths + 8 * count * math.prod(block),
            transcendentals=0,
        ),
        name="spread",
    )(*operands)


def on_device(queries, out_grad, target_len, encoded, row_owner, projections, velocity):
    peers = lax.axis_size("dp")
    tensor_count = lax.axis_size("tensor")
    line = peers // 4
    per_tensor = line // tensor_count
    stored_rows = encoded.shape[0]
    depth = projections.shape[1]
    capacity = max(2, 2 * stored_rows // peers)
    slots = peers * capacity
    place = lax.axis_index("dp")
    tensor_at = lax.axis_index("tensor")
    pos = jnp.stack([place // 4, (place // 2) % 2, place % 2, tensor_at]).astype(jnp.int32)
    columns = [[i for i in range(peers) if (i // 2) % 2 == side] for side in range(2)]
    x_swap = [(i, i ^ 2) for i in range(peers)]

    def tensor_shift(value, shift):
        pairs = [(i, (i + shift) % tensor_count) for i in range(tensor_count)]
        return lax.ppermute(value, "tensor", pairs)

    placement = slot_table(row_owner[:, 0], capacity, peers)
    filled = jnp.sum(placement.astype(jnp.float32), axis=1).astype(jnp.bfloat16)
    flags = filled.reshape(line, 1, 2, 2, capacity).transpose(0, 1, 3, 4, 2)
    flags = jnp.broadcast_to(flags, (line, 2, 2, capacity, 2)).reshape(peers, capacity, 2)
    flags = jnp.pad(flags, ((0, 0), (0, 0), (0, depth - 2)))
    outgoing = jnp.dot(placement, encoded, preferred_element_type=jnp.float32).astype(jnp.bfloat16)
    outgoing = outgoing.reshape(line, 2, 2, capacity, per_tensor, 2, 2, depth)
    outgoing = outgoing.transpose(0, 5, 2, 4, 6, 1, 3, 7).reshape(peers, -1, depth)
    outgoing = jnp.concatenate([outgoing, flags], axis=1)

    parts = []
    first, token = 0, ()
    for size in split_heads(queries.shape[1] // HD):
        block = predict(projections, velocity, first, size, *token)
        gathered = lax.all_gather(block, "dp", axis=0, tiled=True, axis_index_groups=columns)
        parts.append((first, size, gathered))
        first, token = first + size, (block, outgoing)

    incoming = lax.all_to_all(outgoing, "dp", split_axis=0, concat_axis=0, tiled=True)
    usable = jnp.where(
        pos[1] == 0, incoming[:, -capacity:, 0], incoming[:, -capacity:, 1]
    ).reshape(slots, 1)
    usable = (usable.astype(jnp.float32) > 0.5).astype(jnp.float32)
    incoming = incoming[:, :-capacity].reshape(peers, per_tensor, 2, 2, capacity, depth)
    incoming = incoming.transpose(1, 2, 3, 0, 4, 5).reshape(per_tensor, 2, 2, slots, depth)
    rows = jnp.concatenate(
        [incoming] + [tensor_shift(incoming, shift) for shift in range(1, tensor_count)]
    )
    rows = arrange(pos, rows, line, tensor_count)

    query_grad, token, units, early = None, (), [], None
    for at, (first, size, weights) in enumerate(parts):
        final = at == len(parts) - 1
        if final:
            early = spread(
                pos, depth, units, None, (0, 1), 0, line, tensor_count, jnp.float32
            )
            units = []
        products, column = [], 0
        for heads in split_units(size):
            width = 2 * HD * heads
            mine, other = project(rows, weights, column, width, *token)
            products.append((column, mine, lax.ppermute(other, "dp", x_swap)))
            column += width
        for column, mine, received in products:
            query_grad, pair_grad = attend(
                target_len,
                usable,
                queries,
                out_grad,
                mine,
                received,
                first + column // (2 * HD),
                query_grad,
                *((early,) if final else ()),
            )
            units.append((pair_grad, lax.ppermute(pair_grad, "dp", x_swap), weights, column))
            token = (pair_grad,)

    def finish(side, *tokens):
        sent = spread(
            pos, depth, units, early, (side,), per_tensor, line - per_tensor, tensor_count,
            jnp.bfloat16, *tokens,
        )
        passed = [
            tensor_shift(sent[(shift - 1) * per_tensor : shift * per_tensor], shift)
            for shift in range(1, tensor_count)
        ]
        kept = spread(
            pos, depth, units, early, (side,), 0, per_tensor, tensor_count, jnp.float32, sent
        )
        return kept, passed

    def send_home(kept, passed):
        for part in passed:
            kept = kept + part.astype(jnp.float32)
        kept = kept.astype(jnp.bfloat16).reshape(per_tensor, 2, peers, capacity, depth)
        kept = kept.transpose(2, 0, 1, 3, 4).reshape(peers, -1, depth)
        returned = lax.all_to_all(kept, "dp", split_axis=0, concat_axis=0, tiled=True)
        return returned.reshape(line, 2, 2, per_tensor, 2, capacity, depth)

    own_side = finish(0)
    other_side = finish(1, own_side[0])
    homes = placement.reshape(line, 2, 2, capacity, stored_rows)
    encoded_grad = jnp.einsum(
        "zxckr,zxcpqkd->rpxqd", homes, send_home(*own_side), preferred_element_type=jnp.float32
    ) + jnp.einsum(
        "zxckr,zxcpqkd->rpxqd",
        homes[:, ::-1],
        send_home(*other_side),
        preferred_element_type=jnp.float32,
    )
    return (query_grad, encoded_grad.astype(jnp.bfloat16).reshape(stored_rows, -1))


def solution(mesh):
    in_specs = (
        P("dp", "tensor"),
        P("dp", "tensor"),
        P("dp"),
        P("dp", "tensor"),
        P("dp", None),
        P(None, "dp", "tensor"),
        P(None, "dp", "tensor"),
    )
    out_specs = (P("dp", "tensor"), P("dp", "tensor"))
    return jax.shard_map(
        on_device, mesh=mesh, in_specs=in_specs, out_specs=out_specs, check_vma=False
    )
```

time: 364 us -> 304 us (0.84)
  starting transfers between devices: 119 us -> 24 us
  blocking collectives: 36.1 us -> 67.9 us
  other arithmetic: 19 us -> 3.45 us
  between operations: 1.89 us -> 15 us
  Pallas kernels: 73.2 us -> 80.4 us
    ppermute x36 -> x10, starting transfers between devices: 100 us -> 11.2 us  [the longest x5 5.72 us: on_device(): products.append((column, mine, lax.ppermute(other, 'dp', x_swap)))]
    ppermute x36 -> x10, waiting for transfers between devices: 70.5 us -> 7.97 us  [the longest x5 5.74 us: on_device(): products.append((column, mine, lax.ppermute(other, 'dp', x_swap)))]
    all_gather x0 -> x2, waiting for transfers between devices: none -> 44.4 us  [on_device(): lax.all_gather(block, 'dp', axis=0, tiled=True, axis_index_groups=columns)]
    all_to_all x1, blocking collectives: 36.1 us -> 67.9 us  [on_device(): lax.all_to_all(outgoing, 'dp', split_axis=0, concat_axis=0, tiled=True)]
    another operation x17 -> x1, other arithmetic: 12.4 us -> 0.08 us  [on_device(): jnp.stack([place // 4, place // 2 % 2, place % 2, tensor_at])]
    ppermute x2 -> x3, waiting for transfers between devices: 27.7 us -> 38.6 us  [tensor_shift(): return lax.ppermute(value, 'tensor', pairs)]
    all_to_all x2, waiting for transfers between devices: 5.56 us -> 13.9 us  [send_home(): lax.all_to_all(kept, 'dp', split_axis=0, concat_axis=0, tiled=True)]
    all_to_all x2, starting transfers between devices: 15.2 us -> 9.02 us  [send_home(): lax.all_to_all(kept, 'dp', split_axis=0, concat_axis=0, tiled=True)]
  transfers between devices with their start and end apart: 40 -> 17, of which waited for: 21 -> 9; matrix products, arithmetic and copies ran while one was open for 5% -> 3% of each run, Pallas kernels for 19% -> 23%
where the time goes in v2:
time: 304 us; the launch traced here: 303 us
  waiting for transfers between devices  105 us (35%)
  Pallas kernels  80.4 us (26%)
  blocking collectives  67.9 us (22%)
  starting transfers between devices  24 us (8%)
  between operations  15 us (5%)
  local copies, waits for them, and re-layouts  6.47 us (2%)
  other arithmetic  3.45 us (1%)
    all_to_all x1, blocking collectives, on_device(): lax.all_to_all(outgoing, 'dp', split_axis=0, concat_axis=0, tiled=True)  67.9 us
    all_gather x2, waiting for transfers between devices, on_device(): lax.all_gather(block, 'dp', axis=0, tiled=True, axis_index_groups=columns)  44.4 us
    ppermute x3, waiting for transfers between devices, tensor_shift(): return lax.ppermute(value, 'tensor', pairs)  38.6 us
    pallas_call x5, Pallas kernels, attend(): pl.pallas_call(functools.partial(attend_kernel, block), grid=(heads,), in...  26 us
    pallas_call x5, Pallas kernels, spread(): pl.pallas_call(functools.partial(spread_kernel, parts=len(units), sides=s...  24.5 us
    pallas_call x5, Pallas kernels, project(): pl.pallas_call(project_kernel, grid=(width // HD,), in_specs=[pl.BlockSpe...  21.1 us
    all_to_all x2, waiting for transfers between devices, send_home(): lax.all_to_all(kept, 'dp', split_axis=0, concat_axis=0, tiled=True)  13.9 us
    all_to_all x2, starting transfers between devices, send_home(): lax.all_to_all(kept, 'dp', split_axis=0, concat_axis=0, tiled=True)  9.02 us
  transfers between devices with their start and end apart: 17, of which 9 were waited for; matrix products, arithmetic and copies ran while one was open for 3% of the time, Pallas kernels for 23%

profile of v2, /device:TPU:0, one launch (start us, length us, event | category | flops | bytes accessed | tf_op | source)
XLA Modules:
  0.0 303.3 jit_solution(2078873180397663631)
XLA Ops:
  7.2 4.6 %predict.2.rest_0_ = bf16[256,2560]{1,0:T(8,128)(2,1)} custom-call(bf16[2,256,2048]{2,1,0:T(8,128)(2,1)} %weights.3, f32[2,256,2048]{2,1,0:T(8,128)} %velocity.3), custom_call_target="tpu_custom_call" | custom-call | flops 655360 | bytes 5242880 | tf_op jit(solution)/shard_map/predict/pallas_call | solution.py:52
  12.8 0.8 reshape.122
  14.3 1.1 fusion.1.rest_1_
  15.4 3.4 %predict.3 = bf16[256,1536]{1,0:T(8,128)(2,1)} custom-call(bf16[2,256,2048]{2,1,0:T(8,128)(2,1)} %weights.3, f32[2,256,2048]{2,1,0:T(8,128)} %velocity.3, bf16[256,2560]{1,0:T(8,128)(2,1)} %predict.2.rest_0_, bf16[16,144,256]{2,1,0:T(8,128)(2,1)} %fusion.1.rest_1_), custom_call_target="tpu_custom_call" | custom-call | flops 393216 | bytes 3145728 | tf_op jit(solution)/shard_map/predict/pallas_call | solution.py:52
  18.8 67.9 %all_to_all.15 = bf16[16,144,256]{2,1,0:T(8,128)(2,1)} all-to-all(bf16[16,144,256]{2,1,0:T(8,128)(2,1)S(1)} %copy-done.7), channel_id=1, replica_groups=mesh['dp'=16,'tensor'=2] {'dp'}, dimensions={0} | all-to-all | bytes 2359296 | tf_op jit(solution)/shard_map/all_to_all | solution.py:341
  86.7 1.3 slice.14
  88.1 1.5 collective-permute-start
  89.7 23.6 %collective-permute-done = bf16[2,2,2,256,256]{4,3,2,1,0:T(8,128)(2,1)S(1)} collective-permute-done((bf16[2,2,2,256,256]{4,3,2,1,0:T(8,128)(2,1)S(1)}, bf16[2,2,2,256,256]{4,3,2,1,0:T(8,128)(2,1)S(1)}, u32[]{:S(2)}, u32[]{:S(2)}) %collective-permute-start) | collective-permute-done | bytes 1048608 | tf_op jit(solution)/shard_map/ppermute | solution.py:321
  113.5 0.8 arrange.1.rows
  114.3 24.8 %all-gather.5.cloned.1.call-done.weights.refs_2_.refs_5_.refs_8_ = bf16[2048,2560]{1,0:T(8,128)(2,1)} async-done(((bf16[256,2560]{1,0:T(8,128)(2,1)}), bf16[2048,2560]{1,0:T(8,128)(2,1)}) %all-gather.5.cloned.1.call-update) | async-done | bytes 10485776 | tf_op jit(solution)/shard_map/all_gather | solution.py:337
  139.1 5.4 %project.7 = (f32[256,1024]{1,0:T(8,128)S(1)}, bf16[256,1024]{1,0:T(8,128)(2,1)}) custom-call(bf16[512,2048]{1,0:T(8,128)(2,1)S(1)} %arrange.1.rows, bf16[2048,2560]{1,0:T(8,128)(2,1)} %all-gather.5.cloned.1.call-done.weights.refs_2_.refs_5_.refs_8_), custom_call_target="tpu_custom_call" | custom-call | flops 2147483648 | bytes 7864320 | tf_op jit(solution)/shard_map/project/pallas_call | solution.py:109
  144.5 1.5 collective-permute-start.3
  146.0 5.5 %project.6 = (f32[256,1024]{1,0:T(8,128)S(1)}, bf16[256,1024]{1,0:T(8,128)(2,1)}) custom-call(bf16[512,2048]{1,0:T(8,128)(2,1)S(1)} %arrange.1.rows, bf16[2048,2560]{1,0:T(8,128)(2,1)} %all-gather.5.cloned.1.call-done.weights.refs_2_.refs_5_.refs_8_), custom_call_target="tpu_custom_call" | custom-call | flops 2147483648 | bytes 7864320 | tf_op jit(solution)/shard_map/project/pallas_call | solution.py:109
  151.5 1.0 copy-done.5
  152.5 0.8 collective-permute-start.2
  153.9 1.0 fusion.9
  154.9 2.7 project.5
  157.7 1.3 collective-permute-start.1
  159.6 6.1 %attend.5 = (bf16[1024,2048]{1,0:T(8,128)(2,1)}, bf16[256,1024]{1,0:T(8,128)(2,1)}) custom-call(s32[1]{0:T(128)S(6)} %copy.55.live, f32[256,1]{1,0:T(8,128)S(1)} %bitcast.52, bf16[1024,2048]{1,0:T(8,128)(2,1)} %queries.9, bf16[1024,2048]{1,0:T(8,128)(2,1)} %grads.9, f32[256,1024]{1,0:T(8,128)S(1)} %get-tuple-element.26.mine, ...), custom_call_target="tpu_custom_call" | custom-call | flops 1342177280 | bytes 5767168 | tf_op jit(solution)/shard_map/attend/pallas_call | solution.py:194
  165.7 5.1 %collective-permute-done.2.received = bf16[256,1024]{1,0:T(8,128)(2,1)} collective-permute-done((bf16[256,1024]{1,0:T(8,128)(2,1)}, bf16[256,1024]{1,0:T(8,128)(2,1)}, u32[]{:S(2)}, u32[]{:S(2)}) %collective-permute-start.2) | collective-permute-done | bytes 524320 | tf_op jit(solution)/shard_map/ppermute | solution.py:365
  170.8 6.0 %attend.6 = (bf16[1024,2048]{1,0:T(8,128)(2,1)}, bf16[256,1024]{1,0:T(8,128)(2,1)S(1)}) custom-call(s32[1]{0:T(128)S(6)} %copy.55.live, f32[256,1]{1,0:T(8,128)S(1)} %bitcast.53, bf16[1024,2048]{1,0:T(8,128)(2,1)} %queries.9, bf16[1024,2048]{1,0:T(8,128)(2,1)} %grads.9, f32[256,1024]{1,0:T(8,128)S(1)} %copy-done.6, ...), custom_call_target="tpu_custom_call", output_to_operand_aliasing={{0}: (6, {})} | custom-call | flops 1342177280 | bytes 5767168 | tf_op jit(solution)/shard_map/attend/pallas_call | solution.py:194
  176.9 1.5 collective-permute-start.7
  178.9 3.8 %attend.7 = (bf16[1024,2048]{1,0:T(8,128)(2,1)}, bf16[256,512]{1,0:T(8,128)(2,1)S(1)}) custom-call(s32[1]{0:T(128)S(6)} %copy.55.live, f32[256,1]{1,0:T(8,128)S(1)} %bitcast.54, bf16[1024,2048]{1,0:T(8,128)(2,1)S(1)} %copy-done.3, bf16[1024,2048]{1,0:T(8,128)(2,1)} %grads.9, f32[256,512]{1,0:T(8,128)S(1)} %get-tuple-element.22.mine, ...), custom_call_target="tpu_custom_call", output_to_operand_aliasing={{0}: (6, {})} | custom-call | flops 671088640 | bytes 2883584 | tf_op jit(solution)/shard_map/attend/pallas_call | solution.py:194
  182.7 1.5 collective-permute-start.8
  184.2 19.7 %all-gather.3.cloned.1.call-done.weights.refs_1_.refs_3_ = bf16[2048,1536]{1,0:T(8,128)(2,1)} async-done(((bf16[256,1536]{1,0:T(8,128)(2,1)}), bf16[2048,1536]{1,0:T(8,128)(2,1)}) %all-gather.3.cloned.1.call-update) | async-done | bytes 6291472 | tf_op jit(solution)/shard_map/all_gather | solution.py:337
  203.8 4.7 %project.9 = (f32[256,1024]{1,0:T(8,128)S(1)}, bf16[256,1024]{1,0:T(8,128)(2,1)S(1)}) custom-call(bf16[512,2048]{1,0:T(8,128)(2,1)S(1)} %arrange.1.rows, bf16[2048,1536]{1,0:T(8,128)(2,1)} %all-gather.3.cloned.1.call-done.weights.refs_1_.refs_3_, bf16[256,512]{1,0:T(8,128)(2,1)S(1)} %get-tuple-element.30.rest_0_.refs_6_), custom_call_target="tpu_custom_call" | custom-call | flops 2147483648 | bytes 7864320 | tf_op jit(solution)/shard_map/project/pallas_call | solution.py:109
  208.6 1.5 collective-permute-start.5
  210.1 2.7 project.8
  212.8 0.6 collective-permute-start.4
  213.5 11.0 %spread.5.rest_1_.refs_4_ = f32[4,2,2,256,256]{4,3,2,1,0:T(8,128)} custom-call(s32[4]{0:T(128)S(1)} %pad_add_fusion.pos, bf16[256,1024]{1,0:T(8,128)(2,1)} %get-tuple-element.36.refs_0_, bf16[256,1024]{1,0:T(8,128)(2,1)} %collective-permute-done.6.refs_1_, bf16[2048,2560]{1,0:T(8,128)(2,1)} %all-gather.5.cloned.1.call-done.weights.refs_2_.refs_5_.refs_8_, ...), custom_call_target="tpu_custom_call" | custom-call | flops 5368709120 | bytes 18874368 | tf_op jit(solution)/shard_map/spread/pallas_call | solution.py:282
  224.5 6.2 %attend.8 = (bf16[1024,2048]{1,0:T(8,128)(2,1)}, bf16[256,1024]{1,0:T(8,128)(2,1)S(1)}) custom-call(s32[1]{0:T(128)S(6)} %copy.55.live, f32[256,1]{1,0:T(8,128)S(1)} %bitcast.55, bf16[1024,2048]{1,0:T(8,128)(2,1)} %queries.9, bf16[1024,2048]{1,0:T(8,128)(2,1)} %grads.9, f32[256,1024]{1,0:T(8,128)S(1)} %get-tuple-element.33.mine, ...), custom_call_target="tpu_custom_call", output_to_operand_aliasing={{0}: (6, {})} | custom-call | flops 1342177280 | bytes 5767168 | tf_op jit(solution)/shard_map/attend/pallas_call | solution.py:194
  230.7 3.9 %attend.9 = (bf16[1024,2048]{1,0:T(8,128)(2,1)}, bf16[256,512]{1,0:T(8,128)(2,1)S(1)}) custom-call(s32[1]{0:T(128)S(6)} %copy.55.live, f32[256,1]{1,0:T(8,128)S(1)} %bitcast.56, bf16[1024,2048]{1,0:T(8,128)(2,1)S(1)} %copy-done.4, bf16[1024,2048]{1,0:T(8,128)(2,1)} %grads.9, f32[256,512]{1,0:T(8,128)S(1)} %get-tuple-element.31.mine, ...), custom_call_target="tpu_custom_call", output_to_operand_aliasing={{0}: (6, {})} | custom-call | flops 671088640 | bytes 2883584 | tf_op jit(solution)/shard_map/attend/pallas_call | solution.py:194
  234.6 3.2 %spread.6.refs_5_ = bf16[2,2,1,256,256]{4,3,2,1,0:T(8,128)(2,1)S(1)} custom-call(s32[4]{0:T(128)S(1)} %pad_add_fusion.pos, bf16[256,1024]{1,0:T(8,128)(2,1)S(1)} %get-tuple-element.40.refs_0_, bf16[2048,1536]{1,0:T(8,128)(2,1)} %all-gather.3.cloned.1.call-done.weights.refs_1_.refs_3_, bf16[256,512]{1,0:T(8,128)(2,1)S(1)} %get-tuple-element.41.refs_2_, ...), custom_call_target="tpu_custom_call" | custom-call | flops 805306368 | bytes 5242880 | tf_op jit(solution)/shard_map/spread/pallas_call | solution.py:282
  237.8 1.5 collective-permute-start.9
  239.4 1.5 collective-permute-start.10
  241.4 3.4 %spread.7.refs_5_ = f32[2,2,1,256,256]{4,3,2,1,0:T(8,128)S(1)} custom-call(s32[4]{0:T(128)S(1)} %pad_add_fusion.pos, bf16[256,1024]{1,0:T(8,128)(2,1)S(1)} %get-tuple-element.40.refs_0_, bf16[2048,1536]{1,0:T(8,128)(2,1)} %all-gather.3.cloned.1.call-done.weights.refs_1_.refs_3_, bf16[256,512]{1,0:T(8,128)(2,1)S(1)} %get-tuple-element.41.refs_2_, ...), custom_call_target="tpu_custom_call" | custom-call | flops 805306368 | bytes 5242880 | tf_op jit(solution)/shard_map/spread/pallas_call | solution.py:282
  244.8 6.6 %collective-permute-done.9 = bf16[2,2,1,256,256]{4,3,2,1,0:T(8,128)(2,1)S(1)} collective-permute-done((bf16[2,2,1,256,256]{4,3,2,1,0:T(8,128)(2,1)S(1)}, bf16[2,2,1,256,256]{4,3,2,1,0:T(8,128)(2,1)S(1)}, u32[]{:S(2)}, u32[]{:S(2)}) %collective-permute-start.9) | collective-permute-done | bytes 524320 | tf_op jit(solution)/shard_map/ppermute | solution.py:321
  251.6 0.9 copy.27
  252.4 3.6 %all-to-all-start.1 = ((bf16[16,64,256]{2,1,0:T(8,128)(2,1)}), bf16[16,64,256]{2,1,0:T(8,128)(2,1)S(1)}, u32[]{:S(2)}, u32[]{:S(2)}) async-start(bf16[16,64,256]{2,1,0:T(8,128)(2,1)} %bitcast.16), calls=%async_computation.1 | async-start | bytes 1048576 | tf_op jit(solution)/shard_map/all_to_all | solution.py:401
  256.0 2.2 collective-permute-done.11.refs_2_
  258.2 3.4 %spread.8.refs_5_ = bf16[2,2,1,256,256]{4,3,2,1,0:T(8,128)(2,1)S(1)} custom-call(s32[4]{0:T(128)S(1)} %pad_add_fusion.pos, bf16[256,1024]{1,0:T(8,128)(2,1)S(1)} %collective-permute-done.10.refs_0_, bf16[2048,1536]{1,0:T(8,128)(2,1)} %all-gather.3.cloned.1.call-done.weights.refs_1_.refs_3_, bf16[256,512]{1,0:T(8,128)(2,1)S(1)} %collective-permute-done.11.refs_2_, ...), custom_call_target="tpu_custom_call" | custom-call | flops 805306368 | bytes 5242880 | tf_op jit(solution)/shard_map/spread/pallas_call | solution.py:282
  261.6 0.6 collective-permute-start.12
  262.3 3.4 %spread.9 = f32[2,2,1,256,256]{4,3,2,1,0:T(8,128)S(1)} custom-call(s32[4]{0:T(128)S(1)} %pad_add_fusion.pos, bf16[256,1024]{1,0:T(8,128)(2,1)S(1)} %collective-permute-done.10.refs_0_, bf16[2048,1536]{1,0:T(8,128)(2,1)} %all-gather.3.cloned.1.call-done.weights.refs_1_.refs_3_, bf16[256,512]{1,0:T(8,128)(2,1)S(1)} %collective-permute-done.11.refs_2_, ...), custom_call_target="tpu_custom_call" | custom-call | flops 805306368 | bytes 5242880 | tf_op jit(solution)/shard_map/spread/pallas_call | solution.py:282
  265.7 8.4 %collective-permute-done.12 = bf16[2,2,1,256,256]{4,3,2,1,0:T(8,128)(2,1)S(1)} collective-permute-done((bf16[2,2,1,256,256]{4,3,2,1,0:T(8,128)(2,1)S(1)}, bf16[2,2,1,256,256]{4,3,2,1,0:T(8,128)(2,1)S(1)}, u32[]{:S(2)}, u32[]{:S(2)}) %collective-permute-start.12) | collective-permute-done | bytes 524320 | tf_op jit(solution)/shard_map/ppermute | solution.py:321
  274.2 0.9 copy.29
  275.0 5.4 %all-to-all-start.2 = ((bf16[16,64,256]{2,1,0:T(8,128)(2,1)}), bf16[16,64,256]{2,1,0:T(8,128)(2,1)S(1)}, u32[]{:S(2)}, u32[]{:S(2)}) async-start(bf16[16,64,256]{2,1,0:T(8,128)(2,1)} %bitcast.23), calls=%async_computation.2 | async-start | bytes 1048576 | tf_op jit(solution)/shard_map/all_to_all | solution.py:401
  281.0 13.9 %all-to-all-done.2 = bf16[16,64,256]{2,1,0:T(8,128)(2,1)S(1)} async-done(((bf16[16,64,256]{2,1,0:T(8,128)(2,1)}), bf16[16,64,256]{2,1,0:T(8,128)(2,1)S(1)}, u32[]{:S(2)}, u32[]{:S(2)}) %all-to-all-start.2) | async-done | bytes 524320 | tf_op jit(solution)/shard_map/all_to_all | solution.py:401
  295.5 1.0 copy.32
  (54 shorter events, 5.0 us)
Async XLA Ops:
  7.2 5.2 %copy-start = (bf16[128,2048]{1,0:T(8,128)(2,1)S(1)}, bf16[128,2048]{1,0:T(8,128)(2,1)}, u32[]{:S(2)}) copy-start(bf16[128,2048]{1,0:T(8,128)(2,1)} %param.10) | copy-start | bytes 1572868
  7.2 4.8 %copy-start.8 = (s32[128,1]{0,1:T(1,128)S(1)}, s32[128,1]{0,1:T(1,128)}, u32[]{:S(2)}) copy-start(s32[128,1]{0,1:T(1,128)} %param.11) | copy-start | bytes 1540
  7.2 131.9 %all-gather.5.cloned.1.call-start = ((), (), s32[]{:S(2)}) async-start(), calls=%async_computation.4 | async-start | bytes 11796480 | tf_op jit(solution)/shard_map/all_gather | solution.py:337
  11.9 191.9 %all-gather.3.cloned.1.call-start = ((), (), s32[]{:S(2)}) async-start(), calls=%async_computation.3 | async-start | bytes 7077888 | tf_op jit(solution)/shard_map/all_gather | solution.py:337
  15.4 3.4 %copy-start.7 = (bf16[16,144,256]{2,1,0:T(8,128)(2,1)S(1)}, bf16[16,144,256]{2,1,0:T(8,128)(2,1)}, u32[]{:S(2)}) copy-start(bf16[16,144,256]{2,1,0:T(8,128)(2,1)} %fusion.1.rest_1_) | copy-start | bytes 3538948
  88.1 25.2 %collective-permute-start = (bf16[2,2,2,256,256]{4,3,2,1,0:T(8,128)(2,1)S(1)}, bf16[2,2,2,256,256]{4,3,2,1,0:T(8,128)(2,1)S(1)}, u32[]{:S(2)}, u32[]{:S(2)}) collective-permute-start(bf16[2,2,2,256,256]{4,3,2,1,0:T(8,128)(2,1)S(1)} %bitcast.59), channel_id=1, source_target_pairs={{0,1},{1,0},{2,3},{3,2},{4,5},{5,4},{6,7},{7,6},{8,9},{9,8},{10,11... | collective-permute-start | bytes 3145736 | tf_op jit(solution)/shard_map/ppermute | solution.py:321
  144.5 15.1 %collective-permute-start.3 = (bf16[256,1024]{1,0:T(8,128)(2,1)}, bf16[256,1024]{1,0:T(8,128)(2,1)}, u32[]{:S(2)}, u32[]{:S(2)}) collective-permute-start(bf16[256,1024]{1,0:T(8,128)(2,1)} %get-tuple-element.27), channel_id=1, source_target_pairs={{0,4},{2,6},{4,0},{6,2},{8,12},{10,14},{12,8},{14,10},{16,20},{18,... | collective-permute-start | bytes 1572872 | tf_op jit(solution)/shard_map/ppermute | solution.py:365
  151.5 1.0 copy-start.5
  152.5 18.3 %collective-permute-start.2 = (bf16[256,1024]{1,0:T(8,128)(2,1)}, bf16[256,1024]{1,0:T(8,128)(2,1)}, u32[]{:S(2)}, u32[]{:S(2)}) collective-permute-start(bf16[256,1024]{1,0:T(8,128)(2,1)} %get-tuple-element.25), channel_id=1, source_target_pairs={{0,4},{2,6},{4,0},{6,2},{8,12},{10,14},{12,8},{14,10},{16,20},{18,... | collective-permute-start | bytes 1572872 | tf_op jit(solution)/shard_map/ppermute | solution.py:365
  157.7 21.3 %collective-permute-start.1 = (bf16[256,512]{1,0:T(8,128)(2,1)S(1)}, bf16[256,512]{1,0:T(8,128)(2,1)S(1)}, u32[]{:S(2)}, u32[]{:S(2)}) collective-permute-start(bf16[256,512]{1,0:T(8,128)(2,1)S(1)} %get-tuple-element.23), channel_id=1, source_target_pairs={{0,4},{2,6},{4,0},{6,2},{8,12},{10,14},{12,8},{14,10},{16,20},{18,... | collective-permute-start | bytes 786440 | tf_op jit(solution)/shard_map/ppermute | solution.py:365
  159.6 11.2 %copy-start.6 = (f32[256,1024]{1,0:T(8,128)S(1)}, f32[256,1024]{1,0:T(8,128)}, u32[]{:S(2)}) copy-start(f32[256,1024]{1,0:T(8,128)} %copy-done.5) | copy-start | bytes 3145732
  170.8 8.1 %copy-start.3 = (bf16[1024,2048]{1,0:T(8,128)(2,1)S(1)}, bf16[1024,2048]{1,0:T(8,128)(2,1)}, u32[]{:S(2)}) copy-start(bf16[1024,2048]{1,0:T(8,128)(2,1)} %queries.9) | copy-start | bytes 12582916
  176.9 36.6 %collective-permute-start.7 = (bf16[256,1024]{1,0:T(8,128)(2,1)S(1)}, bf16[256,1024]{1,0:T(8,128)(2,1)S(1)}, u32[]{:S(2)}, u32[]{:S(2)}) collective-permute-start(bf16[256,1024]{1,0:T(8,128)(2,1)S(1)} %get-tuple-element.37.refs_3_), channel_id=1, source_target_pairs={{0,4},{2,6},{4,0},{6,2},{8,12},{10,14},{12,8},{14,10},{16,20},{18,... | collective-permute-start | bytes 1572872 | tf_op jit(solution)/shard_map/ppermute | solution.py:379
  178.4 35.1 %collective-permute-start.6 = (bf16[256,1024]{1,0:T(8,128)(2,1)}, bf16[256,1024]{1,0:T(8,128)(2,1)}, u32[]{:S(2)}, u32[]{:S(2)}) collective-permute-start(bf16[256,1024]{1,0:T(8,128)(2,1)} %get-tuple-element.36.refs_0_), channel_id=1, source_target_pairs={{0,4},{2,6},{4,0},{6,2},{8,12},{10,14},{12,8},{14,10},{16,20},{18,... | collective-permute-start | bytes 1572872 | tf_op jit(solution)/shard_map/ppermute | solution.py:379
  182.7 30.8 %collective-permute-start.8 = (bf16[256,512]{1,0:T(8,128)(2,1)S(1)}, bf16[256,512]{1,0:T(8,128)(2,1)}, u32[]{:S(2)}, u32[]{:S(2)}) collective-permute-start(bf16[256,512]{1,0:T(8,128)(2,1)S(1)} %get-tuple-element.30.rest_0_.refs_6_), channel_id=1, source_target_pairs={{0,4},{2,6},{4,0},{6,2},{8,12},{10,14},{12,8},{14,10},{16,20},{18,... | collective-permute-start | bytes 786440 | tf_op jit(solution)/shard_map/ppermute | solution.py:379
  208.6 15.9 %collective-permute-start.5 = (bf16[256,1024]{1,0:T(8,128)(2,1)S(1)}, bf16[256,1024]{1,0:T(8,128)(2,1)S(1)}, u32[]{:S(2)}, u32[]{:S(2)}) collective-permute-start(bf16[256,1024]{1,0:T(8,128)(2,1)S(1)} %get-tuple-element.34), channel_id=1, source_target_pairs={{0,4},{2,6},{4,0},{6,2},{8,12},{10,14},{12,8},{14,10},{16,20},{18,... | collective-permute-start | bytes 1572872 | tf_op jit(solution)/shard_map/ppermute | solution.py:365
  212.8 17.9 %collective-permute-start.4 = (bf16[256,512]{1,0:T(8,128)(2,1)S(1)}, bf16[256,512]{1,0:T(8,128)(2,1)S(1)}, u32[]{:S(2)}, u32[]{:S(2)}) collective-permute-start(bf16[256,512]{1,0:T(8,128)(2,1)S(1)} %get-tuple-element.32), channel_id=1, source_target_pairs={{0,4},{2,6},{4,0},{6,2},{8,12},{10,14},{12,8},{14,10},{16,20},{18,... | collective-permute-start | bytes 786440 | tf_op jit(solution)/shard_map/ppermute | solution.py:365
  224.5 6.2 %copy-start.4 = (bf16[1024,2048]{1,0:T(8,128)(2,1)S(1)}, bf16[1024,2048]{1,0:T(8,128)(2,1)}, u32[]{:S(2)}) copy-start(bf16[1024,2048]{1,0:T(8,128)(2,1)} %queries.9) | copy-start | bytes 12582916
  230.7 3.9 %copy-start.2 = (f32[4,2,2,256,256]{4,3,2,1,0:T(8,128)S(1)}, f32[4,2,2,256,256]{4,3,2,1,0:T(8,128)}, u32[]{:S(2)}) copy-start(f32[4,2,2,256,256]{4,3,2,1,0:T(8,128)} %spread.5.rest_1_.refs_4_) | copy-start | bytes 12582916
  237.8 13.6 %collective-permute-start.9 = (bf16[2,2,1,256,256]{4,3,2,1,0:T(8,128)(2,1)S(1)}, bf16[2,2,1,256,256]{4,3,2,1,0:T(8,128)(2,1)S(1)}, u32[]{:S(2)}, u32[]{:S(2)}) collective-permute-start(bf16[2,2,1,256,256]{4,3,2,1,0:T(8,128)(2,1)S(1)} %spread.6.refs_5_), channel_id=1, source_target_pairs={{0,1},{1,0},{2,3},{3,2},{4,5},{5,4},{6,7},{7,6},{8,9},{9,8},{10,11... | collective-permute-start | bytes 1572872 | tf_op jit(solution)/shard_map/ppermute | solution.py:321
  239.4 18.9 %collective-permute-start.10 = (bf16[256,1024]{1,0:T(8,128)(2,1)S(1)}, bf16[256,1024]{1,0:T(8,128)(2,1)S(1)}, u32[]{:S(2)}, u32[]{:S(2)}) collective-permute-start(bf16[256,1024]{1,0:T(8,128)(2,1)S(1)} %get-tuple-element.40.refs_0_), channel_id=1, source_target_pairs={{0,4},{2,6},{4,0},{6,2},{8,12},{10,14},{12,8},{14,10},{16,20},{18,... | collective-permute-start | bytes 1572872 | tf_op jit(solution)/shard_map/ppermute | solution.py:379
  240.9 17.4 %collective-permute-start.11 = (bf16[256,512]{1,0:T(8,128)(2,1)S(1)}, bf16[256,512]{1,0:T(8,128)(2,1)S(1)}, u32[]{:S(2)}, u32[]{:S(2)}) collective-permute-start(bf16[256,512]{1,0:T(8,128)(2,1)S(1)} %get-tuple-element.41.refs_2_), channel_id=1, source_target_pairs={{0,4},{2,6},{4,0},{6,2},{8,12},{10,14},{12,8},{14,10},{16,20},{18,... | collective-permute-start | bytes 786440 | tf_op jit(solution)/shard_map/ppermute | solution.py:379
  252.4 22.6 %all-to-all-start.1 = ((bf16[16,64,256]{2,1,0:T(8,128)(2,1)}), bf16[16,64,256]{2,1,0:T(8,128)(2,1)S(1)}, u32[]{:S(2)}, u32[]{:S(2)}) async-start(bf16[16,64,256]{2,1,0:T(8,128)(2,1)} %bitcast.16), calls=%async_computation.1 | async-start | bytes 1048576 | tf_op jit(solution)/shard_map/all_to_all | solution.py:401
  261.6 12.4 %collective-permute-start.12 = (bf16[2,2,1,256,256]{4,3,2,1,0:T(8,128)(2,1)S(1)}, bf16[2,2,1,256,256]{4,3,2,1,0:T(8,128)(2,1)S(1)}, u32[]{:S(2)}, u32[]{:S(2)}) collective-permute-start(bf16[2,2,1,256,256]{4,3,2,1,0:T(8,128)(2,1)S(1)} %spread.8.refs_5_), channel_id=1, source_target_pairs={{0,1},{1,0},{2,3},{3,2},{4,5},{5,4},{6,7},{7,6},{8,9},{9,8},{10,11... | collective-permute-start | bytes 1572872 | tf_op jit(solution)/shard_map/ppermute | solution.py:321
  275.0 19.9 %all-to-all-start.2 = ((bf16[16,64,256]{2,1,0:T(8,128)(2,1)}), bf16[16,64,256]{2,1,0:T(8,128)(2,1)S(1)}, u32[]{:S(2)}, u32[]{:S(2)}) async-start(bf16[16,64,256]{2,1,0:T(8,128)(2,1)} %bitcast.23), calls=%async_computation.2 | async-start | bytes 1048576 | tf_op jit(solution)/shard_map/all_to_all | solution.py:401
  295.0 1.5 copy-start.1
Sparse Core Ops, SparseCore 0:
  12.0 127.0 all-gather.4
  140.8 63.0 all-gather.2

commit v3 on v2

--- a/solution.py
+++ b/solution.py
@@ -38,6 +38,22 @@
 ANYWHERE = pl.BlockSpec(memory_space=pl.ANY)
 
 
+def tie_kernel(*refs):
+    pass
+
+
+def tie(value, token):
+    return pl.pallas_call(
+        tie_kernel,
+        in_specs=[ANYWHERE, ANYWHERE],
+        out_specs=ANYWHERE,
+        out_shape=jax.ShapeDtypeStruct(value.shape, value.dtype),
+        input_output_aliases={0: 0},
+        cost_estimate=pl.CostEstimate(flops=0, bytes_accessed=0, transcendentals=0),
+        name="tie",
+    )(value, token)
+
+
 def predict_kernel(weights, velocity, *rest):
     result = rest[-1]
     for side in range(2):
@@ -46,8 +62,64 @@
         ).astype(jnp.bfloat16)
 
 
+def predict_first_kernel(weights, velocity, result, held_weights, held_velocity, held, sems):
+    depth = weights.shape[1]
+    size = held.shape[0]
+    loads, stores = [], []
+    for head in range(size):
+        at = pl.ds(head * HD, HD)
+        loads.append(
+            (
+                pltpu.make_async_copy(weights.at[:, :, at], held_weights.at[head], sems.at[0, head]),
+                pltpu.make_async_copy(
+                    velocity.at[:, :, at], held_velocity.at[head], sems.at[1, head]
+                ),
+            )
+        )
+        stores.append(
+            pltpu.make_async_copy(
+                held.at[head], result.at[:, pl.ds(2 * head * HD, 2 * HD)], sems.at[2, head]
+            )
+        )
+        for load in loads[-1]:
+            load.start()
+    for head in range(size):
+        for load in loads[head]:
+            load.wait()
+        for side in range(2):
+            held[head, :, side * HD : (side + 1) * HD] = (
+                held_weights[head, side].astype(jnp.float32) - held_velocity[head, side]
+            ).astype(jnp.bfloat16)
+        stores[head].start()
+    for store in stores:
+        store.wait()
+
+
+def predict_first(projections, velocity, size):
+    depth = projections.shape[1]
+    return pl.pallas_call(
+        predict_first_kernel,
+        in_specs=[ANYWHERE, ANYWHERE],
+        out_specs=ANYWHERE,
+        out_shape=jax.ShapeDtypeStruct((depth, 2 * HD * size), jnp.bfloat16),
+        scratch_shapes=[
+            pltpu.VMEM((size, 2, depth, HD), jnp.bfloat16),
+            pltpu.VMEM((size, 2, depth, HD), jnp.float32),
+            pltpu.VMEM((size, depth, 2 * HD), jnp.bfloat16),
+            pltpu.SemaphoreType.DMA((3, size)),
+        ],
+        compiler_params=pltpu.CompilerParams(vmem_limit_bytes=VMEM_LIMIT),
+        cost_estimate=pl.CostEstimate(
+            flops=2 * depth * HD * size, bytes_accessed=16 * depth * HD * size, transcendentals=0
+        ),
+        name="predict_first",
+    )(projections, velocity)
+
+
 def predict(projections, velocity, first, size, *tokens):
     depth = projections.shape[1]
+    if first == 0:
+        return predict_first(projections, velocity, size)
     spec = pl.BlockSpec((2, depth, HD), lambda head: (0, 0, first + head))
     return pl.pallas_call(
         predict_kernel,
@@ -62,7 +134,7 @@
     )(projections, velocity, *tokens)
 
 
-def arrange_kernel(pos, rows, result, *, line, tensor_count):
+def arrange_kernel(pos, rows, _, result, *, line, tensor_count):
     per_tensor = line // tensor_count
     slots, depth = rows.shape[3:]
     for x_at in range(2):
@@ -75,13 +147,14 @@
                 ]
 
 
-def arrange(pos, rows, line, tensor_count):
+def arrange(pos, rows, token, line, tensor_count):
     slots, depth = rows.shape[3:]
     return pl.pallas_call(
         functools.partial(arrange_kernel, line=line, tensor_count=tensor_count),
         in_specs=[
             pl.BlockSpec(memory_space=pltpu.SMEM),
             pl.BlockSpec(memory_space=pltpu.VMEM),
+            ANYWHERE,
         ],
         out_specs=pl.BlockSpec(memory_space=pltpu.VMEM),
         out_shape=jax.ShapeDtypeStruct((2 * slots, 2 * line * depth), jnp.bfloat16),
@@ -90,7 +163,7 @@
             flops=0, bytes_accessed=4 * rows.size, transcendentals=0
         ),
         name="arrange",
-    )(pos, rows)
+    )(pos, rows, token)
 
 
 def project_kernel(rows, weights, *rest):
@@ -172,7 +245,7 @@
     query_count, width = queries.shape
     slots, chunk = mine.shape
     heads = chunk // (2 * HD)
-    block = min(256, query_count)
+    block = min(1024, query_count)
     columns = pl.BlockSpec((query_count, HD), lambda head: (0, first_head + head))
     pair = pl.BlockSpec((slots, 2 * HD), lambda head: (0, head))
     operands = [live, usable, queries, grads, mine, received]
@@ -322,35 +395,29 @@
 
     placement = slot_table(row_owner[:, 0], capacity, peers)
     filled = jnp.sum(placement.astype(jnp.float32), axis=1).astype(jnp.bfloat16)
-    flags = filled.reshape(line, 1, 2, 2, capacity).transpose(0, 1, 3, 4, 2)
-    flags = jnp.broadcast_to(flags, (line, 2, 2, capacity, 2)).reshape(peers, capacity, 2)
-    flags = jnp.pad(flags, ((0, 0), (0, 0), (0, depth - 2)))
     outgoing = jnp.dot(placement, encoded, preferred_element_type=jnp.float32).astype(jnp.bfloat16)
     outgoing = outgoing.reshape(line, 2, 2, capacity, per_tensor, 2, 2, depth)
     outgoing = outgoing.transpose(0, 5, 2, 4, 6, 1, 3, 7).reshape(peers, -1, depth)
-    outgoing = jnp.concatenate([outgoing, flags], axis=1)
-
+
+    incoming = lax.all_to_all(outgoing, "dp", split_axis=0, concat_axis=0, tiled=True)
     parts = []
     first, token = 0, ()
     for size in split_heads(queries.shape[1] // HD):
         block = predict(projections, velocity, first, size, *token)
         gathered = lax.all_gather(block, "dp", axis=0, tiled=True, axis_index_groups=columns)
         parts.append((first, size, gathered))
-        first, token = first + size, (block, outgoing)
-
-    incoming = lax.all_to_all(outgoing, "dp", split_axis=0, concat_axis=0, tiled=True)
-    usable = jnp.where(
-        pos[1] == 0, incoming[:, -capacity:, 0], incoming[:, -capacity:, 1]
-    ).reshape(slots, 1)
-    usable = (usable.astype(jnp.float32) > 0.5).astype(jnp.float32)
-    incoming = incoming[:, :-capacity].reshape(peers, per_tensor, 2, 2, capacity, depth)
+        first, token = first + size, (block, incoming)
+
+    usable = lax.all_to_all(filled, "dp", split_axis=0, concat_axis=0, tiled=True)
+    usable = (usable.astype(jnp.float32) > 0.5).astype(jnp.float32)[:, None]
+    incoming = incoming.reshape(peers, per_tensor, 2, 2, capacity, depth)
     incoming = incoming.transpose(1, 2, 3, 0, 4, 5).reshape(per_tensor, 2, 2, slots, depth)
     rows = jnp.concatenate(
         [incoming] + [tensor_shift(incoming, shift) for shift in range(1, tensor_count)]
     )
-    rows = arrange(pos, rows, line, tensor_count)
-
-    query_grad, token, units, early = None, (), [], None
+    rows = arrange(pos, rows, usable, line, tensor_count)
+
+    query_grad, token, units, early, exchanged = None, (), [], None, []
     for at, (first, size, weights) in enumerate(parts):
         final = at == len(parts) - 1
         if final:
@@ -375,23 +442,34 @@
                 first + column // (2 * HD),
                 query_grad,
                 *((early,) if final else ()),
-            )
-            units.append((pair_grad, lax.ppermute(pair_grad, "dp", x_swap), weights, column))
+                *exchanged[-2:-1],
+            )
+            exchanged.append(lax.ppermute(pair_grad, "dp", x_swap))
+            units.append((pair_grad, exchanged[-1], weights, column))
             token = (pair_grad,)
 
-    def finish(side, *tokens):
-        sent = spread(
-            pos, depth, units, early, (side,), per_tensor, line - per_tensor, tensor_count,
-            jnp.bfloat16, *tokens,
+    sent, passed, kept = [], [], []
+    for side in range(2):
+        sent.append(
+            spread(
+                pos, depth, units, early, (side,), per_tensor, line - per_tensor, tensor_count,
+                jnp.bfloat16, *sent,
+            )
         )
-        passed = [
-            tensor_shift(sent[(shift - 1) * per_tensor : shift * per_tensor], shift)
-            for shift in range(1, tensor_count)
-        ]
-        kept = spread(
-            pos, depth, units, early, (side,), 0, per_tensor, tensor_count, jnp.float32, sent
+        passed.append(
+            [
+                tensor_shift(sent[side][(shift - 1) * per_tensor : shift * per_tensor], shift)
+                for shift in range(1, tensor_count)
+            ]
         )
-        return kept, passed
+    for side in range(2):
+        kept.append(
+            spread(
+                pos, depth, units, early, (side,), 0, per_tensor, tensor_count, jnp.float32,
+                sent[side], *kept,
+            )
+        )
+    passed[0] = [tie(part, sent[1]) for part in passed[0]]
 
     def send_home(kept, passed):
         for part in passed:
@@ -401,15 +479,13 @@
         returned = lax.all_to_all(kept, "dp", split_axis=0, concat_axis=0, tiled=True)
         return returned.reshape(line, 2, 2, per_tensor, 2, capacity, depth)
 
-    own_side = finish(0)
-    other_side = finish(1, own_side[0])
     homes = placement.reshape(line, 2, 2, capacity, stored_rows)
     encoded_grad = jnp.einsum(
-        "zxckr,zxcpqkd->rpxqd", homes, send_home(*own_side), preferred_element_type=jnp.float32
+        "zxckr,zxcpqkd->rpxqd", homes, send_home(kept[0], passed[0]), preferred_element_type=jnp.float32
     ) + jnp.einsum(
         "zxckr,zxcpqkd->rpxqd",
         homes[:, ::-1],
-        send_home(*other_side),
+        send_home(kept[1], passed[1]),
         preferred_element_type=jnp.float32,
     )
     return (query_grad, encoded_grad.astype(jnp.bfloat16).reshape(stored_rows, -1))

time: 304 us -> 298 us (0.980)
  blocking collectives: 67.9 us -> 50.3 us
  starting transfers between devices: 24 us -> 40.1 us
  Pallas kernels: 80.4 us -> 72.4 us
  waiting for transfers between devices: 105 us -> 109 us
    ppermute x3, waiting for transfers between devices: 38.6 us -> 9.25 us  [tensor_shift(): return lax.ppermute(value, 'tensor', pairs)]
    all_to_all x1, blocking collectives: 67.9 us -> 50.3 us  [on_device(): lax.all_to_all(outgoing, 'dp', split_axis=0, concat_axis=0, tiled=True)]
    all_to_all x0 -> x1, starting transfers between devices: none -> 14.9 us  [on_device(): lax.all_to_all(filled, 'dp', split_axis=0, concat_axis=0, tiled=True)]
    ppermute x5, waiting for transfers between devices: 5.74 us -> 19 us  [on_device(): products.append((column, mine, lax.ppermute(other, 'dp', x_swap)))]
    all_gather x2, waiting for transfers between devices: 44.4 us -> 54.5 us  [on_device(): lax.all_gather(block, 'dp', axis=0, tiled=True, axis_index_groups=columns)]
    all_to_all x0 -> x1, waiting for transfers between devices: none -> 6.34 us  [on_device(): lax.all_to_all(filled, 'dp', split_axis=0, concat_axis=0, tiled=True)]
    pallas_call x2 -> x1, Pallas kernels: 8.04 us -> 3.4 us  [predict(): pl.pallas_call(predict_kernel, grid=(size,), in_specs=[spec, spec] + [ANY...]
    pallas_call x5, Pallas kernels: 26 us -> 21.4 us  [attend(): pl.pallas_call(functools.partial(attend_kernel, block), grid=(heads,), in...]
  transfers between devices with their start and end apart: 17 -> 18, of which waited for: 9 -> 9; matrix products, arithmetic and copies ran while one was open for 3% -> 1% of each run, Pallas kernels for 23% -> 23%
where the time goes in v3:
time: 298 us; the launch traced here: 297 us
  waiting for transfers between devices  109 us (37%)
  Pallas kernels  72.4 us (24%)
  blocking collectives  50.3 us (17%)
  starting transfers between devices  40.1 us (13%)
  between operations  15.1 us (5%)
  local copies, waits for them, and re-layouts  7.21 us (2%)
    all_gather x2, waiting for transfers between devices, on_device(): lax.all_gather(block, 'dp', axis=0, tiled=True, axis_index_groups=columns)  54.5 us
    all_to_all x1, blocking collectives, on_device(): lax.all_to_all(outgoing, 'dp', split_axis=0, concat_axis=0, tiled=True)  50.3 us
    pallas_call x5, Pallas kernels, spread(): pl.pallas_call(functools.partial(spread_kernel, parts=len(units), sides=s...  24.1 us
    pallas_call x5, Pallas kernels, attend(): pl.pallas_call(functools.partial(attend_kernel, block), grid=(heads,), in...  21.4 us
    pallas_call x5, Pallas kernels, project(): pl.pallas_call(project_kernel, grid=(width // HD,), in_specs=[pl.BlockSpe...  20.1 us
    ppermute x5, waiting for transfers between devices, on_device(): products.append((column, mine, lax.ppermute(other, 'dp', x_swap)))  19 us
    all_to_all x1, starting transfers between devices, on_device(): lax.all_to_all(filled, 'dp', split_axis=0, concat_axis=0, tiled=True)  14.9 us
    all_to_all x2, waiting for transfers between devices, send_home(): lax.all_to_all(kept, 'dp', split_axis=0, concat_axis=0, tiled=True)  13.9 us
  transfers between devices with their start and end apart: 18, of which 9 were waited for; matrix products, arithmetic and copies ran while one was open for 1% of the time, Pallas kernels for 23%

profile of v3, /device:TPU:0, one launch (start us, length us, event | category | flops | bytes accessed | tf_op | source)
XLA Modules:
  0.0 297.3 jit_solution(10100613495398965198)
XLA Ops:
  7.2 1.6 copy-done.6
  8.9 2.6 predict_first.1.rest_0_
  12.5 0.8 reshape.99
  13.6 50.3 %all_to_all.25.rest_1_ = bf16[16,128,256]{2,1,0:T(8,128)(2,1)} all-to-all(bf16[16,128,256]{2,1,0:T(8,128)(2,1)S(1)} %bitcast.48), channel_id=1, replica_groups=mesh['dp'=16,'tensor'=2] {'dp'}, dimensions={0} | all-to-all | bytes 2097152 | tf_op jit(solution)/shard_map/all_to_all | solution.py:402
  63.9 3.4 %predict.1 = bf16[256,1536]{1,0:T(8,128)(2,1)} custom-call(bf16[2,256,2048]{2,1,0:T(8,128)(2,1)} %weights.3, f32[2,256,2048]{2,1,0:T(8,128)} %velocity.3, bf16[256,2560]{1,0:T(8,128)(2,1)} %predict_first.1.rest_0_, bf16[16,128,256]{2,1,0:T(8,128)(2,1)} %all_to_all.25.rest_1_), custom_call_target="tpu_custom_call" | custom-call | flops 393216 | bytes 3145728 | tf_op jit(solution)/shard_map/predict/pallas_call | solution.py:124
  67.4 1.6 collective-permute-start
  69.1 0.7 all_to_all.20
  69.8 14.9 %all-to-all-start = ((bf16[16,16,1]{1,2,0:T(2,128)(2,1)}), bf16[16,16,1]{1,2,0:T(2,128)(2,1)S(1)}, u32[]{:S(2)}, u32[]{:S(2)}) async-start(bf16[16,16,1]{1,2,0:T(2,128)(2,1)} %all_to_all.20), calls=%async_computation | async-start | bytes 16384 | tf_op jit(solution)/shard_map/all_to_all | solution.py:411
  84.8 6.3 %all-to-all-done = bf16[16,16,1]{1,2,0:T(2,128)(2,1)S(1)} async-done(((bf16[16,16,1]{1,2,0:T(2,128)(2,1)}), bf16[16,16,1]{1,2,0:T(2,128)(2,1)S(1)}, u32[]{:S(2)}, u32[]{:S(2)}) %all-to-all-start) | async-done | bytes 544 | tf_op jit(solution)/shard_map/all_to_all | solution.py:411
  91.5 0.8 arrange.1.rows
  92.3 41.3 %all-gather.5.cloned.1.call-done.weights.refs_2_.refs_5_.refs_8_ = bf16[2048,2560]{1,0:T(8,128)(2,1)} async-done(((bf16[256,2560]{1,0:T(8,128)(2,1)}), bf16[2048,2560]{1,0:T(8,128)(2,1)}) %all-gather.5.cloned.1.call-update) | async-done | bytes 10485776 | tf_op jit(solution)/shard_map/all_gather | solution.py:407
  133.5 4.7 %project.7 = (f32[256,1024]{1,0:T(8,128)S(1)}, bf16[256,1024]{1,0:T(8,128)(2,1)S(1)}) custom-call(bf16[512,2048]{1,0:T(8,128)(2,1)S(1)} %arrange.1.rows, bf16[2048,2560]{1,0:T(8,128)(2,1)} %all-gather.5.cloned.1.call-done.weights.refs_2_.refs_5_.refs_8_), custom_call_target="tpu_custom_call" | custom-call | flops 2147483648 | bytes 7864320 | tf_op jit(solution)/shard_map/project/pallas_call | solution.py:182
  138.3 1.5 collective-permute-start.3
  139.8 5.1 %project.6 = (f32[256,1024]{1,0:T(8,128)S(1)}, bf16[256,1024]{1,0:T(8,128)(2,1)S(1)}) custom-call(bf16[512,2048]{1,0:T(8,128)(2,1)S(1)} %arrange.1.rows, bf16[2048,2560]{1,0:T(8,128)(2,1)} %all-gather.5.cloned.1.call-done.weights.refs_2_.refs_5_.refs_8_), custom_call_target="tpu_custom_call" | custom-call | flops 2147483648 | bytes 7864320 | tf_op jit(solution)/shard_map/project/pallas_call | solution.py:182
  146.0 7.1 %collective-permute-done.3.received = bf16[256,1024]{1,0:T(8,128)(2,1)S(1)} collective-permute-done((bf16[256,1024]{1,0:T(8,128)(2,1)S(1)}, bf16[256,1024]{1,0:T(8,128)(2,1)S(1)}, u32[]{:S(2)}, u32[]{:S(2)}) %collective-permute-start.3) | collective-permute-done | bytes 524320 | tf_op jit(solution)/shard_map/ppermute | solution.py:432
  153.1 4.8 %attend.5 = (bf16[1024,2048]{1,0:T(8,128)(2,1)}, bf16[256,1024]{1,0:T(8,128)(2,1)S(1)}) custom-call(s32[1]{0:T(128)S(6)} %copy.97.live, f32[256,1]{1,0:T(8,128)S(1)} %reshape.115._.usable, bf16[1024,2048]{1,0:T(8,128)(2,1)} %queries.9, bf16[1024,2048]{1,0:T(8,128)(2,1)} %grads.9, f32[256,1024]{1,0:T(8,128)S(1)} %get-tuple-element.26.mine, ...), custom_call_target="tpu_custom_call" | custom-call | flops 1342177280 | bytes 5767168 | tf_op jit(solution)/shard_map/attend/pallas_call | solution.py:267
  157.9 1.5 collective-permute-start.4
  159.4 2.7 project.5
  162.7 1.6 collective-permute-done.2.received
  164.3 5.1 %attend.6 = (bf16[1024,2048]{1,0:T(8,128)(2,1)}, bf16[256,1024]{1,0:T(8,128)(2,1)}) custom-call(s32[1]{0:T(128)S(6)} %copy.97.live, f32[256,1]{1,0:T(8,128)S(1)} %reshape.115._.usable, bf16[1024,2048]{1,0:T(8,128)(2,1)} %queries.9, bf16[1024,2048]{1,0:T(8,128)(2,1)} %grads.9, ...), custom_call_target="tpu_custom_call", output_to_operand_aliasing={{0}: (6, {})} | custom-call | flops 1342177280 | bytes 5767168 | tf_op jit(solution)/shard_map/attend/pallas_call | solution.py:267
  169.4 1.5 collective-permute-start.7
  170.9 10.3 %collective-permute-done.1.received = bf16[256,512]{1,0:T(8,128)(2,1)S(1)} collective-permute-done((bf16[256,512]{1,0:T(8,128)(2,1)S(1)}, bf16[256,512]{1,0:T(8,128)(2,1)S(1)}, u32[]{:S(2)}, u32[]{:S(2)}) %collective-permute-start.1) | collective-permute-done | bytes 262176 | tf_op jit(solution)/shard_map/ppermute | solution.py:432
  181.2 3.2 %attend.7 = (bf16[1024,2048]{1,0:T(8,128)(2,1)}, bf16[256,512]{1,0:T(8,128)(2,1)S(1)}) custom-call(s32[1]{0:T(128)S(6)} %copy.97.live, f32[256,1]{1,0:T(8,128)S(1)} %reshape.115._.usable, bf16[1024,2048]{1,0:T(8,128)(2,1)S(1)} %copy-done.4, bf16[1024,2048]{1,0:T(8,128)(2,1)} %grads.9, ...), custom_call_target="tpu_custom_call", output_to_operand_aliasing={{0}: (6, {})} | custom-call | flops 671088640 | bytes 2883584 | tf_op jit(solution)/shard_map/attend/pallas_call | solution.py:267
  184.4 1.5 collective-permute-start.8
  185.8 13.3 %all-gather.3.cloned.1.call-done.weights.refs_1_.refs_3_ = bf16[2048,1536]{1,0:T(8,128)(2,1)} async-done(((bf16[256,1536]{1,0:T(8,128)(2,1)}), bf16[2048,1536]{1,0:T(8,128)(2,1)}) %all-gather.3.cloned.1.call-update) | async-done | bytes 6291472 | tf_op jit(solution)/shard_map/all_gather | solution.py:407
  199.1 4.7 %project.9 = (f32[256,1024]{1,0:T(8,128)S(1)}, bf16[256,1024]{1,0:T(8,128)(2,1)S(1)}) custom-call(bf16[512,2048]{1,0:T(8,128)(2,1)S(1)} %arrange.1.rows, bf16[2048,1536]{1,0:T(8,128)(2,1)} %all-gather.3.cloned.1.call-done.weights.refs_1_.refs_3_, bf16[256,512]{1,0:T(8,128)(2,1)S(1)} %get-tuple-element.31.rest_0_.refs_6_), custom_call_target="tpu_custom_call" | custom-call | flops 2147483648 | bytes 7864320 | tf_op jit(solution)/shard_map/project/pallas_call | solution.py:182
  203.9 1.5 collective-permute-start.6
  205.4 2.7 project.8
  208.7 10.9 %spread.5.rest_1_.refs_4_ = f32[4,2,2,256,256]{4,3,2,1,0:T(8,128)} custom-call(s32[4]{0:T(128)S(1)} %pad_add_fusion.pos, bf16[256,1024]{1,0:T(8,128)(2,1)S(1)} %copy-done.10, bf16[256,1024]{1,0:T(8,128)(2,1)S(1)} %collective-permute-done.4.rest_1_.refs_1_, bf16[2048,2560]{1,0:T(8,128)(2,1)} %all-gather.5.cloned.1.call-done.weights.refs_2_.refs_5_.refs_8_, ...), custom_call_target="tpu_custom_call" | custom-call | flops 5368709120 | bytes 18874368 | tf_op jit(solution)/shard_map/spread/pallas_call | solution.py:355
  219.6 5.0 %attend.8 = (bf16[1024,2048]{1,0:T(8,128)(2,1)}, bf16[256,1024]{1,0:T(8,128)(2,1)S(1)}) custom-call(s32[1]{0:T(128)S(6)} %copy.97.live, f32[256,1]{1,0:T(8,128)S(1)} %reshape.115._.usable, bf16[1024,2048]{1,0:T(8,128)(2,1)} %queries.9, bf16[1024,2048]{1,0:T(8,128)(2,1)} %grads.9, ...), custom_call_target="tpu_custom_call", output_to_operand_aliasing={{0}: (6, {})} | custom-call | flops 1342177280 | bytes 5767168 | tf_op jit(solution)/shard_map/attend/pallas_call | solution.py:267
  224.6 1.5 collective-permute-start.10
  226.1 3.3 %attend.9 = (bf16[1024,2048]{1,0:T(8,128)(2,1)}, bf16[256,512]{1,0:T(8,128)(2,1)S(1)}) custom-call(s32[1]{0:T(128)S(6)} %copy.97.live, f32[256,1]{1,0:T(8,128)S(1)} %reshape.115._.usable, bf16[1024,2048]{1,0:T(8,128)(2,1)S(1)} %copy-done.5, bf16[1024,2048]{1,0:T(8,128)(2,1)} %grads.9, ...), custom_call_target="tpu_custom_call", output_to_operand_aliasing={{0}: (6, {})} | custom-call | flops 671088640 | bytes 2883584 | tf_op jit(solution)/shard_map/attend/pallas_call | solution.py:267
  229.4 3.2 %spread.6.refs_5_ = bf16[2,2,1,256,256]{4,3,2,1,0:T(8,128)(2,1)S(1)} custom-call(s32[4]{0:T(128)S(1)} %pad_add_fusion.pos, bf16[256,1024]{1,0:T(8,128)(2,1)S(1)} %get-tuple-element.40.refs_0_, bf16[2048,1536]{1,0:T(8,128)(2,1)} %all-gather.3.cloned.1.call-done.weights.refs_1_.refs_3_, bf16[256,512]{1,0:T(8,128)(2,1)S(1)} %get-tuple-element.41.refs_2_, ...), custom_call_target="tpu_custom_call" | custom-call | flops 805306368 | bytes 5242880 | tf_op jit(solution)/shard_map/spread/pallas_call | solution.py:355
  232.6 1.6 collective-permute-start.9
  234.7 3.4 %spread.7.refs_6_ = f32[2,2,1,256,256]{4,3,2,1,0:T(8,128)S(1)} custom-call(s32[4]{0:T(128)S(1)} %pad_add_fusion.pos, bf16[256,1024]{1,0:T(8,128)(2,1)S(1)} %get-tuple-element.40.refs_0_, bf16[2048,1536]{1,0:T(8,128)(2,1)} %all-gather.3.cloned.1.call-done.weights.refs_1_.refs_3_, bf16[256,512]{1,0:T(8,128)(2,1)S(1)} %get-tuple-element.41.refs_2_, ...), custom_call_target="tpu_custom_call" | custom-call | flops 805306368 | bytes 5242880 | tf_op jit(solution)/shard_map/spread/pallas_call | solution.py:355
  238.1 5.6 %collective-permute-done.11.refs_2_ = bf16[256,512]{1,0:T(8,128)(2,1)S(1)} collective-permute-done((bf16[256,512]{1,0:T(8,128)(2,1)S(1)}, bf16[256,512]{1,0:T(8,128)(2,1)S(1)}, u32[]{:S(2)}, u32[]{:S(2)}) %collective-permute-start.11) | collective-permute-done | bytes 262176 | tf_op jit(solution)/shard_map/ppermute | solution.py:447
  243.7 3.2 %spread.8.refs_1_.refs_5_ = bf16[2,2,1,256,256]{4,3,2,1,0:T(8,128)(2,1)S(1)} custom-call(s32[4]{0:T(128)S(1)} %pad_add_fusion.pos, bf16[256,1024]{1,0:T(8,128)(2,1)S(1)} %collective-permute-done.10.refs_0_, bf16[2048,1536]{1,0:T(8,128)(2,1)} %all-gather.3.cloned.1.call-done.weights.refs_1_.refs_3_, bf16[256,512]{1,0:T(8,128)(2,1)S(1)} %collective-permute-done.11.refs_2_, ...), custom_call_target="tpu_custom_call" | custom-call | flops 805306368 | bytes 5242880 | tf_op jit(solution)/shard_map/spread/pallas_call | solution.py:355
  247.0 0.8 copy-done.7
  247.8 1.2 add_convert_fusion.1
  249.0 0.9 copy.68
  249.9 3.6 %all-to-all-start.2 = ((bf16[16,64,256]{2,1,0:T(8,128)(2,1)}), bf16[16,64,256]{2,1,0:T(8,128)(2,1)S(1)}, u32[]{:S(2)}, u32[]{:S(2)}) async-start(bf16[16,64,256]{2,1,0:T(8,128)(2,1)} %bitcast.12), calls=%async_computation.2 | async-start | bytes 1048576 | tf_op jit(solution)/shard_map/all_to_all | solution.py:479
  253.5 1.5 collective-permute-start.12
  255.0 3.4 %spread.9 = f32[2,2,1,256,256]{4,3,2,1,0:T(8,128)S(1)} custom-call(s32[4]{0:T(128)S(1)} %pad_add_fusion.pos, bf16[256,1024]{1,0:T(8,128)(2,1)S(1)} %collective-permute-done.10.refs_0_, bf16[2048,1536]{1,0:T(8,128)(2,1)} %all-gather.3.cloned.1.call-done.weights.refs_1_.refs_3_, bf16[256,512]{1,0:T(8,128)(2,1)S(1)} %collective-permute-done.11.refs_2_, ...), custom_call_target="tpu_custom_call" | custom-call | flops 805306368 | bytes 5242880 | tf_op jit(solution)/shard_map/spread/pallas_call | solution.py:355
  258.4 9.2 %collective-permute-done.12 = bf16[2,2,1,256,256]{4,3,2,1,0:T(8,128)(2,1)S(1)} collective-permute-done((bf16[2,2,1,256,256]{4,3,2,1,0:T(8,128)(2,1)S(1)}, bf16[2,2,1,256,256]{4,3,2,1,0:T(8,128)(2,1)S(1)}, u32[]{:S(2)}, u32[]{:S(2)}) %collective-permute-start.12) | collective-permute-done | bytes 524320 | tf_op jit(solution)/shard_map/ppermute | solution.py:394
  267.8 0.9 copy.70
  268.7 5.8 %all-to-all-start.3 = ((bf16[16,64,256]{2,1,0:T(8,128)(2,1)}), bf16[16,64,256]{2,1,0:T(8,128)(2,1)S(1)}, u32[]{:S(2)}, u32[]{:S(2)}) async-start(bf16[16,64,256]{2,1,0:T(8,128)(2,1)} %bitcast.19), calls=%async_computation.3 | async-start | bytes 1048576 | tf_op jit(solution)/shard_map/all_to_all | solution.py:479
  275.1 13.9 %all-to-all-done.3 = bf16[16,64,256]{2,1,0:T(8,128)(2,1)S(1)} async-done(((bf16[16,64,256]{2,1,0:T(8,128)(2,1)}), bf16[16,64,256]{2,1,0:T(8,128)(2,1)S(1)}, u32[]{:S(2)}, u32[]{:S(2)}) %all-to-all-start.3) | async-done | bytes 524320 | tf_op jit(solution)/shard_map/all_to_all | solution.py:479
  289.5 1.0 copy.73
  (62 shorter events, 5.2 us)
Async XLA Ops:
  7.2 4.9 %copy-start = (bf16[128,2048]{1,0:T(8,128)(2,1)S(1)}, bf16[128,2048]{1,0:T(8,128)(2,1)}, u32[]{:S(2)}) copy-start(bf16[128,2048]{1,0:T(8,128)(2,1)} %param.10) | copy-start | bytes 1572868
  7.2 126.4 %all-gather.5.cloned.1.call-start = ((), (), s32[]{:S(2)}) async-start(), calls=%async_computation.5 | async-start | bytes 11796480 | tf_op jit(solution)/shard_map/all_gather | solution.py:407
  7.2 1.6 copy-start.6
  8.9 2.7 copy-start.12
  11.5 187.5 %all-gather.3.cloned.1.call-start = ((), (), s32[]{:S(2)}) async-start(), calls=%async_computation.4 | async-start | bytes 7077888 | tf_op jit(solution)/shard_map/all_gather | solution.py:407
  63.8 3.4 %copy-start.11 = (bf16[16,128,256]{2,1,0:T(8,128)(2,1)S(1)}, bf16[16,128,256]{2,1,0:T(8,128)(2,1)}, u32[]{:S(2)}) copy-start(bf16[16,128,256]{2,1,0:T(8,128)(2,1)} %all_to_all.25.rest_1_) | copy-start | bytes 3145732
  67.4 23.9 %collective-permute-start = (bf16[2,2,2,256,256]{4,3,2,1,0:T(8,128)(2,1)S(1)}, bf16[2,2,2,256,256]{4,3,2,1,0:T(8,128)(2,1)S(1)}, u32[]{:S(2)}, u32[]{:S(2)}) collective-permute-start(bf16[2,2,2,256,256]{4,3,2,1,0:T(8,128)(2,1)S(1)} %bitcast.49), channel_id=1, source_target_pairs={{0,1},{1,0},{2,3},{3,2},{4,5},{5,4},{6,7},{7,6},{8,9},{9,8},{10,11... | collective-permute-start | bytes 3145736 | tf_op jit(solution)/shard_map/ppermute | solution.py:394
  69.8 21.3 %all-to-all-start = ((bf16[16,16,1]{1,2,0:T(2,128)(2,1)}), bf16[16,16,1]{1,2,0:T(2,128)(2,1)S(1)}, u32[]{:S(2)}, u32[]{:S(2)}) async-start(bf16[16,16,1]{1,2,0:T(2,128)(2,1)} %all_to_all.20), calls=%async_computation | async-start | bytes 16384 | tf_op jit(solution)/shard_map/all_to_all | solution.py:411
  138.3 14.8 %collective-permute-start.3 = (bf16[256,1024]{1,0:T(8,128)(2,1)S(1)}, bf16[256,1024]{1,0:T(8,128)(2,1)S(1)}, u32[]{:S(2)}, u32[]{:S(2)}) collective-permute-start(bf16[256,1024]{1,0:T(8,128)(2,1)S(1)} %get-tuple-element.27), channel_id=1, source_target_pairs={{0,4},{2,6},{4,0},{6,2},{8,12},{10,14},{12,8},{14,10},{16,20},{18,... | collective-permute-start | bytes 1572872 | tf_op jit(solution)/shard_map/ppermute | solution.py:432
  145.0 19.4 %collective-permute-start.2 = (bf16[256,1024]{1,0:T(8,128)(2,1)S(1)}, bf16[256,1024]{1,0:T(8,128)(2,1)S(1)}, u32[]{:S(2)}, u32[]{:S(2)}) collective-permute-start(bf16[256,1024]{1,0:T(8,128)(2,1)S(1)} %get-tuple-element.25), channel_id=1, source_target_pairs={{0,4},{2,6},{4,0},{6,2},{8,12},{10,14},{12,8},{14,10},{16,20},{18,... | collective-permute-start | bytes 1572872 | tf_op jit(solution)/shard_map/ppermute | solution.py:432
  157.9 4.2 %copy-start.9 = (bf16[256,1024]{1,0:T(8,128)(2,1)}, bf16[256,1024]{1,0:T(8,128)(2,1)S(1)}, u32[]{:S(2)}) copy-start(bf16[256,1024]{1,0:T(8,128)(2,1)S(1)} %get-tuple-element.30.refs_0_) | copy-start | bytes 1572868
  157.9 23.3 %collective-permute-start.4 = (bf16[256,1024]{1,0:T(8,128)(2,1)S(1)}, bf16[256,1024]{1,0:T(8,128)(2,1)S(1)}, u32[]{:S(2)}, u32[]{:S(2)}) collective-permute-start(bf16[256,1024]{1,0:T(8,128)(2,1)S(1)} %get-tuple-element.30.refs_0_), channel_id=1, source_target_pairs={{0,4},{2,6},{4,0},{6,2},{8,12},{10,14},{12,8},{14,10},{16,20},{18,... | collective-permute-start | bytes 1572872 | tf_op jit(solution)/shard_map/ppermute | solution.py:447
  162.1 19.1 %collective-permute-start.1 = (bf16[256,512]{1,0:T(8,128)(2,1)S(1)}, bf16[256,512]{1,0:T(8,128)(2,1)S(1)}, u32[]{:S(2)}, u32[]{:S(2)}) collective-permute-start(bf16[256,512]{1,0:T(8,128)(2,1)S(1)} %get-tuple-element.23), channel_id=1, source_target_pairs={{0,4},{2,6},{4,0},{6,2},{8,12},{10,14},{12,8},{14,10},{16,20},{18,... | collective-permute-start | bytes 786440 | tf_op jit(solution)/shard_map/ppermute | solution.py:432
  164.3 16.9 %copy-start.4 = (bf16[1024,2048]{1,0:T(8,128)(2,1)S(1)}, bf16[1024,2048]{1,0:T(8,128)(2,1)}, u32[]{:S(2)}) copy-start(bf16[1024,2048]{1,0:T(8,128)(2,1)} %queries.9) | copy-start | bytes 12582916
  169.4 39.3 %collective-permute-start.7 = (bf16[256,1024]{1,0:T(8,128)(2,1)}, bf16[256,1024]{1,0:T(8,128)(2,1)S(1)}, u32[]{:S(2)}, u32[]{:S(2)}) collective-permute-start(bf16[256,1024]{1,0:T(8,128)(2,1)} %get-tuple-element.37.refs_3_), channel_id=1, source_target_pairs={{0,4},{2,6},{4,0},{6,2},{8,12},{10,14},{12,8},{14,10},{16,20},{18,... | collective-permute-start | bytes 1572872 | tf_op jit(solution)/shard_map/ppermute | solution.py:447
  184.4 24.4 %collective-permute-start.8 = (bf16[256,512]{1,0:T(8,128)(2,1)S(1)}, bf16[256,512]{1,0:T(8,128)(2,1)}, u32[]{:S(2)}, u32[]{:S(2)}) collective-permute-start(bf16[256,512]{1,0:T(8,128)(2,1)S(1)} %get-tuple-element.31.rest_0_.refs_6_), channel_id=1, source_target_pairs={{0,4},{2,6},{4,0},{6,2},{8,12},{10,14},{12,8},{14,10},{16,20},{18,... | collective-permute-start | bytes 786440 | tf_op jit(solution)/shard_map/ppermute | solution.py:447
  203.8 4.9 %copy-start.10 = (bf16[256,1024]{1,0:T(8,128)(2,1)S(1)}, bf16[256,1024]{1,0:T(8,128)(2,1)}, u32[]{:S(2)}) copy-start(bf16[256,1024]{1,0:T(8,128)(2,1)} %copy-done.9) | copy-start | bytes 1572868
  203.9 15.8 %collective-permute-start.6 = (bf16[256,1024]{1,0:T(8,128)(2,1)S(1)}, bf16[256,1024]{1,0:T(8,128)(2,1)S(1)}, u32[]{:S(2)}, u32[]{:S(2)}) collective-permute-start(bf16[256,1024]{1,0:T(8,128)(2,1)S(1)} %get-tuple-element.35), channel_id=1, source_target_pairs={{0,4},{2,6},{4,0},{6,2},{8,12},{10,14},{12,8},{14,10},{16,20},{18,... | collective-permute-start | bytes 1572872 | tf_op jit(solution)/shard_map/ppermute | solution.py:432
  208.1 18.0 %collective-permute-start.5 = (bf16[256,512]{1,0:T(8,128)(2,1)S(1)}, bf16[256,512]{1,0:T(8,128)(2,1)S(1)}, u32[]{:S(2)}, u32[]{:S(2)}) collective-permute-start(bf16[256,512]{1,0:T(8,128)(2,1)S(1)} %get-tuple-element.33), channel_id=1, source_target_pairs={{0,4},{2,6},{4,0},{6,2},{8,12},{10,14},{12,8},{14,10},{16,20},{18,... | collective-permute-start | bytes 786440 | tf_op jit(solution)/shard_map/ppermute | solution.py:432
  219.6 6.5 %copy-start.5 = (bf16[1024,2048]{1,0:T(8,128)(2,1)S(1)}, bf16[1024,2048]{1,0:T(8,128)(2,1)}, u32[]{:S(2)}) copy-start(bf16[1024,2048]{1,0:T(8,128)(2,1)} %queries.9) | copy-start | bytes 12582916
  224.6 19.1 %collective-permute-start.10 = (bf16[256,1024]{1,0:T(8,128)(2,1)S(1)}, bf16[256,1024]{1,0:T(8,128)(2,1)S(1)}, u32[]{:S(2)}, u32[]{:S(2)}) collective-permute-start(bf16[256,1024]{1,0:T(8,128)(2,1)S(1)} %get-tuple-element.40.refs_0_), channel_id=1, source_target_pairs={{0,4},{2,6},{4,0},{6,2},{8,12},{10,14},{12,8},{14,10},{16,20},{18,... | collective-permute-start | bytes 1572872 | tf_op jit(solution)/shard_map/ppermute | solution.py:447
  226.1 3.3 %copy-start.2 = (f32[4,2,2,256,256]{4,3,2,1,0:T(8,128)S(1)}, f32[4,2,2,256,256]{4,3,2,1,0:T(8,128)}, u32[]{:S(2)}) copy-start(f32[4,2,2,256,256]{4,3,2,1,0:T(8,128)} %spread.5.rest_1_.refs_4_) | copy-start | bytes 12582916
  232.6 11.1 %copy-start.3 = (f32[4,2,2,256,256]{4,3,2,1,0:T(8,128)S(1)}, f32[4,2,2,256,256]{4,3,2,1,0:T(8,128)}, u32[]{:S(2)}) copy-start(f32[4,2,2,256,256]{4,3,2,1,0:T(8,128)} %spread.5.rest_1_.refs_4_) | copy-start | bytes 12582916
  232.6 15.2 %collective-permute-start.9 = (bf16[2,2,1,256,256]{4,3,2,1,0:T(8,128)(2,1)S(1)}, bf16[2,2,1,256,256]{4,3,2,1,0:T(8,128)(2,1)}, u32[]{:S(2)}, u32[]{:S(2)}) collective-permute-start(bf16[2,2,1,256,256]{4,3,2,1,0:T(8,128)(2,1)S(1)} %spread.6.refs_5_), channel_id=1, source_target_pairs={{0,1},{1,0},{2,3},{3,2},{4,5},{5,4},{6,7},{7,6},{8,9},{9,8},{10,11... | collective-permute-start | bytes 1572872 | tf_op jit(solution)/shard_map/ppermute | solution.py:394
  234.2 9.6 %collective-permute-start.11 = (bf16[256,512]{1,0:T(8,128)(2,1)S(1)}, bf16[256,512]{1,0:T(8,128)(2,1)S(1)}, u32[]{:S(2)}, u32[]{:S(2)}) collective-permute-start(bf16[256,512]{1,0:T(8,128)(2,1)S(1)} %get-tuple-element.41.refs_2_), channel_id=1, source_target_pairs={{0,4},{2,6},{4,0},{6,2},{8,12},{10,14},{12,8},{14,10},{16,20},{18,... | collective-permute-start | bytes 786440 | tf_op jit(solution)/shard_map/ppermute | solution.py:447
  247.0 0.8 copy-start.7
  247.8 5.7 %copy-start.8 = (bf16[2,2,1,256,256]{4,3,2,1,0:T(8,128)(2,1)S(1)}, bf16[2,2,1,256,256]{4,3,2,1,0:T(8,128)(2,1)}, u32[]{:S(2)}) copy-start(bf16[2,2,1,256,256]{4,3,2,1,0:T(8,128)(2,1)} %copy-done.7) | copy-start | bytes 1572868
  249.9 18.8 %all-to-all-start.2 = ((bf16[16,64,256]{2,1,0:T(8,128)(2,1)}), bf16[16,64,256]{2,1,0:T(8,128)(2,1)S(1)}, u32[]{:S(2)}, u32[]{:S(2)}) async-start(bf16[16,64,256]{2,1,0:T(8,128)(2,1)} %bitcast.12), calls=%async_computation.2 | async-start | bytes 1048576 | tf_op jit(solution)/shard_map/all_to_all | solution.py:479
  253.5 14.2 %collective-permute-start.12 = (bf16[2,2,1,256,256]{4,3,2,1,0:T(8,128)(2,1)S(1)}, bf16[2,2,1,256,256]{4,3,2,1,0:T(8,128)(2,1)S(1)}, u32[]{:S(2)}, u32[]{:S(2)}) collective-permute-start(bf16[2,2,1,256,256]{4,3,2,1,0:T(8,128)(2,1)S(1)} %copy-done.8), channel_id=1, source_target_pairs={{0,1},{1,0},{2,3},{3,2},{4,5},{5,4},{6,7},{7,6},{8,9},{9,8},{10,11... | collective-permute-start | bytes 1572872 | tf_op jit(solution)/shard_map/ppermute | solution.py:394
  268.7 20.3 %all-to-all-start.3 = ((bf16[16,64,256]{2,1,0:T(8,128)(2,1)}), bf16[16,64,256]{2,1,0:T(8,128)(2,1)S(1)}, u32[]{:S(2)}, u32[]{:S(2)}) async-start(bf16[16,64,256]{2,1,0:T(8,128)(2,1)} %bitcast.19), calls=%async_computation.3 | async-start | bytes 1048576 | tf_op jit(solution)/shard_map/all_to_all | solution.py:479
  274.6 15.9 %copy-start.1 = (bf16[128,2048]{1,0:T(8,128)(2,1)S(1)}, bf16[128,2048]{1,0:T(8,128)(2,1)}, u32[]{:S(2)}) copy-start(bf16[128,2048]{1,0:T(8,128)(2,1)} %param.10) | copy-start | bytes 1572868
Sparse Core Ops, SparseCore 0:
  11.7 121.8 all-gather.4
  135.2 63.8 all-gather.2

commit v4 on v3

--- a/solution.py
+++ b/solution.py
@@ -11,6 +11,7 @@
 HD = 256
 CAP_LIMIT = 10.0
 VMEM_LIMIT = 48 * 1024 * 1024
+VMEM_WHOLE = 60 * 1024 * 1024
 
 
 def slot_table(labels, capacity, peer_count):
@@ -108,7 +109,7 @@
             pltpu.VMEM((size, depth, 2 * HD), jnp.bfloat16),
             pltpu.SemaphoreType.DMA((3, size)),
         ],
-        compiler_params=pltpu.CompilerParams(vmem_limit_bytes=VMEM_LIMIT),
+        compiler_params=pltpu.CompilerParams(vmem_limit_bytes=VMEM_WHOLE),
         cost_estimate=pl.CostEstimate(
             flops=2 * depth * HD * size, bytes_accessed=16 * depth * HD * size, transcendentals=0
         ),
@@ -287,7 +288,9 @@
 
 def spread_kernel(pos, *refs, parts, sides, earlier):
     scratch = parts if len(sides) > 1 else 0
-    result, joined = refs[len(refs) - 1 - scratch], refs[len(refs) - scratch :]
+    result, mark = refs[len(refs) - 2 - scratch : len(refs) - scratch]
+    joined = refs[len(refs) - scratch :]
+    mark[...] = jnp.zeros_like(mark)
     stride = len(sides) + 1
     depth = result.shape[-1]
     slots = refs[0].shape[0]
@@ -360,10 +363,16 @@
             num_scalar_prefetch=1,
             grid=(count,),
             in_specs=in_specs,
-            out_specs=pl.BlockSpec(block, lambda step, pos: (step, 0, 0, 0, 0)),
+            out_specs=[
+                pl.BlockSpec(block, lambda step, pos: (step, 0, 0, 0, 0)),
+                pl.BlockSpec((8, 128), lambda step, pos: (0, 0)),
+            ],
             scratch_shapes=scratch,
         ),
-        out_shape=jax.ShapeDtypeStruct((count,) + block[1:], dtype),
+        out_shape=(
+            jax.ShapeDtypeStruct((count,) + block[1:], dtype),
+            jax.ShapeDtypeStruct((8, 128), jnp.float32),
+        ),
         compiler_params=pltpu.CompilerParams(vmem_limit_bytes=VMEM_LIMIT),
         cost_estimate=pl.CostEstimate(
             flops=2 * len(sides) * slots * 2 * count * depth * widths,
@@ -421,7 +430,7 @@
     for at, (first, size, weights) in enumerate(parts):
         final = at == len(parts) - 1
         if final:
-            early = spread(
+            early, done = spread(
                 pos, depth, units, None, (0, 1), 0, line, tensor_count, jnp.float32
             )
             units = []
@@ -441,24 +450,23 @@
                 received,
                 first + column // (2 * HD),
                 query_grad,
-                *((early,) if final else ()),
+                *((done,) if final else ()),
                 *exchanged[-2:-1],
             )
             exchanged.append(lax.ppermute(pair_grad, "dp", x_swap))
             units.append((pair_grad, exchanged[-1], weights, column))
             token = (pair_grad,)
 
-    sent, passed, kept = [], [], []
+    passed, kept, marks = [], [], []
     for side in range(2):
-        sent.append(
-            spread(
-                pos, depth, units, early, (side,), per_tensor, line - per_tensor, tensor_count,
-                jnp.bfloat16, *sent,
-            )
+        sent, mark = spread(
+            pos, depth, units, early, (side,), per_tensor, line - per_tensor, tensor_count,
+            jnp.bfloat16, *marks,
         )
+        marks.append(mark)
         passed.append(
             [
-                tensor_shift(sent[side][(shift - 1) * per_tensor : shift * per_tensor], shift)
+                tensor_shift(sent[(shift - 1) * per_tensor : shift * per_tensor], shift)
                 for shift in range(1, tensor_count)
             ]
         )
@@ -466,10 +474,10 @@
         kept.append(
             spread(
                 pos, depth, units, early, (side,), 0, per_tensor, tensor_count, jnp.float32,
-                sent[side], *kept,
-            )
+                marks[side],
+            )[0]
         )
-    passed[0] = [tie(part, sent[1]) for part in passed[0]]
+    kept[0] = tie(kept[0], marks[1])
 
     def send_home(kept, passed):
         for part in passed:

time: 298 us -> 297 us (level)
  waiting for transfers between devices: 109 us -> 105 us
  transfers between devices with their start and end apart: 18 -> 18, of which waited for: 9 -> 9; matrix products, arithmetic and copies ran while one was open for 1% -> 1% of each run, Pallas kernels for 23% -> 24%
where the time goes in v4:
time: 297 us; the launch traced here: 296 us
  waiting for transfers between devices  105 us (35%)
  Pallas kernels  73.3 us (25%)
  blocking collectives  50.3 us (17%)
  starting transfers between devices  40.1 us (14%)
  between operations  15.1 us (5%)
  local copies, waits for them, and re-layouts  8.52 us (3%)
    all_gather x2, waiting for transfers between devices, on_device(): lax.all_gather(block, 'dp', axis=0, tiled=True, axis_index_groups=columns)  54.5 us
    all_to_all x1, blocking collectives, on_device(): lax.all_to_all(outgoing, 'dp', split_axis=0, concat_axis=0, tiled=True)  50.3 us
    pallas_call x5, Pallas kernels, spread(): pl.pallas_call(functools.partial(spread_kernel, parts=len(units), sides=s...  24.5 us
    pallas_call x5, Pallas kernels, attend(): pl.pallas_call(functools.partial(attend_kernel, block), grid=(heads,), in...  21.4 us
    pallas_call x5, Pallas kernels, project(): pl.pallas_call(project_kernel, grid=(width // HD,), in_specs=[pl.BlockSpe...  20.1 us
    ppermute x5, waiting for transfers between devices, on_device(): products.append((column, mine, lax.ppermute(other, 'dp', x_swap)))  19 us
    all_to_all x1, starting transfers between devices, on_device(): lax.all_to_all(filled, 'dp', split_axis=0, concat_axis=0, tiled=True)  14.9 us
    all_to_all x2, waiting for transfers between devices, send_home(): lax.all_to_all(kept, 'dp', split_axis=0, concat_axis=0, tiled=True)  13.9 us
  transfers between devices with their start and end apart: 18, of which 9 were waited for; matrix products, arithmetic and copies ran while one was open for 1% of the time, Pallas kernels for 24%

profile of v4, /device:TPU:0, one launch (start us, length us, event | category | flops | bytes accessed | tf_op | source)
XLA Modules:
  0.0 296.1 jit_solution(11316093709675627914)
XLA Ops:
  7.2 3.1 %predict_first.1.rest_0_ = bf16[256,2560]{1,0:T(8,128)(2,1)} custom-call(bf16[2,256,2048]{2,1,0:T(8,128)(2,1)} %weights.3, f32[2,256,2048]{2,1,0:T(8,128)} %velocity.3), custom_call_target="tpu_custom_call" | custom-call | flops 655360 | bytes 5242880 | tf_op jit(solution)/shard_map/predict_first/pallas_call | solution.py:101
  11.3 0.8 reshape.99
  12.4 50.3 %all_to_all.25.rest_1_ = bf16[16,128,256]{2,1,0:T(8,128)(2,1)} all-to-all(bf16[16,128,256]{2,1,0:T(8,128)(2,1)S(1)} %bitcast.48), channel_id=1, replica_groups=mesh['dp'=16,'tensor'=2] {'dp'}, dimensions={0} | all-to-all | bytes 2097152 | tf_op jit(solution)/shard_map/all_to_all | solution.py:411
  62.7 3.4 %predict.1 = bf16[256,1536]{1,0:T(8,128)(2,1)} custom-call(bf16[2,256,2048]{2,1,0:T(8,128)(2,1)} %weights.3, f32[2,256,2048]{2,1,0:T(8,128)} %velocity.3, bf16[256,2560]{1,0:T(8,128)(2,1)} %predict_first.1.rest_0_, bf16[16,128,256]{2,1,0:T(8,128)(2,1)} %all_to_all.25.rest_1_), custom_call_target="tpu_custom_call" | custom-call | flops 393216 | bytes 3145728 | tf_op jit(solution)/shard_map/predict/pallas_call | solution.py:125
  66.3 1.6 collective-permute-start
  68.0 0.7 all_to_all.20
  68.7 14.9 %all-to-all-start = ((bf16[16,16,1]{1,2,0:T(2,128)(2,1)}), bf16[16,16,1]{1,2,0:T(2,128)(2,1)S(1)}, u32[]{:S(2)}, u32[]{:S(2)}) async-start(bf16[16,16,1]{1,2,0:T(2,128)(2,1)} %all_to_all.20), calls=%async_computation | async-start | bytes 16384 | tf_op jit(solution)/shard_map/all_to_all | solution.py:420
  83.6 6.3 %all-to-all-done = bf16[16,16,1]{1,2,0:T(2,128)(2,1)S(1)} async-done(((bf16[16,16,1]{1,2,0:T(2,128)(2,1)}), bf16[16,16,1]{1,2,0:T(2,128)(2,1)S(1)}, u32[]{:S(2)}, u32[]{:S(2)}) %all-to-all-start) | async-done | bytes 544 | tf_op jit(solution)/shard_map/all_to_all | solution.py:420
  90.3 0.8 arrange.1.rows
  91.1 41.2 %all-gather.5.cloned.1.call-done.weights.refs_2_.refs_5_.refs_8_ = bf16[2048,2560]{1,0:T(8,128)(2,1)} async-done(((bf16[256,2560]{1,0:T(8,128)(2,1)}), bf16[2048,2560]{1,0:T(8,128)(2,1)}) %all-gather.5.cloned.1.call-update) | async-done | bytes 10485776 | tf_op jit(solution)/shard_map/all_gather | solution.py:416
  132.4 4.7 %project.7 = (f32[256,1024]{1,0:T(8,128)S(1)}, bf16[256,1024]{1,0:T(8,128)(2,1)S(1)}) custom-call(bf16[512,2048]{1,0:T(8,128)(2,1)S(1)} %arrange.1.rows, bf16[2048,2560]{1,0:T(8,128)(2,1)} %all-gather.5.cloned.1.call-done.weights.refs_2_.refs_5_.refs_8_), custom_call_target="tpu_custom_call" | custom-call | flops 2147483648 | bytes 7864320 | tf_op jit(solution)/shard_map/project/pallas_call | solution.py:183
  137.1 1.5 collective-permute-start.3
  138.7 5.2 %project.6 = (f32[256,1024]{1,0:T(8,128)S(1)}, bf16[256,1024]{1,0:T(8,128)(2,1)S(1)}) custom-call(bf16[512,2048]{1,0:T(8,128)(2,1)S(1)} %arrange.1.rows, bf16[2048,2560]{1,0:T(8,128)(2,1)} %all-gather.5.cloned.1.call-done.weights.refs_2_.refs_5_.refs_8_), custom_call_target="tpu_custom_call" | custom-call | flops 2147483648 | bytes 7864320 | tf_op jit(solution)/shard_map/project/pallas_call | solution.py:183
  144.8 7.1 %collective-permute-done.3.received = bf16[256,1024]{1,0:T(8,128)(2,1)S(1)} collective-permute-done((bf16[256,1024]{1,0:T(8,128)(2,1)S(1)}, bf16[256,1024]{1,0:T(8,128)(2,1)S(1)}, u32[]{:S(2)}, u32[]{:S(2)}) %collective-permute-start.3) | collective-permute-done | bytes 524320 | tf_op jit(solution)/shard_map/ppermute | solution.py:441
  151.9 4.8 %attend.5 = (bf16[1024,2048]{1,0:T(8,128)(2,1)}, bf16[256,1024]{1,0:T(8,128)(2,1)S(1)}) custom-call(s32[1]{0:T(128)S(6)} %copy.97.live, f32[256,1]{1,0:T(8,128)S(1)} %reshape.115._.usable, bf16[1024,2048]{1,0:T(8,128)(2,1)} %queries.9, bf16[1024,2048]{1,0:T(8,128)(2,1)} %grads.9, f32[256,1024]{1,0:T(8,128)S(1)} %get-tuple-element.34.mine, ...), custom_call_target="tpu_custom_call" | custom-call | flops 1342177280 | bytes 5767168 | tf_op jit(solution)/shard_map/attend/pallas_call | solution.py:268
  156.8 1.5 collective-permute-start.4
  158.2 2.7 project.5
  161.6 1.6 collective-permute-done.2.received
  163.2 5.1 %attend.6 = (bf16[1024,2048]{1,0:T(8,128)(2,1)}, bf16[256,1024]{1,0:T(8,128)(2,1)}) custom-call(s32[1]{0:T(128)S(6)} %copy.97.live, f32[256,1]{1,0:T(8,128)S(1)} %reshape.115._.usable, bf16[1024,2048]{1,0:T(8,128)(2,1)} %queries.9, bf16[1024,2048]{1,0:T(8,128)(2,1)} %grads.9, ...), custom_call_target="tpu_custom_call", output_to_operand_aliasing={{0}: (6, {})} | custom-call | flops 1342177280 | bytes 5767168 | tf_op jit(solution)/shard_map/attend/pallas_call | solution.py:268
  168.3 1.4 collective-permute-start.7
  169.7 10.3 %collective-permute-done.1.received = bf16[256,512]{1,0:T(8,128)(2,1)S(1)} collective-permute-done((bf16[256,512]{1,0:T(8,128)(2,1)S(1)}, bf16[256,512]{1,0:T(8,128)(2,1)S(1)}, u32[]{:S(2)}, u32[]{:S(2)}) %collective-permute-start.1) | collective-permute-done | bytes 262176 | tf_op jit(solution)/shard_map/ppermute | solution.py:441
  180.0 3.2 %attend.7 = (bf16[1024,2048]{1,0:T(8,128)(2,1)}, bf16[256,512]{1,0:T(8,128)(2,1)S(1)}) custom-call(s32[1]{0:T(128)S(6)} %copy.97.live, f32[256,1]{1,0:T(8,128)S(1)} %reshape.115._.usable, bf16[1024,2048]{1,0:T(8,128)(2,1)S(1)} %copy-done.2, bf16[1024,2048]{1,0:T(8,128)(2,1)} %grads.9, ...), custom_call_target="tpu_custom_call", output_to_operand_aliasing={{0}: (6, {})} | custom-call | flops 671088640 | bytes 2883584 | tf_op jit(solution)/shard_map/attend/pallas_call | solution.py:268
  183.2 1.5 collective-permute-start.8
  184.7 13.3 %all-gather.3.cloned.1.call-done.weights.refs_1_.refs_3_ = bf16[2048,1536]{1,0:T(8,128)(2,1)} async-done(((bf16[256,1536]{1,0:T(8,128)(2,1)}), bf16[2048,1536]{1,0:T(8,128)(2,1)}) %all-gather.3.cloned.1.call-update) | async-done | bytes 6291472 | tf_op jit(solution)/shard_map/all_gather | solution.py:416
  197.9 4.7 %project.9 = (f32[256,1024]{1,0:T(8,128)S(1)}, bf16[256,1024]{1,0:T(8,128)(2,1)S(1)}) custom-call(bf16[512,2048]{1,0:T(8,128)(2,1)S(1)} %arrange.1.rows, bf16[2048,1536]{1,0:T(8,128)(2,1)} %all-gather.3.cloned.1.call-done.weights.refs_1_.refs_3_, bf16[256,512]{1,0:T(8,128)(2,1)S(1)} %get-tuple-element.39.rest_0_.refs_6_), custom_call_target="tpu_custom_call" | custom-call | flops 2147483648 | bytes 7864320 | tf_op jit(solution)/shard_map/project/pallas_call | solution.py:183
  202.7 1.5 collective-permute-start.6
  204.2 2.7 project.8
  207.6 10.9 %spread.5 = (f32[4,2,2,256,256]{4,3,2,1,0:T(8,128)}, f32[8,128]{1,0:T(8,128)S(1)}) custom-call(s32[4]{0:T(128)S(1)} %pad_add_fusion.pos, bf16[256,1024]{1,0:T(8,128)(2,1)S(1)} %copy-done.8, bf16[256,1024]{1,0:T(8,128)(2,1)S(1)} %collective-permute-done.4.rest_1_.refs_1_, bf16[2048,2560]{1,0:T(8,128)(2,1)} %all-gather.5.cloned.1.call-done.weights.refs_2_.refs_5_.refs_8_, ...), custom_call_target="tpu_custom_call" | custom-call | flops 5368709120 | bytes 18874368 | tf_op jit(solution)/shard_map/spread/pallas_call | solution.py:358
  218.5 5.0 %attend.8 = (bf16[1024,2048]{1,0:T(8,128)(2,1)}, bf16[256,1024]{1,0:T(8,128)(2,1)S(1)}) custom-call(s32[1]{0:T(128)S(6)} %copy.97.live, f32[256,1]{1,0:T(8,128)S(1)} %reshape.115._.usable, bf16[1024,2048]{1,0:T(8,128)(2,1)} %queries.9, bf16[1024,2048]{1,0:T(8,128)(2,1)} %grads.9, ...), custom_call_target="tpu_custom_call", output_to_operand_aliasing={{0}: (6, {})} | custom-call | flops 1342177280 | bytes 5767168 | tf_op jit(solution)/shard_map/attend/pallas_call | solution.py:268
  223.5 1.5 collective-permute-start.9
  224.9 3.3 %attend.9 = (bf16[1024,2048]{1,0:T(8,128)(2,1)}, bf16[256,512]{1,0:T(8,128)(2,1)S(1)}) custom-call(s32[1]{0:T(128)S(6)} %copy.97.live, f32[256,1]{1,0:T(8,128)S(1)} %reshape.115._.usable, bf16[1024,2048]{1,0:T(8,128)(2,1)S(1)} %copy-done.3, bf16[1024,2048]{1,0:T(8,128)(2,1)} %grads.9, ...), custom_call_target="tpu_custom_call", output_to_operand_aliasing={{0}: (6, {})} | custom-call | flops 671088640 | bytes 2883584 | tf_op jit(solution)/shard_map/attend/pallas_call | solution.py:268
  228.2 3.2 %spread.6 = (bf16[2,2,1,256,256]{4,3,2,1,0:T(8,128)(2,1)S(1)}, f32[8,128]{1,0:T(8,128)S(1)}) custom-call(s32[4]{0:T(128)S(1)} %pad_add_fusion.pos, bf16[256,1024]{1,0:T(8,128)(2,1)S(1)} %get-tuple-element.49.refs_0_, bf16[2048,1536]{1,0:T(8,128)(2,1)} %all-gather.3.cloned.1.call-done.weights.refs_1_.refs_3_, bf16[256,512]{1,0:T(8,128)(2,1)S(1)} %get-tuple-element.50.refs_2_, ...), custom_call_target="tpu_custom_call" | custom-call | flops 805306368 | bytes 5242880 | tf_op jit(solution)/shard_map/spread/pallas_call | solution.py:358
  231.5 1.5 collective-permute-start.11
  233.6 3.6 %spread.7 = (f32[2,2,1,256,256]{4,3,2,1,0:T(8,128)S(1)}, f32[8,128]{1,0:T(8,128)}) custom-call(s32[4]{0:T(128)S(1)} %pad_add_fusion.pos, bf16[256,1024]{1,0:T(8,128)(2,1)S(1)} %get-tuple-element.49.refs_0_, bf16[2048,1536]{1,0:T(8,128)(2,1)} %all-gather.3.cloned.1.call-done.weights.refs_1_.refs_3_, bf16[256,512]{1,0:T(8,128)(2,1)S(1)} %get-tuple-element.50.refs_2_, ...), custom_call_target="tpu_custom_call" | custom-call | flops 805306368 | bytes 5242880 | tf_op jit(solution)/shard_map/spread/pallas_call | solution.py:358
  237.2 1.0 copy-done.6
  238.2 4.4 %collective-permute-done.10.refs_2_ = bf16[256,512]{1,0:T(8,128)(2,1)S(1)} collective-permute-done((bf16[256,512]{1,0:T(8,128)(2,1)S(1)}, bf16[256,512]{1,0:T(8,128)(2,1)S(1)}, u32[]{:S(2)}, u32[]{:S(2)}) %collective-permute-start.10) | collective-permute-done | bytes 262176 | tf_op jit(solution)/shard_map/ppermute | solution.py:456
  242.6 3.2 %spread.8 = (bf16[2,2,1,256,256]{4,3,2,1,0:T(8,128)(2,1)S(1)}, f32[8,128]{1,0:T(8,128)S(1)}) custom-call(s32[4]{0:T(128)S(1)} %pad_add_fusion.pos, bf16[256,1024]{1,0:T(8,128)(2,1)S(1)} %collective-permute-done.9.refs_0_, bf16[2048,1536]{1,0:T(8,128)(2,1)} %all-gather.3.cloned.1.call-done.weights.refs_1_.refs_3_, ...), custom_call_target="tpu_custom_call" | custom-call | flops 805306368 | bytes 5242880 | tf_op jit(solution)/shard_map/spread/pallas_call | solution.py:358
  246.4 1.4 add_convert_fusion.1
  247.8 0.8 copy.68
  248.7 3.6 %all-to-all-start.2 = ((bf16[16,64,256]{2,1,0:T(8,128)(2,1)}), bf16[16,64,256]{2,1,0:T(8,128)(2,1)S(1)}, u32[]{:S(2)}, u32[]{:S(2)}) async-start(bf16[16,64,256]{2,1,0:T(8,128)(2,1)} %bitcast.12), calls=%async_computation.2 | async-start | bytes 1048576 | tf_op jit(solution)/shard_map/all_to_all | solution.py:487
  252.3 1.5 collective-permute-start.12
  253.8 2.2 copy-done.5
  256.0 3.6 %spread.9 = (f32[2,2,1,256,256]{4,3,2,1,0:T(8,128)S(1)}, f32[8,128]{1,0:T(8,128)}) custom-call(s32[4]{0:T(128)S(1)} %pad_add_fusion.pos, bf16[256,1024]{1,0:T(8,128)(2,1)S(1)} %collective-permute-done.9.refs_0_, bf16[2048,1536]{1,0:T(8,128)(2,1)} %all-gather.3.cloned.1.call-done.weights.refs_1_.refs_3_, ...), custom_call_target="tpu_custom_call" | custom-call | flops 805306368 | bytes 5242880 | tf_op jit(solution)/shard_map/spread/pallas_call | solution.py:358
  259.6 6.8 %collective-permute-done.12 = bf16[2,2,1,256,256]{4,3,2,1,0:T(8,128)(2,1)S(1)} collective-permute-done((bf16[2,2,1,256,256]{4,3,2,1,0:T(8,128)(2,1)S(1)}, bf16[2,2,1,256,256]{4,3,2,1,0:T(8,128)(2,1)S(1)}, u32[]{:S(2)}, u32[]{:S(2)}) %collective-permute-start.12) | collective-permute-done | bytes 524320 | tf_op jit(solution)/shard_map/ppermute | solution.py:403
  266.5 0.9 copy.70
  267.4 5.8 %all-to-all-start.3 = ((bf16[16,64,256]{2,1,0:T(8,128)(2,1)}), bf16[16,64,256]{2,1,0:T(8,128)(2,1)S(1)}, u32[]{:S(2)}, u32[]{:S(2)}) async-start(bf16[16,64,256]{2,1,0:T(8,128)(2,1)} %bitcast.19), calls=%async_computation.3 | async-start | bytes 1048576 | tf_op jit(solution)/shard_map/all_to_all | solution.py:487
  273.8 13.9 %all-to-all-done.3 = bf16[16,64,256]{2,1,0:T(8,128)(2,1)S(1)} async-done(((bf16[16,64,256]{2,1,0:T(8,128)(2,1)}), bf16[16,64,256]{2,1,0:T(8,128)(2,1)S(1)}, u32[]{:S(2)}, u32[]{:S(2)}) %all-to-all-start.3) | async-done | bytes 524320 | tf_op jit(solution)/shard_map/all_to_all | solution.py:487
  288.2 1.0 copy.73
  (62 shorter events, 5.8 us)
Async XLA Ops:
  7.2 3.7 %copy-start = (bf16[128,2048]{1,0:T(8,128)(2,1)S(1)}, bf16[128,2048]{1,0:T(8,128)(2,1)}, u32[]{:S(2)}) copy-start(bf16[128,2048]{1,0:T(8,128)(2,1)} %param.10) | copy-start | bytes 1572868
  7.2 3.3 %copy-start.12 = (s32[128,1]{0,1:T(1,128)S(1)}, s32[128,1]{0,1:T(1,128)}, u32[]{:S(2)}) copy-start(s32[128,1]{0,1:T(1,128)} %param.11) | copy-start | bytes 1540
  7.2 125.2 %all-gather.5.cloned.1.call-start = ((), (), s32[]{:S(2)}) async-start(), calls=%async_computation.5 | async-start | bytes 11796480 | tf_op jit(solution)/shard_map/all_gather | solution.py:416
  10.4 187.5 %all-gather.3.cloned.1.call-start = ((), (), s32[]{:S(2)}) async-start(), calls=%async_computation.4 | async-start | bytes 7077888 | tf_op jit(solution)/shard_map/all_gather | solution.py:416
  62.7 3.5 %copy-start.11 = (bf16[16,128,256]{2,1,0:T(8,128)(2,1)S(1)}, bf16[16,128,256]{2,1,0:T(8,128)(2,1)}, u32[]{:S(2)}) copy-start(bf16[16,128,256]{2,1,0:T(8,128)(2,1)} %all_to_all.25.rest_1_) | copy-start | bytes 3145732
  66.3 23.9 %collective-permute-start = (bf16[2,2,2,256,256]{4,3,2,1,0:T(8,128)(2,1)S(1)}, bf16[2,2,2,256,256]{4,3,2,1,0:T(8,128)(2,1)S(1)}, u32[]{:S(2)}, u32[]{:S(2)}) collective-permute-start(bf16[2,2,2,256,256]{4,3,2,1,0:T(8,128)(2,1)S(1)} %bitcast.49), channel_id=1, source_target_pairs={{0,1},{1,0},{2,3},{3,2},{4,5},{5,4},{6,7},{7,6},{8,9},{9,8},{10,11... | collective-permute-start | bytes 3145736 | tf_op jit(solution)/shard_map/ppermute | solution.py:403
  68.7 21.3 %all-to-all-start = ((bf16[16,16,1]{1,2,0:T(2,128)(2,1)}), bf16[16,16,1]{1,2,0:T(2,128)(2,1)S(1)}, u32[]{:S(2)}, u32[]{:S(2)}) async-start(bf16[16,16,1]{1,2,0:T(2,128)(2,1)} %all_to_all.20), calls=%async_computation | async-start | bytes 16384 | tf_op jit(solution)/shard_map/all_to_all | solution.py:420
  137.1 14.8 %collective-permute-start.3 = (bf16[256,1024]{1,0:T(8,128)(2,1)S(1)}, bf16[256,1024]{1,0:T(8,128)(2,1)S(1)}, u32[]{:S(2)}, u32[]{:S(2)}) collective-permute-start(bf16[256,1024]{1,0:T(8,128)(2,1)S(1)} %get-tuple-element.35), channel_id=1, source_target_pairs={{0,4},{2,6},{4,0},{6,2},{8,12},{10,14},{12,8},{14,10},{16,20},{18,... | collective-permute-start | bytes 1572872 | tf_op jit(solution)/shard_map/ppermute | solution.py:441
  143.8 19.4 %collective-permute-start.2 = (bf16[256,1024]{1,0:T(8,128)(2,1)S(1)}, bf16[256,1024]{1,0:T(8,128)(2,1)S(1)}, u32[]{:S(2)}, u32[]{:S(2)}) collective-permute-start(bf16[256,1024]{1,0:T(8,128)(2,1)S(1)} %get-tuple-element.33), channel_id=1, source_target_pairs={{0,4},{2,6},{4,0},{6,2},{8,12},{10,14},{12,8},{14,10},{16,20},{18,... | collective-permute-start | bytes 1572872 | tf_op jit(solution)/shard_map/ppermute | solution.py:441
  156.8 4.2 %copy-start.7 = (bf16[256,1024]{1,0:T(8,128)(2,1)}, bf16[256,1024]{1,0:T(8,128)(2,1)S(1)}, u32[]{:S(2)}) copy-start(bf16[256,1024]{1,0:T(8,128)(2,1)S(1)} %get-tuple-element.38.refs_0_) | copy-start | bytes 1572868
  156.8 23.3 %collective-permute-start.4 = (bf16[256,1024]{1,0:T(8,128)(2,1)S(1)}, bf16[256,1024]{1,0:T(8,128)(2,1)S(1)}, u32[]{:S(2)}, u32[]{:S(2)}) collective-permute-start(bf16[256,1024]{1,0:T(8,128)(2,1)S(1)} %get-tuple-element.38.refs_0_), channel_id=1, source_target_pairs={{0,4},{2,6},{4,0},{6,2},{8,12},{10,14},{12,8},{14,10},{16,20},{18,... | collective-permute-start | bytes 1572872 | tf_op jit(solution)/shard_map/ppermute | solution.py:456
  161.0 19.1 %collective-permute-start.1 = (bf16[256,512]{1,0:T(8,128)(2,1)S(1)}, bf16[256,512]{1,0:T(8,128)(2,1)S(1)}, u32[]{:S(2)}, u32[]{:S(2)}) collective-permute-start(bf16[256,512]{1,0:T(8,128)(2,1)S(1)} %get-tuple-element.31), channel_id=1, source_target_pairs={{0,4},{2,6},{4,0},{6,2},{8,12},{10,14},{12,8},{14,10},{16,20},{18,... | collective-permute-start | bytes 786440 | tf_op jit(solution)/shard_map/ppermute | solution.py:441
  163.2 16.9 %copy-start.2 = (bf16[1024,2048]{1,0:T(8,128)(2,1)S(1)}, bf16[1024,2048]{1,0:T(8,128)(2,1)}, u32[]{:S(2)}) copy-start(bf16[1024,2048]{1,0:T(8,128)(2,1)} %queries.9) | copy-start | bytes 12582916
  168.3 39.3 %collective-permute-start.7 = (bf16[256,1024]{1,0:T(8,128)(2,1)}, bf16[256,1024]{1,0:T(8,128)(2,1)S(1)}, u32[]{:S(2)}, u32[]{:S(2)}) collective-permute-start(bf16[256,1024]{1,0:T(8,128)(2,1)} %get-tuple-element.45.refs_3_), channel_id=1, source_target_pairs={{0,4},{2,6},{4,0},{6,2},{8,12},{10,14},{12,8},{14,10},{16,20},{18,... | collective-permute-start | bytes 1572872 | tf_op jit(solution)/shard_map/ppermute | solution.py:456
  183.2 24.4 %collective-permute-start.8 = (bf16[256,512]{1,0:T(8,128)(2,1)S(1)}, bf16[256,512]{1,0:T(8,128)(2,1)}, u32[]{:S(2)}, u32[]{:S(2)}) collective-permute-start(bf16[256,512]{1,0:T(8,128)(2,1)S(1)} %get-tuple-element.39.rest_0_.refs_6_), channel_id=1, source_target_pairs={{0,4},{2,6},{4,0},{6,2},{8,12},{10,14},{12,8},{14,10},{16,20},{18,... | collective-permute-start | bytes 786440 | tf_op jit(solution)/shard_map/ppermute | solution.py:456
  202.7 4.9 %copy-start.8 = (bf16[256,1024]{1,0:T(8,128)(2,1)S(1)}, bf16[256,1024]{1,0:T(8,128)(2,1)}, u32[]{:S(2)}) copy-start(bf16[256,1024]{1,0:T(8,128)(2,1)} %copy-done.7) | copy-start | bytes 1572868
  202.7 15.8 %collective-permute-start.6 = (bf16[256,1024]{1,0:T(8,128)(2,1)S(1)}, bf16[256,1024]{1,0:T(8,128)(2,1)S(1)}, u32[]{:S(2)}, u32[]{:S(2)}) collective-permute-start(bf16[256,1024]{1,0:T(8,128)(2,1)S(1)} %get-tuple-element.43), channel_id=1, source_target_pairs={{0,4},{2,6},{4,0},{6,2},{8,12},{10,14},{12,8},{14,10},{16,20},{18,... | collective-permute-start | bytes 1572872 | tf_op jit(solution)/shard_map/ppermute | solution.py:441
  206.9 18.0 %collective-permute-start.5 = (bf16[256,512]{1,0:T(8,128)(2,1)S(1)}, bf16[256,512]{1,0:T(8,128)(2,1)S(1)}, u32[]{:S(2)}, u32[]{:S(2)}) collective-permute-start(bf16[256,512]{1,0:T(8,128)(2,1)S(1)} %get-tuple-element.41), channel_id=1, source_target_pairs={{0,4},{2,6},{4,0},{6,2},{8,12},{10,14},{12,8},{14,10},{16,20},{18,... | collective-permute-start | bytes 786440 | tf_op jit(solution)/shard_map/ppermute | solution.py:441
  218.5 6.5 %copy-start.3 = (bf16[1024,2048]{1,0:T(8,128)(2,1)S(1)}, bf16[1024,2048]{1,0:T(8,128)(2,1)}, u32[]{:S(2)}) copy-start(bf16[1024,2048]{1,0:T(8,128)(2,1)} %queries.9) | copy-start | bytes 12582916
  223.5 19.1 %collective-permute-start.9 = (bf16[256,1024]{1,0:T(8,128)(2,1)S(1)}, bf16[256,1024]{1,0:T(8,128)(2,1)S(1)}, u32[]{:S(2)}, u32[]{:S(2)}) collective-permute-start(bf16[256,1024]{1,0:T(8,128)(2,1)S(1)} %get-tuple-element.49.refs_0_), channel_id=1, source_target_pairs={{0,4},{2,6},{4,0},{6,2},{8,12},{10,14},{12,8},{14,10},{16,20},{18,... | collective-permute-start | bytes 1572872 | tf_op jit(solution)/shard_map/ppermute | solution.py:456
  224.9 3.3 %copy-start.4 = (f32[4,2,2,256,256]{4,3,2,1,0:T(8,128)S(1)}, f32[4,2,2,256,256]{4,3,2,1,0:T(8,128)}, u32[]{:S(2)}) copy-start(f32[4,2,2,256,256]{4,3,2,1,0:T(8,128)} %get-tuple-element.51.refs_4_) | copy-start | bytes 12582916
  231.5 15.0 %collective-permute-start.11 = (bf16[2,2,1,256,256]{4,3,2,1,0:T(8,128)(2,1)S(1)}, bf16[2,2,1,256,256]{4,3,2,1,0:T(8,128)(2,1)S(1)}, u32[]{:S(2)}, u32[]{:S(2)}) collective-permute-start(bf16[2,2,1,256,256]{4,3,2,1,0:T(8,128)(2,1)S(1)} %get-tuple-element.55), channel_id=1, source_target_pairs={{0,1},{1,0},{2,3},{3,2},{4,5},{5,4},{6,7},{7,6},{8,9},{9,8},{10,11... | collective-permute-start | bytes 1572872 | tf_op jit(solution)/shard_map/ppermute | solution.py:403
  233.0 9.6 %collective-permute-start.10 = (bf16[256,512]{1,0:T(8,128)(2,1)S(1)}, bf16[256,512]{1,0:T(8,128)(2,1)S(1)}, u32[]{:S(2)}, u32[]{:S(2)}) collective-permute-start(bf16[256,512]{1,0:T(8,128)(2,1)S(1)} %get-tuple-element.50.refs_2_), channel_id=1, source_target_pairs={{0,4},{2,6},{4,0},{6,2},{8,12},{10,14},{12,8},{14,10},{16,20},{18,... | collective-permute-start | bytes 786440 | tf_op jit(solution)/shard_map/ppermute | solution.py:456
  237.2 1.0 copy-start.6
  245.8 0.6 copy-start.9
  246.4 7.4 %copy-start.10 = (f32[8,128]{1,0:T(8,128)S(1)}, f32[8,128]{1,0:T(8,128)}, u32[]{:S(2)}) copy-start(f32[8,128]{1,0:T(8,128)} %copy-done.9) | copy-start | bytes 12292
  248.7 18.7 %all-to-all-start.2 = ((bf16[16,64,256]{2,1,0:T(8,128)(2,1)}), bf16[16,64,256]{2,1,0:T(8,128)(2,1)S(1)}, u32[]{:S(2)}, u32[]{:S(2)}) async-start(bf16[16,64,256]{2,1,0:T(8,128)(2,1)} %bitcast.12), calls=%async_computation.2 | async-start | bytes 1048576 | tf_op jit(solution)/shard_map/all_to_all | solution.py:487
  252.3 14.1 %collective-permute-start.12 = (bf16[2,2,1,256,256]{4,3,2,1,0:T(8,128)(2,1)S(1)}, bf16[2,2,1,256,256]{4,3,2,1,0:T(8,128)(2,1)S(1)}, u32[]{:S(2)}, u32[]{:S(2)}) collective-permute-start(bf16[2,2,1,256,256]{4,3,2,1,0:T(8,128)(2,1)S(1)} %get-tuple-element.57), channel_id=1, source_target_pairs={{0,1},{1,0},{2,3},{3,2},{4,5},{5,4},{6,7},{7,6},{8,9},{9,8},{10,11... | collective-permute-start | bytes 1572872 | tf_op jit(solution)/shard_map/ppermute | solution.py:403
  253.8 2.2 copy-start.5
  267.4 20.3 %all-to-all-start.3 = ((bf16[16,64,256]{2,1,0:T(8,128)(2,1)}), bf16[16,64,256]{2,1,0:T(8,128)(2,1)S(1)}, u32[]{:S(2)}, u32[]{:S(2)}) async-start(bf16[16,64,256]{2,1,0:T(8,128)(2,1)} %bitcast.19), calls=%async_computation.3 | async-start | bytes 1048576 | tf_op jit(solution)/shard_map/all_to_all | solution.py:487
  273.4 15.9 %copy-start.1 = (bf16[128,2048]{1,0:T(8,128)(2,1)S(1)}, bf16[128,2048]{1,0:T(8,128)(2,1)}, u32[]{:S(2)}) copy-start(bf16[128,2048]{1,0:T(8,128)(2,1)} %param.10) | copy-start | bytes 1572868
Sparse Core Ops, SparseCore 0:
  10.5 121.8 all-gather.4
  134.0 63.8 all-gather.2

commit v5 on v4

--- a/solution.py
+++ b/solution.py
@@ -317,7 +317,7 @@
         for at in range(len(sides)):
             share = total[at * slots : (at + 1) * slots, core * depth : (core + 1) * depth]
             if earlier:
-                share = share + refs[stride * parts][0, core, at]
+                share = share + refs[stride * parts][0, core, at].astype(jnp.float32)
             result[0, core, at] = share.astype(result.dtype)
 
 
@@ -431,7 +431,7 @@
         final = at == len(parts) - 1
         if final:
             early, done = spread(
-                pos, depth, units, None, (0, 1), 0, line, tensor_count, jnp.float32
+                pos, depth, units, None, (0, 1), 0, line, tensor_count, jnp.bfloat16
             )
             units = []
         products, column = [], 0
@@ -477,7 +477,6 @@
                 marks[side],
             )[0]
         )
-    kept[0] = tie(kept[0], marks[1])
 
     def send_home(kept, passed):
         for part in passed:

time: 297 us -> 296 us (level)
  waiting for transfers between devices: 105 us -> 109 us
  local copies, waits for them, and re-layouts: 8.52 us -> 4.78 us
    ppermute x3, waiting for transfers between devices: 6.8 us -> 14.4 us  [tensor_shift(): return lax.ppermute(value, 'tensor', pairs)]
    unnamed x27 -> x17, local copies, waits for them, and re-layouts: 4.82 us -> 1.05 us
  transfers between devices with their start and end apart: 18 -> 18, of which waited for: 9 -> 11; matrix products, arithmetic and copies ran while one was open for 1% -> 2% of each run, Pallas kernels for 24% -> 21%
where the time goes in v5:
time: 296 us; the launch traced here: 295 us
  waiting for transfers between devices  109 us (37%)
  Pallas kernels  71.9 us (24%)
  blocking collectives  50.3 us (17%)
  starting transfers between devices  39.8 us (13%)
  between operations  15.1 us (5%)
  local copies, waits for them, and re-layouts  4.78 us (2%)
    all_gather x2, waiting for transfers between devices, on_device(): lax.all_gather(block, 'dp', axis=0, tiled=True, axis_index_groups=columns)  54.5 us
    all_to_all x1, blocking collectives, on_device(): lax.all_to_all(outgoing, 'dp', split_axis=0, concat_axis=0, tiled=True)  50.3 us
    pallas_call x5, Pallas kernels, spread(): pl.pallas_call(functools.partial(spread_kernel, parts=len(units), sides=s...  23.3 us
    pallas_call x5, Pallas kernels, attend(): pl.pallas_call(functools.partial(attend_kernel, block), grid=(heads,), in...  21.2 us
    pallas_call x5, Pallas kernels, project(): pl.pallas_call(project_kernel, grid=(width // HD,), in_specs=[pl.BlockSpe...  20.1 us
    ppermute x5, waiting for transfers between devices, on_device(): products.append((column, mine, lax.ppermute(other, 'dp', x_swap)))  19.5 us
    all_to_all x1, starting transfers between devices, on_device(): lax.all_to_all(filled, 'dp', split_axis=0, concat_axis=0, tiled=True)  14.9 us
    ppermute x3, waiting for transfers between devices, tensor_shift(): return lax.ppermute(value, 'tensor', pairs)  14.4 us
  transfers between devices with their start and end apart: 18, of which 11 were waited for; matrix products, arithmetic and copies ran while one was open for 2% of the time, Pallas kernels for 21%

profile of v5, /device:TPU:0, one launch (start us, length us, event | category | flops | bytes accessed | tf_op | source)
XLA Modules:
  0.0 294.6 jit_solution(6826946951605201157)
XLA Ops:
  7.2 3.1 %predict_first.1.rest_0_ = bf16[256,2560]{1,0:T(8,128)(2,1)} custom-call(bf16[2,256,2048]{2,1,0:T(8,128)(2,1)} %weights.3, f32[2,256,2048]{2,1,0:T(8,128)} %velocity.3), custom_call_target="tpu_custom_call" | custom-call | flops 655360 | bytes 5242880 | tf_op jit(solution)/shard_map/predict_first/pallas_call | solution.py:101
  11.3 0.8 reshape.99
  12.4 50.3 %all_to_all.25.rest_1_ = bf16[16,128,256]{2,1,0:T(8,128)(2,1)} all-to-all(bf16[16,128,256]{2,1,0:T(8,128)(2,1)S(1)} %bitcast.48), channel_id=1, replica_groups=mesh['dp'=16,'tensor'=2] {'dp'}, dimensions={0} | all-to-all | bytes 2097152 | tf_op jit(solution)/shard_map/all_to_all | solution.py:411
  62.7 3.4 %predict.1 = bf16[256,1536]{1,0:T(8,128)(2,1)} custom-call(bf16[2,256,2048]{2,1,0:T(8,128)(2,1)} %weights.3, f32[2,256,2048]{2,1,0:T(8,128)} %velocity.3, bf16[256,2560]{1,0:T(8,128)(2,1)} %predict_first.1.rest_0_, bf16[16,128,256]{2,1,0:T(8,128)(2,1)} %all_to_all.25.rest_1_), custom_call_target="tpu_custom_call" | custom-call | flops 393216 | bytes 3145728 | tf_op jit(solution)/shard_map/predict/pallas_call | solution.py:125
  66.2 1.6 collective-permute-start
  67.9 0.7 all_to_all.20
  68.6 14.9 %all-to-all-start = ((bf16[16,16,1]{1,2,0:T(2,128)(2,1)}), bf16[16,16,1]{1,2,0:T(2,128)(2,1)S(1)}, u32[]{:S(2)}, u32[]{:S(2)}) async-start(bf16[16,16,1]{1,2,0:T(2,128)(2,1)} %all_to_all.20), calls=%async_computation | async-start | bytes 16384 | tf_op jit(solution)/shard_map/all_to_all | solution.py:420
  83.6 6.4 %all-to-all-done = bf16[16,16,1]{1,2,0:T(2,128)(2,1)S(1)} async-done(((bf16[16,16,1]{1,2,0:T(2,128)(2,1)}), bf16[16,16,1]{1,2,0:T(2,128)(2,1)S(1)}, u32[]{:S(2)}, u32[]{:S(2)}) %all-to-all-start) | async-done | bytes 544 | tf_op jit(solution)/shard_map/all_to_all | solution.py:420
  90.3 0.8 arrange.1.rows
  91.1 41.3 %all-gather.5.cloned.1.call-done.weights.refs_2_.refs_5_.refs_8_ = bf16[2048,2560]{1,0:T(8,128)(2,1)} async-done(((bf16[256,2560]{1,0:T(8,128)(2,1)}), bf16[2048,2560]{1,0:T(8,128)(2,1)}) %all-gather.5.cloned.1.call-update) | async-done | bytes 10485776 | tf_op jit(solution)/shard_map/all_gather | solution.py:416
  132.4 4.7 %project.7 = (f32[256,1024]{1,0:T(8,128)S(1)}, bf16[256,1024]{1,0:T(8,128)(2,1)S(1)}) custom-call(bf16[512,2048]{1,0:T(8,128)(2,1)S(1)} %arrange.1.rows, bf16[2048,2560]{1,0:T(8,128)(2,1)} %all-gather.5.cloned.1.call-done.weights.refs_2_.refs_5_.refs_8_), custom_call_target="tpu_custom_call" | custom-call | flops 2147483648 | bytes 7864320 | tf_op jit(solution)/shard_map/project/pallas_call | solution.py:183
  137.1 1.5 collective-permute-start.3
  138.7 5.2 %project.6 = (f32[256,1024]{1,0:T(8,128)S(1)}, bf16[256,1024]{1,0:T(8,128)(2,1)S(1)}) custom-call(bf16[512,2048]{1,0:T(8,128)(2,1)S(1)} %arrange.1.rows, bf16[2048,2560]{1,0:T(8,128)(2,1)} %all-gather.5.cloned.1.call-done.weights.refs_2_.refs_5_.refs_8_), custom_call_target="tpu_custom_call" | custom-call | flops 2147483648 | bytes 7864320 | tf_op jit(solution)/shard_map/project/pallas_call | solution.py:183
  144.8 7.1 %collective-permute-done.3.received = bf16[256,1024]{1,0:T(8,128)(2,1)S(1)} collective-permute-done((bf16[256,1024]{1,0:T(8,128)(2,1)S(1)}, bf16[256,1024]{1,0:T(8,128)(2,1)S(1)}, u32[]{:S(2)}, u32[]{:S(2)}) %collective-permute-start.3) | collective-permute-done | bytes 524320 | tf_op jit(solution)/shard_map/ppermute | solution.py:441
  151.9 4.8 %attend.5 = (bf16[1024,2048]{1,0:T(8,128)(2,1)}, bf16[256,1024]{1,0:T(8,128)(2,1)S(1)}) custom-call(s32[1]{0:T(128)S(6)} %copy.95.live, f32[256,1]{1,0:T(8,128)S(1)} %reshape.115._.usable, bf16[1024,2048]{1,0:T(8,128)(2,1)} %queries.9, bf16[1024,2048]{1,0:T(8,128)(2,1)} %grads.9, f32[256,1024]{1,0:T(8,128)S(1)} %get-tuple-element.34.mine, ...), custom_call_target="tpu_custom_call" | custom-call | flops 1342177280 | bytes 5767168 | tf_op jit(solution)/shard_map/attend/pallas_call | solution.py:268
  156.8 1.5 collective-permute-start.4
  158.2 2.7 project.5
  161.0 0.6 collective-permute-start.1
  161.6 1.6 collective-permute-done.2.received
  163.2 5.1 %attend.6 = (bf16[1024,2048]{1,0:T(8,128)(2,1)}, bf16[256,1024]{1,0:T(8,128)(2,1)}) custom-call(s32[1]{0:T(128)S(6)} %copy.95.live, f32[256,1]{1,0:T(8,128)S(1)} %reshape.115._.usable, bf16[1024,2048]{1,0:T(8,128)(2,1)} %queries.9, bf16[1024,2048]{1,0:T(8,128)(2,1)} %grads.9, ...), custom_call_target="tpu_custom_call", output_to_operand_aliasing={{0}: (6, {})} | custom-call | flops 1342177280 | bytes 5767168 | tf_op jit(solution)/shard_map/attend/pallas_call | solution.py:268
  168.3 1.4 collective-permute-start.7
  169.7 10.3 %collective-permute-done.1.received = bf16[256,512]{1,0:T(8,128)(2,1)S(1)} collective-permute-done((bf16[256,512]{1,0:T(8,128)(2,1)S(1)}, bf16[256,512]{1,0:T(8,128)(2,1)S(1)}, u32[]{:S(2)}, u32[]{:S(2)}) %collective-permute-start.1) | collective-permute-done | bytes 262176 | tf_op jit(solution)/shard_map/ppermute | solution.py:441
  180.0 3.2 %attend.7 = (bf16[1024,2048]{1,0:T(8,128)(2,1)}, bf16[256,512]{1,0:T(8,128)(2,1)S(1)}) custom-call(s32[1]{0:T(128)S(6)} %copy.95.live, f32[256,1]{1,0:T(8,128)S(1)} %reshape.115._.usable, bf16[1024,2048]{1,0:T(8,128)(2,1)S(1)} %copy-done.2, bf16[1024,2048]{1,0:T(8,128)(2,1)} %grads.9, ...), custom_call_target="tpu_custom_call", output_to_operand_aliasing={{0}: (6, {})} | custom-call | flops 671088640 | bytes 2883584 | tf_op jit(solution)/shard_map/attend/pallas_call | solution.py:268
  183.2 1.5 collective-permute-start.8
  184.7 13.3 %all-gather.3.cloned.1.call-done.weights.refs_1_.refs_3_ = bf16[2048,1536]{1,0:T(8,128)(2,1)} async-done(((bf16[256,1536]{1,0:T(8,128)(2,1)}), bf16[2048,1536]{1,0:T(8,128)(2,1)}) %all-gather.3.cloned.1.call-update) | async-done | bytes 6291472 | tf_op jit(solution)/shard_map/all_gather | solution.py:416
  197.9 4.7 %project.9 = (f32[256,1024]{1,0:T(8,128)S(1)}, bf16[256,1024]{1,0:T(8,128)(2,1)S(1)}) custom-call(bf16[512,2048]{1,0:T(8,128)(2,1)S(1)} %arrange.1.rows, bf16[2048,1536]{1,0:T(8,128)(2,1)} %all-gather.3.cloned.1.call-done.weights.refs_1_.refs_3_, bf16[256,512]{1,0:T(8,128)(2,1)S(1)} %get-tuple-element.39.rest_0_.refs_6_), custom_call_target="tpu_custom_call" | custom-call | flops 2147483648 | bytes 7864320 | tf_op jit(solution)/shard_map/project/pallas_call | solution.py:183
  202.7 1.5 collective-permute-start.6
  204.2 2.7 project.8
  206.9 0.6 collective-permute-start.5
  207.6 9.5 %spread.5 = (bf16[4,2,2,256,256]{4,3,2,1,0:T(8,128)(2,1)S(1)}, f32[8,128]{1,0:T(8,128)S(1)}) custom-call(s32[4]{0:T(128)S(1)} %pad_add_fusion.pos, bf16[256,1024]{1,0:T(8,128)(2,1)S(1)} %copy-done.5, bf16[256,1024]{1,0:T(8,128)(2,1)S(1)} %collective-permute-done.4.rest_1_.refs_1_, ...), custom_call_target="tpu_custom_call" | custom-call | flops 5368709120 | bytes 18874368 | tf_op jit(solution)/shard_map/spread/pallas_call | solution.py:358
  217.5 5.0 %attend.8 = (bf16[1024,2048]{1,0:T(8,128)(2,1)}, bf16[256,1024]{1,0:T(8,128)(2,1)S(1)}) custom-call(s32[1]{0:T(128)S(6)} %copy.95.live, f32[256,1]{1,0:T(8,128)S(1)} %reshape.115._.usable, bf16[1024,2048]{1,0:T(8,128)(2,1)} %queries.9, bf16[1024,2048]{1,0:T(8,128)(2,1)} %grads.9, ...), custom_call_target="tpu_custom_call", output_to_operand_aliasing={{0}: (6, {})} | custom-call | flops 1342177280 | bytes 5767168 | tf_op jit(solution)/shard_map/attend/pallas_call | solution.py:268
  222.5 3.2 %attend.9 = (bf16[1024,2048]{1,0:T(8,128)(2,1)}, bf16[256,512]{1,0:T(8,128)(2,1)S(1)}) custom-call(s32[1]{0:T(128)S(6)} %copy.95.live, f32[256,1]{1,0:T(8,128)S(1)} %reshape.115._.usable, bf16[1024,2048]{1,0:T(8,128)(2,1)S(1)} %copy-done.3, bf16[1024,2048]{1,0:T(8,128)(2,1)} %grads.9, ...), custom_call_target="tpu_custom_call", output_to_operand_aliasing={{0}: (6, {})} | custom-call | flops 671088640 | bytes 2883584 | tf_op jit(solution)/shard_map/attend/pallas_call | solution.py:268
  225.6 3.2 %spread.6 = (bf16[2,2,1,256,256]{4,3,2,1,0:T(8,128)(2,1)S(1)}, f32[8,128]{1,0:T(8,128)S(1)}) custom-call(s32[4]{0:T(128)S(1)} %pad_add_fusion.pos, bf16[256,1024]{1,0:T(8,128)(2,1)S(1)} %get-tuple-element.49.refs_0_, bf16[2048,1536]{1,0:T(8,128)(2,1)} %all-gather.3.cloned.1.call-done.weights.refs_1_.refs_3_, bf16[256,512]{1,0:T(8,128)(2,1)S(1)} %get-tuple-element.50.refs_2_, ...), custom_call_target="tpu_custom_call" | custom-call | flops 805306368 | bytes 5242880 | tf_op jit(solution)/shard_map/spread/pallas_call | solution.py:358
  228.9 1.5 collective-permute-start.9
  230.4 1.5 collective-permute-start.10
  232.5 3.6 %spread.7 = (f32[2,2,1,256,256]{4,3,2,1,0:T(8,128)S(1)}, f32[8,128]{1,0:T(8,128)}) custom-call(s32[4]{0:T(128)S(1)} %pad_add_fusion.pos, bf16[256,1024]{1,0:T(8,128)(2,1)S(1)} %get-tuple-element.49.refs_0_, bf16[2048,1536]{1,0:T(8,128)(2,1)} %all-gather.3.cloned.1.call-done.weights.refs_1_.refs_3_, bf16[256,512]{1,0:T(8,128)(2,1)S(1)} %get-tuple-element.50.refs_2_, ...), custom_call_target="tpu_custom_call" | custom-call | flops 805306368 | bytes 5242880 | tf_op jit(solution)/shard_map/spread/pallas_call | solution.py:358
  236.0 6.1 %collective-permute-done.9 = bf16[2,2,1,256,256]{4,3,2,1,0:T(8,128)(2,1)S(1)} collective-permute-done((bf16[2,2,1,256,256]{4,3,2,1,0:T(8,128)(2,1)S(1)}, bf16[2,2,1,256,256]{4,3,2,1,0:T(8,128)(2,1)S(1)}, u32[]{:S(2)}, u32[]{:S(2)}) %collective-permute-start.9) | collective-permute-done | bytes 524320 | tf_op jit(solution)/shard_map/ppermute | solution.py:403
  242.3 0.9 copy.67
  243.2 4.3 %all-to-all-start.2 = ((bf16[16,64,256]{2,1,0:T(8,128)(2,1)}), bf16[16,64,256]{2,1,0:T(8,128)(2,1)}, u32[]{:S(2)}, u32[]{:S(2)}) async-start(bf16[16,64,256]{2,1,0:T(8,128)(2,1)} %bitcast.51), calls=%async_computation.2 | async-start | bytes 1048576 | tf_op jit(solution)/shard_map/all_to_all | solution.py:486
  247.5 1.6 collective-permute-done.11.refs_2_
  249.1 3.3 %spread.8 = (bf16[2,2,1,256,256]{4,3,2,1,0:T(8,128)(2,1)S(1)}, f32[8,128]{1,0:T(8,128)S(1)}) custom-call(s32[4]{0:T(128)S(1)} %pad_add_fusion.pos, bf16[256,1024]{1,0:T(8,128)(2,1)S(1)} %collective-permute-done.10.refs_0_, bf16[2048,1536]{1,0:T(8,128)(2,1)} %all-gather.3.cloned.1.call-done.weights.refs_1_.refs_3_, ...), custom_call_target="tpu_custom_call" | custom-call | flops 805306368 | bytes 5242880 | tf_op jit(solution)/shard_map/spread/pallas_call | solution.py:358
  253.0 3.7 %spread.9 = (f32[2,2,1,256,256]{4,3,2,1,0:T(8,128)S(1)}, f32[8,128]{1,0:T(8,128)}) custom-call(s32[4]{0:T(128)S(1)} %pad_add_fusion.pos, bf16[256,1024]{1,0:T(8,128)(2,1)S(1)} %collective-permute-done.10.refs_0_, bf16[2048,1536]{1,0:T(8,128)(2,1)} %all-gather.3.cloned.1.call-done.weights.refs_1_.refs_3_, bf16[256,512]{1,0:T(8,128)(2,1)} %collective-permute-done.11.refs_2_, ...), custom_call_target="tpu_custom_call" | custom-call | flops 805306368 | bytes 5242880 | tf_op jit(solution)/shard_map/spread/pallas_call | solution.py:358
  256.7 8.2 %collective-permute-done.12 = bf16[2,2,1,256,256]{4,3,2,1,0:T(8,128)(2,1)S(1)} collective-permute-done((bf16[2,2,1,256,256]{4,3,2,1,0:T(8,128)(2,1)S(1)}, bf16[2,2,1,256,256]{4,3,2,1,0:T(8,128)(2,1)S(1)}, u32[]{:S(2)}, u32[]{:S(2)}) %collective-permute-start.12) | collective-permute-done | bytes 524320 | tf_op jit(solution)/shard_map/ppermute | solution.py:403
  265.1 0.9 copy.69
  266.0 5.8 %all-to-all-start.3 = ((bf16[16,64,256]{2,1,0:T(8,128)(2,1)}), bf16[16,64,256]{2,1,0:T(8,128)(2,1)S(1)}, u32[]{:S(2)}, u32[]{:S(2)}) async-start(bf16[16,64,256]{2,1,0:T(8,128)(2,1)} %bitcast.19), calls=%async_computation.3 | async-start | bytes 1048576 | tf_op jit(solution)/shard_map/all_to_all | solution.py:486
  272.0 1.5 fusion.4
  273.5 12.8 %all-to-all-done.3 = bf16[16,64,256]{2,1,0:T(8,128)(2,1)S(1)} async-done(((bf16[16,64,256]{2,1,0:T(8,128)(2,1)}), bf16[16,64,256]{2,1,0:T(8,128)(2,1)S(1)}, u32[]{:S(2)}, u32[]{:S(2)}) %all-to-all-start.3) | async-done | bytes 524320 | tf_op jit(solution)/shard_map/all_to_all | solution.py:486
  286.8 1.0 copy.72
  (51 shorter events, 4.8 us)
Async XLA Ops:
  7.2 3.7 %copy-start = (bf16[128,2048]{1,0:T(8,128)(2,1)S(1)}, bf16[128,2048]{1,0:T(8,128)(2,1)}, u32[]{:S(2)}) copy-start(bf16[128,2048]{1,0:T(8,128)(2,1)} %param.10) | copy-start | bytes 1572868
  7.2 3.3 %copy-start.7 = (s32[128,1]{0,1:T(1,128)S(1)}, s32[128,1]{0,1:T(1,128)}, u32[]{:S(2)}) copy-start(s32[128,1]{0,1:T(1,128)} %param.11) | copy-start | bytes 1540
  7.2 125.2 %all-gather.5.cloned.1.call-start = ((), (), s32[]{:S(2)}) async-start(), calls=%async_computation.5 | async-start | bytes 11796480 | tf_op jit(solution)/shard_map/all_gather | solution.py:416
  10.4 187.5 %all-gather.3.cloned.1.call-start = ((), (), s32[]{:S(2)}) async-start(), calls=%async_computation.4 | async-start | bytes 7077888 | tf_op jit(solution)/shard_map/all_gather | solution.py:416
  62.7 3.4 %copy-start.6 = (bf16[16,128,256]{2,1,0:T(8,128)(2,1)S(1)}, bf16[16,128,256]{2,1,0:T(8,128)(2,1)}, u32[]{:S(2)}) copy-start(bf16[16,128,256]{2,1,0:T(8,128)(2,1)} %all_to_all.25.rest_1_) | copy-start | bytes 3145732
  66.2 23.9 %collective-permute-start = (bf16[2,2,2,256,256]{4,3,2,1,0:T(8,128)(2,1)S(1)}, bf16[2,2,2,256,256]{4,3,2,1,0:T(8,128)(2,1)S(1)}, u32[]{:S(2)}, u32[]{:S(2)}) collective-permute-start(bf16[2,2,2,256,256]{4,3,2,1,0:T(8,128)(2,1)S(1)} %bitcast.49), channel_id=1, source_target_pairs={{0,1},{1,0},{2,3},{3,2},{4,5},{5,4},{6,7},{7,6},{8,9},{9,8},{10,11... | collective-permute-start | bytes 3145736 | tf_op jit(solution)/shard_map/ppermute | solution.py:403
  68.6 21.3 %all-to-all-start = ((bf16[16,16,1]{1,2,0:T(2,128)(2,1)}), bf16[16,16,1]{1,2,0:T(2,128)(2,1)S(1)}, u32[]{:S(2)}, u32[]{:S(2)}) async-start(bf16[16,16,1]{1,2,0:T(2,128)(2,1)} %all_to_all.20), calls=%async_computation | async-start | bytes 16384 | tf_op jit(solution)/shard_map/all_to_all | solution.py:420
  137.1 14.8 %collective-permute-start.3 = (bf16[256,1024]{1,0:T(8,128)(2,1)S(1)}, bf16[256,1024]{1,0:T(8,128)(2,1)S(1)}, u32[]{:S(2)}, u32[]{:S(2)}) collective-permute-start(bf16[256,1024]{1,0:T(8,128)(2,1)S(1)} %get-tuple-element.35), channel_id=1, source_target_pairs={{0,4},{2,6},{4,0},{6,2},{8,12},{10,14},{12,8},{14,10},{16,20},{18,... | collective-permute-start | bytes 1572872 | tf_op jit(solution)/shard_map/ppermute | solution.py:441
  143.8 19.4 %collective-permute-start.2 = (bf16[256,1024]{1,0:T(8,128)(2,1)S(1)}, bf16[256,1024]{1,0:T(8,128)(2,1)S(1)}, u32[]{:S(2)}, u32[]{:S(2)}) collective-permute-start(bf16[256,1024]{1,0:T(8,128)(2,1)S(1)} %get-tuple-element.33), channel_id=1, source_target_pairs={{0,4},{2,6},{4,0},{6,2},{8,12},{10,14},{12,8},{14,10},{16,20},{18,... | collective-permute-start | bytes 1572872 | tf_op jit(solution)/shard_map/ppermute | solution.py:441
  156.8 4.2 %copy-start.4 = (bf16[256,1024]{1,0:T(8,128)(2,1)}, bf16[256,1024]{1,0:T(8,128)(2,1)S(1)}, u32[]{:S(2)}) copy-start(bf16[256,1024]{1,0:T(8,128)(2,1)S(1)} %get-tuple-element.38.refs_0_) | copy-start | bytes 1572868
  156.8 23.3 %collective-permute-start.4 = (bf16[256,1024]{1,0:T(8,128)(2,1)S(1)}, bf16[256,1024]{1,0:T(8,128)(2,1)S(1)}, u32[]{:S(2)}, u32[]{:S(2)}) collective-permute-start(bf16[256,1024]{1,0:T(8,128)(2,1)S(1)} %get-tuple-element.38.refs_0_), channel_id=1, source_target_pairs={{0,4},{2,6},{4,0},{6,2},{8,12},{10,14},{12,8},{14,10},{16,20},{18,... | collective-permute-start | bytes 1572872 | tf_op jit(solution)/shard_map/ppermute | solution.py:456
  161.0 19.1 %collective-permute-start.1 = (bf16[256,512]{1,0:T(8,128)(2,1)S(1)}, bf16[256,512]{1,0:T(8,128)(2,1)S(1)}, u32[]{:S(2)}, u32[]{:S(2)}) collective-permute-start(bf16[256,512]{1,0:T(8,128)(2,1)S(1)} %get-tuple-element.31), channel_id=1, source_target_pairs={{0,4},{2,6},{4,0},{6,2},{8,12},{10,14},{12,8},{14,10},{16,20},{18,... | collective-permute-start | bytes 786440 | tf_op jit(solution)/shard_map/ppermute | solution.py:441
  163.2 16.9 %copy-start.2 = (bf16[1024,2048]{1,0:T(8,128)(2,1)S(1)}, bf16[1024,2048]{1,0:T(8,128)(2,1)}, u32[]{:S(2)}) copy-start(bf16[1024,2048]{1,0:T(8,128)(2,1)} %queries.9) | copy-start | bytes 12582916
  168.3 39.3 %collective-permute-start.7 = (bf16[256,1024]{1,0:T(8,128)(2,1)}, bf16[256,1024]{1,0:T(8,128)(2,1)S(1)}, u32[]{:S(2)}, u32[]{:S(2)}) collective-permute-start(bf16[256,1024]{1,0:T(8,128)(2,1)} %get-tuple-element.45.refs_3_), channel_id=1, source_target_pairs={{0,4},{2,6},{4,0},{6,2},{8,12},{10,14},{12,8},{14,10},{16,20},{18,... | collective-permute-start | bytes 1572872 | tf_op jit(solution)/shard_map/ppermute | solution.py:456
  183.2 24.4 %collective-permute-start.8 = (bf16[256,512]{1,0:T(8,128)(2,1)S(1)}, bf16[256,512]{1,0:T(8,128)(2,1)}, u32[]{:S(2)}, u32[]{:S(2)}) collective-permute-start(bf16[256,512]{1,0:T(8,128)(2,1)S(1)} %get-tuple-element.39.rest_0_.refs_6_), channel_id=1, source_target_pairs={{0,4},{2,6},{4,0},{6,2},{8,12},{10,14},{12,8},{14,10},{16,20},{18,... | collective-permute-start | bytes 786440 | tf_op jit(solution)/shard_map/ppermute | solution.py:456
  202.7 4.9 %copy-start.5 = (bf16[256,1024]{1,0:T(8,128)(2,1)S(1)}, bf16[256,1024]{1,0:T(8,128)(2,1)}, u32[]{:S(2)}) copy-start(bf16[256,1024]{1,0:T(8,128)(2,1)} %copy-done.4) | copy-start | bytes 1572868
  202.7 14.8 %collective-permute-start.6 = (bf16[256,1024]{1,0:T(8,128)(2,1)S(1)}, bf16[256,1024]{1,0:T(8,128)(2,1)S(1)}, u32[]{:S(2)}, u32[]{:S(2)}) collective-permute-start(bf16[256,1024]{1,0:T(8,128)(2,1)S(1)} %get-tuple-element.43), channel_id=1, source_target_pairs={{0,4},{2,6},{4,0},{6,2},{8,12},{10,14},{12,8},{14,10},{16,20},{18,... | collective-permute-start | bytes 1572872 | tf_op jit(solution)/shard_map/ppermute | solution.py:441
  206.9 15.5 %collective-permute-start.5 = (bf16[256,512]{1,0:T(8,128)(2,1)S(1)}, bf16[256,512]{1,0:T(8,128)(2,1)S(1)}, u32[]{:S(2)}, u32[]{:S(2)}) collective-permute-start(bf16[256,512]{1,0:T(8,128)(2,1)S(1)} %get-tuple-element.41), channel_id=1, source_target_pairs={{0,4},{2,6},{4,0},{6,2},{8,12},{10,14},{12,8},{14,10},{16,20},{18,... | collective-permute-start | bytes 786440 | tf_op jit(solution)/shard_map/ppermute | solution.py:441
  217.5 5.0 %copy-start.3 = (bf16[1024,2048]{1,0:T(8,128)(2,1)S(1)}, bf16[1024,2048]{1,0:T(8,128)(2,1)}, u32[]{:S(2)}) copy-start(bf16[1024,2048]{1,0:T(8,128)(2,1)} %queries.9) | copy-start | bytes 12582916
  228.9 13.3 %collective-permute-start.9 = (bf16[2,2,1,256,256]{4,3,2,1,0:T(8,128)(2,1)S(1)}, bf16[2,2,1,256,256]{4,3,2,1,0:T(8,128)(2,1)S(1)}, u32[]{:S(2)}, u32[]{:S(2)}) collective-permute-start(bf16[2,2,1,256,256]{4,3,2,1,0:T(8,128)(2,1)S(1)} %get-tuple-element.54), channel_id=1, source_target_pairs={{0,1},{1,0},{2,3},{3,2},{4,5},{5,4},{6,7},{7,6},{8,9},{9,8},{10,11... | collective-permute-start | bytes 1572872 | tf_op jit(solution)/shard_map/ppermute | solution.py:403
  230.4 18.7 %collective-permute-start.10 = (bf16[256,1024]{1,0:T(8,128)(2,1)S(1)}, bf16[256,1024]{1,0:T(8,128)(2,1)S(1)}, u32[]{:S(2)}, u32[]{:S(2)}) collective-permute-start(bf16[256,1024]{1,0:T(8,128)(2,1)S(1)} %get-tuple-element.49.refs_0_), channel_id=1, source_target_pairs={{0,4},{2,6},{4,0},{6,2},{8,12},{10,14},{12,8},{14,10},{16,20},{18,... | collective-permute-start | bytes 1572872 | tf_op jit(solution)/shard_map/ppermute | solution.py:456
  231.9 17.2 %collective-permute-start.11 = (bf16[256,512]{1,0:T(8,128)(2,1)S(1)}, bf16[256,512]{1,0:T(8,128)(2,1)}, u32[]{:S(2)}, u32[]{:S(2)}) collective-permute-start(bf16[256,512]{1,0:T(8,128)(2,1)S(1)} %get-tuple-element.50.refs_2_), channel_id=1, source_target_pairs={{0,4},{2,6},{4,0},{6,2},{8,12},{10,14},{12,8},{14,10},{16,20},{18,... | collective-permute-start | bytes 786440 | tf_op jit(solution)/shard_map/ppermute | solution.py:456
  243.2 22.8 %all-to-all-start.2 = ((bf16[16,64,256]{2,1,0:T(8,128)(2,1)}), bf16[16,64,256]{2,1,0:T(8,128)(2,1)}, u32[]{:S(2)}, u32[]{:S(2)}) async-start(bf16[16,64,256]{2,1,0:T(8,128)(2,1)} %bitcast.51), calls=%async_computation.2 | async-start | bytes 1048576 | tf_op jit(solution)/shard_map/all_to_all | solution.py:486
  252.4 12.5 %collective-permute-start.12 = (bf16[2,2,1,256,256]{4,3,2,1,0:T(8,128)(2,1)S(1)}, bf16[2,2,1,256,256]{4,3,2,1,0:T(8,128)(2,1)S(1)}, u32[]{:S(2)}, u32[]{:S(2)}) collective-permute-start(bf16[2,2,1,256,256]{4,3,2,1,0:T(8,128)(2,1)S(1)} %get-tuple-element.57), channel_id=1, source_target_pairs={{0,1},{1,0},{2,3},{3,2},{4,5},{5,4},{6,7},{7,6},{8,9},{9,8},{10,11... | collective-permute-start | bytes 1572872 | tf_op jit(solution)/shard_map/ppermute | solution.py:403
  266.0 20.3 %all-to-all-start.3 = ((bf16[16,64,256]{2,1,0:T(8,128)(2,1)}), bf16[16,64,256]{2,1,0:T(8,128)(2,1)S(1)}, u32[]{:S(2)}, u32[]{:S(2)}) async-start(bf16[16,64,256]{2,1,0:T(8,128)(2,1)} %bitcast.19), calls=%async_computation.3 | async-start | bytes 1048576 | tf_op jit(solution)/shard_map/all_to_all | solution.py:486
  271.9 15.9 %copy-start.1 = (bf16[128,2048]{1,0:T(8,128)(2,1)S(1)}, bf16[128,2048]{1,0:T(8,128)(2,1)}, u32[]{:S(2)}) copy-start(bf16[128,2048]{1,0:T(8,128)(2,1)} %param.10) | copy-start | bytes 1572868
Sparse Core Ops, SparseCore 0:
  10.5 121.8 all-gather.4
  134.0 63.8 all-gather.2

commit v6 on v5

--- a/solution.py
+++ b/solution.py
@@ -451,7 +451,6 @@
                 first + column // (2 * HD),
                 query_grad,
                 *((done,) if final else ()),
-                *exchanged[-2:-1],
             )
             exchanged.append(lax.ppermute(pair_grad, "dp", x_swap))
             units.append((pair_grad, exchanged[-1], weights, column))

time: 296 us -> 296 us (level)
    ppermute x5, waiting for transfers between devices: 19.5 us -> 9.26 us  [on_device(): products.append((column, mine, lax.ppermute(other, 'dp', x_swap)))]
    all_gather x2, waiting for transfers between devices: 54.5 us -> 64.3 us  [on_device(): lax.all_gather(block, 'dp', axis=0, tiled=True, axis_index_groups=columns)]
  transfers between devices with their start and end apart: 18 -> 18, of which waited for: 11 -> 10; matrix products, arithmetic and copies ran while one was open for 2% -> 2% of each run, Pallas kernels for 21% -> 21%
where the time goes in v6:
time: 296 us; the launch traced here: 295 us
  waiting for transfers between devices  109 us (37%)
  Pallas kernels  72 us (24%)
  blocking collectives  50.3 us (17%)
  starting transfers between devices  40.1 us (14%)
  between operations  15 us (5%)
  local copies, waits for them, and re-layouts  4.77 us (2%)
    all_gather x2, waiting for transfers between devices, on_device(): lax.all_gather(block, 'dp', axis=0, tiled=True, axis_index_groups=columns)  64.3 us
    all_to_all x1, blocking collectives, on_device(): lax.all_to_all(outgoing, 'dp', split_axis=0, concat_axis=0, tiled=True)  50.3 us
    pallas_call x5, Pallas kernels, spread(): pl.pallas_call(functools.partial(spread_kernel, parts=len(units), sides=s...  23.5 us
    pallas_call x5, Pallas kernels, attend(): pl.pallas_call(functools.partial(attend_kernel, block), grid=(heads,), in...  21.1 us
    pallas_call x5, Pallas kernels, project(): pl.pallas_call(project_kernel, grid=(width // HD,), in_specs=[pl.BlockSpe...  20.1 us
    all_to_all x1, starting transfers between devices, on_device(): lax.all_to_all(filled, 'dp', split_axis=0, concat_axis=0, tiled=True)  14.9 us
    ppermute x3, waiting for transfers between devices, tensor_shift(): return lax.ppermute(value, 'tensor', pairs)  14.4 us
    all_to_all x2, waiting for transfers between devices, send_home(): lax.all_to_all(kept, 'dp', split_axis=0, concat_axis=0, tiled=True)  12.8 us
  transfers between devices with their start and end apart: 18, of which 10 were waited for; matrix products, arithmetic and copies ran while one was open for 2% of the time, Pallas kernels for 21%

profile of v6, /device:TPU:0, one launch (start us, length us, event | category | flops | bytes accessed | tf_op | source)
XLA Modules:
  0.0 294.7 jit_solution(10839625819376888343)
XLA Ops:
  7.2 3.1 %predict_first.1.rest_0_ = bf16[256,2560]{1,0:T(8,128)(2,1)} custom-call(bf16[2,256,2048]{2,1,0:T(8,128)(2,1)} %weights.3, f32[2,256,2048]{2,1,0:T(8,128)} %velocity.3), custom_call_target="tpu_custom_call" | custom-call | flops 655360 | bytes 5242880 | tf_op jit(solution)/shard_map/predict_first/pallas_call | solution.py:101
  11.3 0.8 reshape.99
  12.4 50.3 %all_to_all.25.rest_1_ = bf16[16,128,256]{2,1,0:T(8,128)(2,1)} all-to-all(bf16[16,128,256]{2,1,0:T(8,128)(2,1)S(1)} %bitcast.48), channel_id=1, replica_groups=mesh['dp'=16,'tensor'=2] {'dp'}, dimensions={0} | all-to-all | bytes 2097152 | tf_op jit(solution)/shard_map/all_to_all | solution.py:411
  62.7 3.5 %predict.1 = bf16[256,1536]{1,0:T(8,128)(2,1)} custom-call(bf16[2,256,2048]{2,1,0:T(8,128)(2,1)} %weights.3, f32[2,256,2048]{2,1,0:T(8,128)} %velocity.3, bf16[256,2560]{1,0:T(8,128)(2,1)} %predict_first.1.rest_0_, bf16[16,128,256]{2,1,0:T(8,128)(2,1)} %all_to_all.25.rest_1_), custom_call_target="tpu_custom_call" | custom-call | flops 393216 | bytes 3145728 | tf_op jit(solution)/shard_map/predict/pallas_call | solution.py:125
  66.3 1.6 collective-permute-start
  68.0 0.7 all_to_all.20
  68.7 14.9 %all-to-all-start = ((bf16[16,16,1]{1,2,0:T(2,128)(2,1)}), bf16[16,16,1]{1,2,0:T(2,128)(2,1)S(1)}, u32[]{:S(2)}, u32[]{:S(2)}) async-start(bf16[16,16,1]{1,2,0:T(2,128)(2,1)} %all_to_all.20), calls=%async_computation | async-start | bytes 16384 | tf_op jit(solution)/shard_map/all_to_all | solution.py:420
  83.7 6.4 %all-to-all-done = bf16[16,16,1]{1,2,0:T(2,128)(2,1)S(1)} async-done(((bf16[16,16,1]{1,2,0:T(2,128)(2,1)}), bf16[16,16,1]{1,2,0:T(2,128)(2,1)S(1)}, u32[]{:S(2)}, u32[]{:S(2)}) %all-to-all-start) | async-done | bytes 544 | tf_op jit(solution)/shard_map/all_to_all | solution.py:420
  90.4 0.8 arrange.1.rows
  91.2 41.2 %all-gather.5.cloned.1.call-done.weights.refs_2_.refs_5_.refs_8_ = bf16[2048,2560]{1,0:T(8,128)(2,1)} async-done(((bf16[256,2560]{1,0:T(8,128)(2,1)}), bf16[2048,2560]{1,0:T(8,128)(2,1)}) %all-gather.5.cloned.1.call-update) | async-done | bytes 10485776 | tf_op jit(solution)/shard_map/all_gather | solution.py:416
  132.4 4.7 %project.7 = (f32[256,1024]{1,0:T(8,128)S(1)}, bf16[256,1024]{1,0:T(8,128)(2,1)S(1)}) custom-call(bf16[512,2048]{1,0:T(8,128)(2,1)S(1)} %arrange.1.rows, bf16[2048,2560]{1,0:T(8,128)(2,1)} %all-gather.5.cloned.1.call-done.weights.refs_2_.refs_5_.refs_8_), custom_call_target="tpu_custom_call" | custom-call | flops 2147483648 | bytes 7864320 | tf_op jit(solution)/shard_map/project/pallas_call | solution.py:183
  137.1 1.5 collective-permute-start.3
  138.7 5.2 %project.6 = (f32[256,1024]{1,0:T(8,128)S(1)}, bf16[256,1024]{1,0:T(8,128)(2,1)S(1)}) custom-call(bf16[512,2048]{1,0:T(8,128)(2,1)S(1)} %arrange.1.rows, bf16[2048,2560]{1,0:T(8,128)(2,1)} %all-gather.5.cloned.1.call-done.weights.refs_2_.refs_5_.refs_8_), custom_call_target="tpu_custom_call" | custom-call | flops 2147483648 | bytes 7864320 | tf_op jit(solution)/shard_map/project/pallas_call | solution.py:183
  144.8 2.7 project.5
  147.5 1.8 collective-permute-start.1
  149.4 2.6 collective-permute-done.3.received
  151.9 4.8 %attend.5 = (bf16[1024,2048]{1,0:T(8,128)(2,1)}, bf16[256,1024]{1,0:T(8,128)(2,1)S(1)}) custom-call(s32[1]{0:T(128)S(6)} %copy.95.live, f32[256,1]{1,0:T(8,128)S(1)} %reshape.115._.usable, bf16[1024,2048]{1,0:T(8,128)(2,1)} %queries.9, bf16[1024,2048]{1,0:T(8,128)(2,1)} %grads.9, f32[256,1024]{1,0:T(8,128)S(1)} %get-tuple-element.34.mine, ...), custom_call_target="tpu_custom_call" | custom-call | flops 1342177280 | bytes 5767168 | tf_op jit(solution)/shard_map/attend/pallas_call | solution.py:268
  156.8 6.4 %collective-permute-done.2.received = bf16[256,1024]{1,0:T(8,128)(2,1)S(1)} collective-permute-done((bf16[256,1024]{1,0:T(8,128)(2,1)S(1)}, bf16[256,1024]{1,0:T(8,128)(2,1)S(1)}, u32[]{:S(2)}, u32[]{:S(2)}) %collective-permute-start.2) | collective-permute-done | bytes 524320 | tf_op jit(solution)/shard_map/ppermute | solution.py:441
  163.2 5.0 %attend.6 = (bf16[1024,2048]{1,0:T(8,128)(2,1)}, bf16[256,1024]{1,0:T(8,128)(2,1)S(1)}) custom-call(s32[1]{0:T(128)S(6)} %copy.95.live, f32[256,1]{1,0:T(8,128)S(1)} %reshape.115._.usable, bf16[1024,2048]{1,0:T(8,128)(2,1)} %queries.9, bf16[1024,2048]{1,0:T(8,128)(2,1)} %grads.9, ...), custom_call_target="tpu_custom_call", output_to_operand_aliasing={{0}: (6, {})} | custom-call | flops 1342177280 | bytes 5767168 | tf_op jit(solution)/shard_map/attend/pallas_call | solution.py:268
  168.2 1.5 collective-permute-start.7
  169.6 0.6 collective-permute-start.6
  170.2 3.2 %attend.7 = (bf16[1024,2048]{1,0:T(8,128)(2,1)}, bf16[256,512]{1,0:T(8,128)(2,1)S(1)}) custom-call(s32[1]{0:T(128)S(6)} %copy.95.live, f32[256,1]{1,0:T(8,128)S(1)} %reshape.115._.usable, bf16[1024,2048]{1,0:T(8,128)(2,1)S(1)} %copy-done.2, bf16[1024,2048]{1,0:T(8,128)(2,1)} %grads.9, ...), custom_call_target="tpu_custom_call", output_to_operand_aliasing={{0}: (6, {})} | custom-call | flops 671088640 | bytes 2883584 | tf_op jit(solution)/shard_map/attend/pallas_call | solution.py:268
  173.3 1.5 collective-permute-start.8
  174.8 23.1 %all-gather.3.cloned.1.call-done.weights.refs_1_.refs_3_ = bf16[2048,1536]{1,0:T(8,128)(2,1)} async-done(((bf16[256,1536]{1,0:T(8,128)(2,1)}), bf16[2048,1536]{1,0:T(8,128)(2,1)}) %all-gather.3.cloned.1.call-update) | async-done | bytes 6291472 | tf_op jit(solution)/shard_map/all_gather | solution.py:416
  197.9 4.7 %project.9 = (f32[256,1024]{1,0:T(8,128)S(1)}, bf16[256,1024]{1,0:T(8,128)(2,1)S(1)}) custom-call(bf16[512,2048]{1,0:T(8,128)(2,1)S(1)} %arrange.1.rows, bf16[2048,1536]{1,0:T(8,128)(2,1)} %all-gather.3.cloned.1.call-done.weights.refs_1_.refs_3_, bf16[256,512]{1,0:T(8,128)(2,1)S(1)} %get-tuple-element.38.rest_0_.refs_6_), custom_call_target="tpu_custom_call" | custom-call | flops 2147483648 | bytes 7864320 | tf_op jit(solution)/shard_map/project/pallas_call | solution.py:183
  202.7 1.5 collective-permute-start.5
  204.2 2.7 project.8
  206.9 0.6 collective-permute-start.4
  207.6 9.7 %spread.5 = (bf16[4,2,2,256,256]{4,3,2,1,0:T(8,128)(2,1)S(1)}, f32[8,128]{1,0:T(8,128)S(1)}) custom-call(s32[4]{0:T(128)S(1)} %pad_add_fusion.pos, bf16[256,1024]{1,0:T(8,128)(2,1)S(1)} %get-tuple-element.44.refs_0_, bf16[256,1024]{1,0:T(8,128)(2,1)} %collective-permute-done.6.refs_1_, ...), custom_call_target="tpu_custom_call" | custom-call | flops 5368709120 | bytes 18874368 | tf_op jit(solution)/shard_map/spread/pallas_call | solution.py:358
  217.5 5.0 %attend.8 = (bf16[1024,2048]{1,0:T(8,128)(2,1)}, bf16[256,1024]{1,0:T(8,128)(2,1)S(1)}) custom-call(s32[1]{0:T(128)S(6)} %copy.95.live, f32[256,1]{1,0:T(8,128)S(1)} %reshape.115._.usable, bf16[1024,2048]{1,0:T(8,128)(2,1)} %queries.9, bf16[1024,2048]{1,0:T(8,128)(2,1)} %grads.9, ...), custom_call_target="tpu_custom_call", output_to_operand_aliasing={{0}: (6, {})} | custom-call | flops 1342177280 | bytes 5767168 | tf_op jit(solution)/shard_map/attend/pallas_call | solution.py:268
  222.5 3.2 %attend.9 = (bf16[1024,2048]{1,0:T(8,128)(2,1)}, bf16[256,512]{1,0:T(8,128)(2,1)S(1)}) custom-call(s32[1]{0:T(128)S(6)} %copy.95.live, f32[256,1]{1,0:T(8,128)S(1)} %reshape.115._.usable, bf16[1024,2048]{1,0:T(8,128)(2,1)S(1)} %copy-done.3, bf16[1024,2048]{1,0:T(8,128)(2,1)} %grads.9, ...), custom_call_target="tpu_custom_call", output_to_operand_aliasing={{0}: (6, {})} | custom-call | flops 671088640 | bytes 2883584 | tf_op jit(solution)/shard_map/attend/pallas_call | solution.py:268
  225.6 3.2 %spread.6 = (bf16[2,2,1,256,256]{4,3,2,1,0:T(8,128)(2,1)S(1)}, f32[8,128]{1,0:T(8,128)S(1)}) custom-call(s32[4]{0:T(128)S(1)} %pad_add_fusion.pos, bf16[256,1024]{1,0:T(8,128)(2,1)S(1)} %get-tuple-element.49.refs_0_, bf16[2048,1536]{1,0:T(8,128)(2,1)} %all-gather.3.cloned.1.call-done.weights.refs_1_.refs_3_, bf16[256,512]{1,0:T(8,128)(2,1)S(1)} %get-tuple-element.50.refs_2_, ...), custom_call_target="tpu_custom_call" | custom-call | flops 805306368 | bytes 5242880 | tf_op jit(solution)/shard_map/spread/pallas_call | solution.py:358
  228.9 1.5 collective-permute-start.9
  230.4 1.5 collective-permute-start.10
  232.4 3.6 %spread.7 = (f32[2,2,1,256,256]{4,3,2,1,0:T(8,128)S(1)}, f32[8,128]{1,0:T(8,128)}) custom-call(s32[4]{0:T(128)S(1)} %pad_add_fusion.pos, bf16[256,1024]{1,0:T(8,128)(2,1)S(1)} %get-tuple-element.49.refs_0_, bf16[2048,1536]{1,0:T(8,128)(2,1)} %all-gather.3.cloned.1.call-done.weights.refs_1_.refs_3_, bf16[256,512]{1,0:T(8,128)(2,1)S(1)} %get-tuple-element.50.refs_2_, ...), custom_call_target="tpu_custom_call" | custom-call | flops 805306368 | bytes 5242880 | tf_op jit(solution)/shard_map/spread/pallas_call | solution.py:358
  236.0 6.2 %collective-permute-done.9 = bf16[2,2,1,256,256]{4,3,2,1,0:T(8,128)(2,1)S(1)} collective-permute-done((bf16[2,2,1,256,256]{4,3,2,1,0:T(8,128)(2,1)S(1)}, bf16[2,2,1,256,256]{4,3,2,1,0:T(8,128)(2,1)S(1)}, u32[]{:S(2)}, u32[]{:S(2)}) %collective-permute-start.9) | collective-permute-done | bytes 524320 | tf_op jit(solution)/shard_map/ppermute | solution.py:403
  242.4 0.9 copy.67
  243.3 4.2 %all-to-all-start.2 = ((bf16[16,64,256]{2,1,0:T(8,128)(2,1)}), bf16[16,64,256]{2,1,0:T(8,128)(2,1)}, u32[]{:S(2)}, u32[]{:S(2)}) async-start(bf16[16,64,256]{2,1,0:T(8,128)(2,1)} %bitcast.51), calls=%async_computation.2 | async-start | bytes 1048576 | tf_op jit(solution)/shard_map/all_to_all | solution.py:485
  247.5 1.6 collective-permute-done.11.refs_2_
  249.1 3.3 %spread.8 = (bf16[2,2,1,256,256]{4,3,2,1,0:T(8,128)(2,1)S(1)}, f32[8,128]{1,0:T(8,128)S(1)}) custom-call(s32[4]{0:T(128)S(1)} %pad_add_fusion.pos, bf16[256,1024]{1,0:T(8,128)(2,1)S(1)} %collective-permute-done.10.refs_0_, bf16[2048,1536]{1,0:T(8,128)(2,1)} %all-gather.3.cloned.1.call-done.weights.refs_1_.refs_3_, ...), custom_call_target="tpu_custom_call" | custom-call | flops 805306368 | bytes 5242880 | tf_op jit(solution)/shard_map/spread/pallas_call | solution.py:358
  252.5 0.6 collective-permute-start.12
  253.1 3.7 %spread.9 = (f32[2,2,1,256,256]{4,3,2,1,0:T(8,128)S(1)}, f32[8,128]{1,0:T(8,128)}) custom-call(s32[4]{0:T(128)S(1)} %pad_add_fusion.pos, bf16[256,1024]{1,0:T(8,128)(2,1)S(1)} %collective-permute-done.10.refs_0_, bf16[2048,1536]{1,0:T(8,128)(2,1)} %all-gather.3.cloned.1.call-done.weights.refs_1_.refs_3_, bf16[256,512]{1,0:T(8,128)(2,1)} %collective-permute-done.11.refs_2_, ...), custom_call_target="tpu_custom_call" | custom-call | flops 805306368 | bytes 5242880 | tf_op jit(solution)/shard_map/spread/pallas_call | solution.py:358
  256.8 8.2 %collective-permute-done.12 = bf16[2,2,1,256,256]{4,3,2,1,0:T(8,128)(2,1)S(1)} collective-permute-done((bf16[2,2,1,256,256]{4,3,2,1,0:T(8,128)(2,1)S(1)}, bf16[2,2,1,256,256]{4,3,2,1,0:T(8,128)(2,1)S(1)}, u32[]{:S(2)}, u32[]{:S(2)}) %collective-permute-start.12) | collective-permute-done | bytes 524320 | tf_op jit(solution)/shard_map/ppermute | solution.py:403
  265.2 0.9 copy.69
  266.0 5.8 %all-to-all-start.3 = ((bf16[16,64,256]{2,1,0:T(8,128)(2,1)}), bf16[16,64,256]{2,1,0:T(8,128)(2,1)S(1)}, u32[]{:S(2)}, u32[]{:S(2)}) async-start(bf16[16,64,256]{2,1,0:T(8,128)(2,1)} %bitcast.19), calls=%async_computation.3 | async-start | bytes 1048576 | tf_op jit(solution)/shard_map/all_to_all | solution.py:485
  272.0 1.5 fusion.4
  273.5 12.8 %all-to-all-done.3 = bf16[16,64,256]{2,1,0:T(8,128)(2,1)S(1)} async-done(((bf16[16,64,256]{2,1,0:T(8,128)(2,1)}), bf16[16,64,256]{2,1,0:T(8,128)(2,1)S(1)}, u32[]{:S(2)}, u32[]{:S(2)}) %all-to-all-start.3) | async-done | bytes 524320 | tf_op jit(solution)/shard_map/all_to_all | solution.py:485
  286.8 1.0 copy.72
  (47 shorter events, 4.0 us)
Async XLA Ops:
  7.2 3.7 %copy-start = (bf16[128,2048]{1,0:T(8,128)(2,1)S(1)}, bf16[128,2048]{1,0:T(8,128)(2,1)}, u32[]{:S(2)}) copy-start(bf16[128,2048]{1,0:T(8,128)(2,1)} %param.10) | copy-start | bytes 1572868
  7.2 3.3 %copy-start.5 = (s32[128,1]{0,1:T(1,128)S(1)}, s32[128,1]{0,1:T(1,128)}, u32[]{:S(2)}) copy-start(s32[128,1]{0,1:T(1,128)} %param.11) | copy-start | bytes 1540
  7.2 125.2 %all-gather.5.cloned.1.call-start = ((), (), s32[]{:S(2)}) async-start(), calls=%async_computation.5 | async-start | bytes 11796480 | tf_op jit(solution)/shard_map/all_gather | solution.py:416
  10.4 187.5 %all-gather.3.cloned.1.call-start = ((), (), s32[]{:S(2)}) async-start(), calls=%async_computation.4 | async-start | bytes 7077888 | tf_op jit(solution)/shard_map/all_gather | solution.py:416
  62.7 3.5 %copy-start.4 = (bf16[16,128,256]{2,1,0:T(8,128)(2,1)S(1)}, bf16[16,128,256]{2,1,0:T(8,128)(2,1)}, u32[]{:S(2)}) copy-start(bf16[16,128,256]{2,1,0:T(8,128)(2,1)} %all_to_all.25.rest_1_) | copy-start | bytes 3145732
  66.3 23.9 %collective-permute-start = (bf16[2,2,2,256,256]{4,3,2,1,0:T(8,128)(2,1)S(1)}, bf16[2,2,2,256,256]{4,3,2,1,0:T(8,128)(2,1)S(1)}, u32[]{:S(2)}, u32[]{:S(2)}) collective-permute-start(bf16[2,2,2,256,256]{4,3,2,1,0:T(8,128)(2,1)S(1)} %bitcast.49), channel_id=1, source_target_pairs={{0,1},{1,0},{2,3},{3,2},{4,5},{5,4},{6,7},{7,6},{8,9},{9,8},{10,11... | collective-permute-start | bytes 3145736 | tf_op jit(solution)/shard_map/ppermute | solution.py:403
  68.7 21.3 %all-to-all-start = ((bf16[16,16,1]{1,2,0:T(2,128)(2,1)}), bf16[16,16,1]{1,2,0:T(2,128)(2,1)S(1)}, u32[]{:S(2)}, u32[]{:S(2)}) async-start(bf16[16,16,1]{1,2,0:T(2,128)(2,1)} %all_to_all.20), calls=%async_computation | async-start | bytes 16384 | tf_op jit(solution)/shard_map/all_to_all | solution.py:420
  137.1 14.8 %collective-permute-start.3 = (bf16[256,1024]{1,0:T(8,128)(2,1)S(1)}, bf16[256,1024]{1,0:T(8,128)(2,1)S(1)}, u32[]{:S(2)}, u32[]{:S(2)}) collective-permute-start(bf16[256,1024]{1,0:T(8,128)(2,1)S(1)} %get-tuple-element.35), channel_id=1, source_target_pairs={{0,4},{2,6},{4,0},{6,2},{8,12},{10,14},{12,8},{14,10},{16,20},{18,... | collective-permute-start | bytes 1572872 | tf_op jit(solution)/shard_map/ppermute | solution.py:441
  143.8 19.4 %collective-permute-start.2 = (bf16[256,1024]{1,0:T(8,128)(2,1)S(1)}, bf16[256,1024]{1,0:T(8,128)(2,1)S(1)}, u32[]{:S(2)}, u32[]{:S(2)}) collective-permute-start(bf16[256,1024]{1,0:T(8,128)(2,1)S(1)} %get-tuple-element.33), channel_id=1, source_target_pairs={{0,4},{2,6},{4,0},{6,2},{8,12},{10,14},{12,8},{14,10},{16,20},{18,... | collective-permute-start | bytes 1572872 | tf_op jit(solution)/shard_map/ppermute | solution.py:441
  147.5 22.6 %collective-permute-start.1 = (bf16[256,512]{1,0:T(8,128)(2,1)S(1)}, bf16[256,512]{1,0:T(8,128)(2,1)S(1)}, u32[]{:S(2)}, u32[]{:S(2)}) collective-permute-start(bf16[256,512]{1,0:T(8,128)(2,1)S(1)} %get-tuple-element.31), channel_id=1, source_target_pairs={{0,4},{2,6},{4,0},{6,2},{8,12},{10,14},{12,8},{14,10},{16,20},{18,... | collective-permute-start | bytes 786440 | tf_op jit(solution)/shard_map/ppermute | solution.py:441
  163.2 7.0 %copy-start.2 = (bf16[1024,2048]{1,0:T(8,128)(2,1)S(1)}, bf16[1024,2048]{1,0:T(8,128)(2,1)}, u32[]{:S(2)}) copy-start(bf16[1024,2048]{1,0:T(8,128)(2,1)} %queries.9) | copy-start | bytes 12582916
  168.2 39.4 %collective-permute-start.7 = (bf16[256,1024]{1,0:T(8,128)(2,1)S(1)}, bf16[256,1024]{1,0:T(8,128)(2,1)}, u32[]{:S(2)}, u32[]{:S(2)}) collective-permute-start(bf16[256,1024]{1,0:T(8,128)(2,1)S(1)} %get-tuple-element.45.refs_3_), channel_id=1, source_target_pairs={{0,4},{2,6},{4,0},{6,2},{8,12},{10,14},{12,8},{14,10},{16,20},{18,... | collective-permute-start | bytes 1572872 | tf_op jit(solution)/shard_map/ppermute | solution.py:455
  169.6 38.0 %collective-permute-start.6 = (bf16[256,1024]{1,0:T(8,128)(2,1)S(1)}, bf16[256,1024]{1,0:T(8,128)(2,1)}, u32[]{:S(2)}, u32[]{:S(2)}) collective-permute-start(bf16[256,1024]{1,0:T(8,128)(2,1)S(1)} %get-tuple-element.44.refs_0_), channel_id=1, source_target_pairs={{0,4},{2,6},{4,0},{6,2},{8,12},{10,14},{12,8},{14,10},{16,20},{18,... | collective-permute-start | bytes 1572872 | tf_op jit(solution)/shard_map/ppermute | solution.py:455
  173.3 34.2 %collective-permute-start.8 = (bf16[256,512]{1,0:T(8,128)(2,1)S(1)}, bf16[256,512]{1,0:T(8,128)(2,1)}, u32[]{:S(2)}, u32[]{:S(2)}) collective-permute-start(bf16[256,512]{1,0:T(8,128)(2,1)S(1)} %get-tuple-element.38.rest_0_.refs_6_), channel_id=1, source_target_pairs={{0,4},{2,6},{4,0},{6,2},{8,12},{10,14},{12,8},{14,10},{16,20},{18,... | collective-permute-start | bytes 786440 | tf_op jit(solution)/shard_map/ppermute | solution.py:455
  202.7 14.8 %collective-permute-start.5 = (bf16[256,1024]{1,0:T(8,128)(2,1)S(1)}, bf16[256,1024]{1,0:T(8,128)(2,1)S(1)}, u32[]{:S(2)}, u32[]{:S(2)}) collective-permute-start(bf16[256,1024]{1,0:T(8,128)(2,1)S(1)} %get-tuple-element.42), channel_id=1, source_target_pairs={{0,4},{2,6},{4,0},{6,2},{8,12},{10,14},{12,8},{14,10},{16,20},{18,... | collective-permute-start | bytes 1572872 | tf_op jit(solution)/shard_map/ppermute | solution.py:441
  206.9 15.5 %collective-permute-start.4 = (bf16[256,512]{1,0:T(8,128)(2,1)S(1)}, bf16[256,512]{1,0:T(8,128)(2,1)S(1)}, u32[]{:S(2)}, u32[]{:S(2)}) collective-permute-start(bf16[256,512]{1,0:T(8,128)(2,1)S(1)} %get-tuple-element.40), channel_id=1, source_target_pairs={{0,4},{2,6},{4,0},{6,2},{8,12},{10,14},{12,8},{14,10},{16,20},{18,... | collective-permute-start | bytes 786440 | tf_op jit(solution)/shard_map/ppermute | solution.py:441
  217.5 5.0 %copy-start.3 = (bf16[1024,2048]{1,0:T(8,128)(2,1)S(1)}, bf16[1024,2048]{1,0:T(8,128)(2,1)}, u32[]{:S(2)}) copy-start(bf16[1024,2048]{1,0:T(8,128)(2,1)} %queries.9) | copy-start | bytes 12582916
  228.9 13.3 %collective-permute-start.9 = (bf16[2,2,1,256,256]{4,3,2,1,0:T(8,128)(2,1)S(1)}, bf16[2,2,1,256,256]{4,3,2,1,0:T(8,128)(2,1)S(1)}, u32[]{:S(2)}, u32[]{:S(2)}) collective-permute-start(bf16[2,2,1,256,256]{4,3,2,1,0:T(8,128)(2,1)S(1)} %get-tuple-element.54), channel_id=1, source_target_pairs={{0,1},{1,0},{2,3},{3,2},{4,5},{5,4},{6,7},{7,6},{8,9},{9,8},{10,11... | collective-permute-start | bytes 1572872 | tf_op jit(solution)/shard_map/ppermute | solution.py:403
  230.4 18.7 %collective-permute-start.10 = (bf16[256,1024]{1,0:T(8,128)(2,1)S(1)}, bf16[256,1024]{1,0:T(8,128)(2,1)S(1)}, u32[]{:S(2)}, u32[]{:S(2)}) collective-permute-start(bf16[256,1024]{1,0:T(8,128)(2,1)S(1)} %get-tuple-element.49.refs_0_), channel_id=1, source_target_pairs={{0,4},{2,6},{4,0},{6,2},{8,12},{10,14},{12,8},{14,10},{16,20},{18,... | collective-permute-start | bytes 1572872 | tf_op jit(solution)/shard_map/ppermute | solution.py:455
  231.9 17.2 %collective-permute-start.11 = (bf16[256,512]{1,0:T(8,128)(2,1)S(1)}, bf16[256,512]{1,0:T(8,128)(2,1)}, u32[]{:S(2)}, u32[]{:S(2)}) collective-permute-start(bf16[256,512]{1,0:T(8,128)(2,1)S(1)} %get-tuple-element.50.refs_2_), channel_id=1, source_target_pairs={{0,4},{2,6},{4,0},{6,2},{8,12},{10,14},{12,8},{14,10},{16,20},{18,... | collective-permute-start | bytes 786440 | tf_op jit(solution)/shard_map/ppermute | solution.py:455
  243.3 22.8 %all-to-all-start.2 = ((bf16[16,64,256]{2,1,0:T(8,128)(2,1)}), bf16[16,64,256]{2,1,0:T(8,128)(2,1)}, u32[]{:S(2)}, u32[]{:S(2)}) async-start(bf16[16,64,256]{2,1,0:T(8,128)(2,1)} %bitcast.51), calls=%async_computation.2 | async-start | bytes 1048576 | tf_op jit(solution)/shard_map/all_to_all | solution.py:485
  252.5 12.5 %collective-permute-start.12 = (bf16[2,2,1,256,256]{4,3,2,1,0:T(8,128)(2,1)S(1)}, bf16[2,2,1,256,256]{4,3,2,1,0:T(8,128)(2,1)S(1)}, u32[]{:S(2)}, u32[]{:S(2)}) collective-permute-start(bf16[2,2,1,256,256]{4,3,2,1,0:T(8,128)(2,1)S(1)} %get-tuple-element.57), channel_id=1, source_target_pairs={{0,1},{1,0},{2,3},{3,2},{4,5},{5,4},{6,7},{7,6},{8,9},{9,8},{10,11... | collective-permute-start | bytes 1572872 | tf_op jit(solution)/shard_map/ppermute | solution.py:403
  266.0 20.3 %all-to-all-start.3 = ((bf16[16,64,256]{2,1,0:T(8,128)(2,1)}), bf16[16,64,256]{2,1,0:T(8,128)(2,1)S(1)}, u32[]{:S(2)}, u32[]{:S(2)}) async-start(bf16[16,64,256]{2,1,0:T(8,128)(2,1)} %bitcast.19), calls=%async_computation.3 | async-start | bytes 1048576 | tf_op jit(solution)/shard_map/all_to_all | solution.py:485
  272.0 15.9 %copy-start.1 = (bf16[128,2048]{1,0:T(8,128)(2,1)S(1)}, bf16[128,2048]{1,0:T(8,128)(2,1)}, u32[]{:S(2)}) copy-start(bf16[128,2048]{1,0:T(8,128)(2,1)} %param.10) | copy-start | bytes 1572868
Sparse Core Ops, SparseCore 0:
  10.5 121.8 all-gather.4
  134.0 63.8 all-gather.2

commit v7 on v5

--- a/solution.py
+++ b/solution.py
@@ -434,12 +434,14 @@
                 pos, depth, units, None, (0, 1), 0, line, tensor_count, jnp.bfloat16
             )
             units = []
-        products, column = [], 0
+        spans, column = [], 0
         for heads in split_units(size):
-            width = 2 * HD * heads
+            spans.append((column, 2 * HD * heads))
+            column += 2 * HD * heads
+        products = []
+        for column, width in reversed(spans) if final else spans:
             mine, other = project(rows, weights, column, width, *token)
             products.append((column, mine, lax.ppermute(other, "dp", x_swap)))
-            column += width
         for column, mine, received in products:
             query_grad, pair_grad = attend(
                 target_len,

time: 296 us -> 296 us (level)
  no operation moved by 1% of the time
where the time goes in v7:
time: 296 us; the launch traced here: 295 us
  waiting for transfers between devices  109 us (37%)
  Pallas kernels  72 us (24%)
  blocking collectives  50.3 us (17%)
  starting transfers between devices  39.8 us (13%)
  between operations  15.1 us (5%)
  local copies, waits for them, and re-layouts  4.79 us (2%)
    all_gather x2, waiting for transfers between devices, on_device(): lax.all_gather(block, 'dp', axis=0, tiled=True, axis_index_groups=columns)  54.5 us
    all_to_all x1, blocking collectives, on_device(): lax.all_to_all(outgoing, 'dp', split_axis=0, concat_axis=0, tiled=True)  50.3 us
    pallas_call x5, Pallas kernels, spread(): pl.pallas_call(functools.partial(spread_kernel, parts=len(units), sides=s...  23.4 us
    pallas_call x5, Pallas kernels, attend(): pl.pallas_call(functools.partial(attend_kernel, block), grid=(heads,), in...  21.2 us
    pallas_call x5, Pallas kernels, project(): pl.pallas_call(project_kernel, grid=(width // HD,), in_specs=[pl.BlockSpe...  20.1 us
    ppermute x5, waiting for transfers between devices, on_device(): products.append((column, mine, lax.ppermute(other, 'dp', x_swap)))  19.4 us
    all_to_all x1, starting transfers between devices, on_device(): lax.all_to_all(filled, 'dp', split_axis=0, concat_axis=0, tiled=True)  14.9 us
    ppermute x3, waiting for transfers between devices, tensor_shift(): return lax.ppermute(value, 'tensor', pairs)  14.8 us
  transfers between devices with their start and end apart: 18, of which 11 were waited for; matrix products, arithmetic and copies ran while one was open for 2% of the time, Pallas kernels for 21%

profile of v7, /device:TPU:0, one launch (start us, length us, event | category | flops | bytes accessed | tf_op | source)
XLA Modules:
  0.0 295.1 jit_solution(15664177736847910963)
XLA Ops:
  7.2 3.1 %predict_first.1.rest_0_ = bf16[256,2560]{1,0:T(8,128)(2,1)} custom-call(bf16[2,256,2048]{2,1,0:T(8,128)(2,1)} %weights.3, f32[2,256,2048]{2,1,0:T(8,128)} %velocity.3), custom_call_target="tpu_custom_call" | custom-call | flops 655360 | bytes 5242880 | tf_op jit(solution)/shard_map/predict_first/pallas_call | solution.py:101
  11.3 0.8 reshape.99
  12.4 50.3 %all_to_all.25.rest_1_ = bf16[16,128,256]{2,1,0:T(8,128)(2,1)} all-to-all(bf16[16,128,256]{2,1,0:T(8,128)(2,1)S(1)} %bitcast.48), channel_id=1, replica_groups=mesh['dp'=16,'tensor'=2] {'dp'}, dimensions={0} | all-to-all | bytes 2097152 | tf_op jit(solution)/shard_map/all_to_all | solution.py:411
  62.7 3.4 %predict.1 = bf16[256,1536]{1,0:T(8,128)(2,1)} custom-call(bf16[2,256,2048]{2,1,0:T(8,128)(2,1)} %weights.3, f32[2,256,2048]{2,1,0:T(8,128)} %velocity.3, bf16[256,2560]{1,0:T(8,128)(2,1)} %predict_first.1.rest_0_, bf16[16,128,256]{2,1,0:T(8,128)(2,1)} %all_to_all.25.rest_1_), custom_call_target="tpu_custom_call" | custom-call | flops 393216 | bytes 3145728 | tf_op jit(solution)/shard_map/predict/pallas_call | solution.py:125
  66.2 1.6 collective-permute-start
  67.9 0.7 all_to_all.20
  68.6 14.9 %all-to-all-start = ((bf16[16,16,1]{1,2,0:T(2,128)(2,1)}), bf16[16,16,1]{1,2,0:T(2,128)(2,1)S(1)}, u32[]{:S(2)}, u32[]{:S(2)}) async-start(bf16[16,16,1]{1,2,0:T(2,128)(2,1)} %all_to_all.20), calls=%async_computation | async-start | bytes 16384 | tf_op jit(solution)/shard_map/all_to_all | solution.py:420
  83.6 6.4 %all-to-all-done = bf16[16,16,1]{1,2,0:T(2,128)(2,1)S(1)} async-done(((bf16[16,16,1]{1,2,0:T(2,128)(2,1)}), bf16[16,16,1]{1,2,0:T(2,128)(2,1)S(1)}, u32[]{:S(2)}, u32[]{:S(2)}) %all-to-all-start) | async-done | bytes 544 | tf_op jit(solution)/shard_map/all_to_all | solution.py:420
  90.3 0.8 arrange.1.rows
  91.1 41.3 %all-gather.5.cloned.1.call-done.weights.refs_2_.refs_5_.refs_8_ = bf16[2048,2560]{1,0:T(8,128)(2,1)} async-done(((bf16[256,2560]{1,0:T(8,128)(2,1)}), bf16[2048,2560]{1,0:T(8,128)(2,1)}) %all-gather.5.cloned.1.call-update) | async-done | bytes 10485776 | tf_op jit(solution)/shard_map/all_gather | solution.py:416
  132.4 4.7 %project.7 = (f32[256,1024]{1,0:T(8,128)S(1)}, bf16[256,1024]{1,0:T(8,128)(2,1)S(1)}) custom-call(bf16[512,2048]{1,0:T(8,128)(2,1)S(1)} %arrange.1.rows, bf16[2048,2560]{1,0:T(8,128)(2,1)} %all-gather.5.cloned.1.call-done.weights.refs_2_.refs_5_.refs_8_), custom_call_target="tpu_custom_call" | custom-call | flops 2147483648 | bytes 7864320 | tf_op jit(solution)/shard_map/project/pallas_call | solution.py:183
  137.1 1.5 collective-permute-start.3
  138.7 5.2 %project.6 = (f32[256,1024]{1,0:T(8,128)S(1)}, bf16[256,1024]{1,0:T(8,128)(2,1)S(1)}) custom-call(bf16[512,2048]{1,0:T(8,128)(2,1)S(1)} %arrange.1.rows, bf16[2048,2560]{1,0:T(8,128)(2,1)} %all-gather.5.cloned.1.call-done.weights.refs_2_.refs_5_.refs_8_), custom_call_target="tpu_custom_call" | custom-call | flops 2147483648 | bytes 7864320 | tf_op jit(solution)/shard_map/project/pallas_call | solution.py:183
  144.8 7.1 %collective-permute-done.3.received = bf16[256,1024]{1,0:T(8,128)(2,1)S(1)} collective-permute-done((bf16[256,1024]{1,0:T(8,128)(2,1)S(1)}, bf16[256,1024]{1,0:T(8,128)(2,1)S(1)}, u32[]{:S(2)}, u32[]{:S(2)}) %collective-permute-start.3) | collective-permute-done | bytes 524320 | tf_op jit(solution)/shard_map/ppermute | solution.py:444
  151.9 4.8 %attend.5 = (bf16[1024,2048]{1,0:T(8,128)(2,1)}, bf16[256,1024]{1,0:T(8,128)(2,1)S(1)}) custom-call(s32[1]{0:T(128)S(6)} %copy.95.live, f32[256,1]{1,0:T(8,128)S(1)} %reshape.115._.usable, bf16[1024,2048]{1,0:T(8,128)(2,1)} %queries.9, bf16[1024,2048]{1,0:T(8,128)(2,1)} %grads.9, f32[256,1024]{1,0:T(8,128)S(1)} %get-tuple-element.34.mine, ...), custom_call_target="tpu_custom_call" | custom-call | flops 1342177280 | bytes 5767168 | tf_op jit(solution)/shard_map/attend/pallas_call | solution.py:268
  156.8 1.5 collective-permute-start.4
  158.2 2.7 project.5
  161.0 0.6 collective-permute-start.1
  161.6 1.6 collective-permute-done.2.received
  163.2 5.1 %attend.6 = (bf16[1024,2048]{1,0:T(8,128)(2,1)}, bf16[256,1024]{1,0:T(8,128)(2,1)}) custom-call(s32[1]{0:T(128)S(6)} %copy.95.live, f32[256,1]{1,0:T(8,128)S(1)} %reshape.115._.usable, bf16[1024,2048]{1,0:T(8,128)(2,1)} %queries.9, bf16[1024,2048]{1,0:T(8,128)(2,1)} %grads.9, ...), custom_call_target="tpu_custom_call", output_to_operand_aliasing={{0}: (6, {})} | custom-call | flops 1342177280 | bytes 5767168 | tf_op jit(solution)/shard_map/attend/pallas_call | solution.py:268
  168.3 1.4 collective-permute-start.7
  169.7 10.3 %collective-permute-done.1.received = bf16[256,512]{1,0:T(8,128)(2,1)S(1)} collective-permute-done((bf16[256,512]{1,0:T(8,128)(2,1)S(1)}, bf16[256,512]{1,0:T(8,128)(2,1)S(1)}, u32[]{:S(2)}, u32[]{:S(2)}) %collective-permute-start.1) | collective-permute-done | bytes 262176 | tf_op jit(solution)/shard_map/ppermute | solution.py:444
  180.0 3.2 %attend.7 = (bf16[1024,2048]{1,0:T(8,128)(2,1)}, bf16[256,512]{1,0:T(8,128)(2,1)S(1)}) custom-call(s32[1]{0:T(128)S(6)} %copy.95.live, f32[256,1]{1,0:T(8,128)S(1)} %reshape.115._.usable, bf16[1024,2048]{1,0:T(8,128)(2,1)S(1)} %copy-done.2, bf16[1024,2048]{1,0:T(8,128)(2,1)} %grads.9, ...), custom_call_target="tpu_custom_call", output_to_operand_aliasing={{0}: (6, {})} | custom-call | flops 671088640 | bytes 2883584 | tf_op jit(solution)/shard_map/attend/pallas_call | solution.py:268
  183.2 1.5 collective-permute-start.8
  184.7 13.3 %all-gather.3.cloned.1.call-done.weights.refs_1_.refs_3_ = bf16[2048,1536]{1,0:T(8,128)(2,1)} async-done(((bf16[256,1536]{1,0:T(8,128)(2,1)}), bf16[2048,1536]{1,0:T(8,128)(2,1)}) %all-gather.3.cloned.1.call-update) | async-done | bytes 6291472 | tf_op jit(solution)/shard_map/all_gather | solution.py:416
  197.9 2.7 project.9
  200.7 1.5 collective-permute-start.6
  202.2 4.7 %project.8 = (f32[256,1024]{1,0:T(8,128)S(1)}, bf16[256,1024]{1,0:T(8,128)(2,1)S(1)}) custom-call(bf16[512,2048]{1,0:T(8,128)(2,1)S(1)} %arrange.1.rows, bf16[2048,1536]{1,0:T(8,128)(2,1)} %all-gather.3.cloned.1.call-done.weights.refs_1_.refs_3_, bf16[256,512]{1,0:T(8,128)(2,1)S(1)} %get-tuple-element.39.rest_0_.refs_6_), custom_call_target="tpu_custom_call" | custom-call | flops 2147483648 | bytes 7864320 | tf_op jit(solution)/shard_map/project/pallas_call | solution.py:183
  207.6 9.5 %spread.5 = (bf16[4,2,2,256,256]{4,3,2,1,0:T(8,128)(2,1)S(1)}, f32[8,128]{1,0:T(8,128)S(1)}) custom-call(s32[4]{0:T(128)S(1)} %pad_add_fusion.pos, bf16[256,1024]{1,0:T(8,128)(2,1)S(1)} %copy-done.5, bf16[256,1024]{1,0:T(8,128)(2,1)S(1)} %collective-permute-done.4.rest_1_.refs_1_, ...), custom_call_target="tpu_custom_call" | custom-call | flops 5368709120 | bytes 18874368 | tf_op jit(solution)/shard_map/spread/pallas_call | solution.py:358
  217.1 3.3 %attend.8 = (bf16[1024,2048]{1,0:T(8,128)(2,1)}, bf16[256,512]{1,0:T(8,128)(2,1)}) custom-call(s32[1]{0:T(128)S(6)} %copy.95.live, f32[256,1]{1,0:T(8,128)S(1)} %reshape.115._.usable, bf16[1024,2048]{1,0:T(8,128)(2,1)S(1)} %copy-done.3, bf16[1024,2048]{1,0:T(8,128)(2,1)} %grads.9, ...), custom_call_target="tpu_custom_call", output_to_operand_aliasing={{0}: (6, {})} | custom-call | flops 671088640 | bytes 2883584 | tf_op jit(solution)/shard_map/attend/pallas_call | solution.py:268
  220.8 4.8 %attend.9 = (bf16[1024,2048]{1,0:T(8,128)(2,1)}, bf16[256,1024]{1,0:T(8,128)(2,1)S(1)}) custom-call(s32[1]{0:T(128)S(6)} %copy.95.live, f32[256,1]{1,0:T(8,128)S(1)} %reshape.115._.usable, bf16[1024,2048]{1,0:T(8,128)(2,1)} %queries.9, bf16[1024,2048]{1,0:T(8,128)(2,1)} %grads.9, ...), custom_call_target="tpu_custom_call", output_to_operand_aliasing={{0}: (6, {})} | custom-call | flops 1342177280 | bytes 5767168 | tf_op jit(solution)/shard_map/attend/pallas_call | solution.py:268
  225.6 3.3 %spread.6 = (bf16[2,2,1,256,256]{4,3,2,1,0:T(8,128)(2,1)S(1)}, f32[8,128]{1,0:T(8,128)S(1)}) custom-call(s32[4]{0:T(128)S(1)} %pad_add_fusion.pos, bf16[256,512]{1,0:T(8,128)(2,1)} %get-tuple-element.49.refs_0_, bf16[2048,1536]{1,0:T(8,128)(2,1)} %all-gather.3.cloned.1.call-done.weights.refs_1_.refs_3_, bf16[256,1024]{1,0:T(8,128)(2,1)S(1)} %get-tuple-element.50.refs_2_, ...), custom_call_target="tpu_custom_call" | custom-call | flops 805306368 | bytes 5242880 | tf_op jit(solution)/shard_map/spread/pallas_call | solution.py:358
  229.0 1.6 collective-permute-start.9
  230.5 1.2 collective-permute-start.11
  231.7 0.8 collective-permute-start.10
  232.5 3.7 %spread.7 = (f32[2,2,1,256,256]{4,3,2,1,0:T(8,128)S(1)}, f32[8,128]{1,0:T(8,128)}) custom-call(s32[4]{0:T(128)S(1)} %pad_add_fusion.pos, bf16[256,512]{1,0:T(8,128)(2,1)} %get-tuple-element.49.refs_0_, bf16[2048,1536]{1,0:T(8,128)(2,1)} %all-gather.3.cloned.1.call-done.weights.refs_1_.refs_3_, bf16[256,1024]{1,0:T(8,128)(2,1)S(1)} %get-tuple-element.50.refs_2_, ...), custom_call_target="tpu_custom_call" | custom-call | flops 805306368 | bytes 5242880 | tf_op jit(solution)/shard_map/spread/pallas_call | solution.py:358
  236.2 6.4 %collective-permute-done.9 = bf16[2,2,1,256,256]{4,3,2,1,0:T(8,128)(2,1)S(1)} collective-permute-done((bf16[2,2,1,256,256]{4,3,2,1,0:T(8,128)(2,1)S(1)}, bf16[2,2,1,256,256]{4,3,2,1,0:T(8,128)(2,1)S(1)}, u32[]{:S(2)}, u32[]{:S(2)}) %collective-permute-start.9) | collective-permute-done | bytes 524320 | tf_op jit(solution)/shard_map/ppermute | solution.py:403
  242.8 0.9 copy.67
  243.7 4.3 %all-to-all-start.2 = ((bf16[16,64,256]{2,1,0:T(8,128)(2,1)}), bf16[16,64,256]{2,1,0:T(8,128)(2,1)}, u32[]{:S(2)}, u32[]{:S(2)}) async-start(bf16[16,64,256]{2,1,0:T(8,128)(2,1)} %bitcast.51), calls=%async_computation.2 | async-start | bytes 1048576 | tf_op jit(solution)/shard_map/all_to_all | solution.py:488
  247.9 1.5 collective-permute-done.10.refs_0_
  249.5 3.3 %spread.8 = (bf16[2,2,1,256,256]{4,3,2,1,0:T(8,128)(2,1)S(1)}, f32[8,128]{1,0:T(8,128)S(1)}) custom-call(s32[4]{0:T(128)S(1)} %pad_add_fusion.pos, bf16[256,512]{1,0:T(8,128)(2,1)S(1)} %collective-permute-done.10.refs_0_, bf16[2048,1536]{1,0:T(8,128)(2,1)} %all-gather.3.cloned.1.call-done.weights.refs_1_.refs_3_, ...), custom_call_target="tpu_custom_call" | custom-call | flops 805306368 | bytes 5242880 | tf_op jit(solution)/shard_map/spread/pallas_call | solution.py:358
  253.3 3.6 %spread.9 = (f32[2,2,1,256,256]{4,3,2,1,0:T(8,128)S(1)}, f32[8,128]{1,0:T(8,128)}) custom-call(s32[4]{0:T(128)S(1)} %pad_add_fusion.pos, bf16[256,512]{1,0:T(8,128)(2,1)S(1)} %collective-permute-done.10.refs_0_, bf16[2048,1536]{1,0:T(8,128)(2,1)} %all-gather.3.cloned.1.call-done.weights.refs_1_.refs_3_, ...), custom_call_target="tpu_custom_call" | custom-call | flops 805306368 | bytes 5242880 | tf_op jit(solution)/shard_map/spread/pallas_call | solution.py:358
  257.0 8.4 %collective-permute-done.12 = bf16[2,2,1,256,256]{4,3,2,1,0:T(8,128)(2,1)S(1)} collective-permute-done((bf16[2,2,1,256,256]{4,3,2,1,0:T(8,128)(2,1)S(1)}, bf16[2,2,1,256,256]{4,3,2,1,0:T(8,128)(2,1)S(1)}, u32[]{:S(2)}, u32[]{:S(2)}) %collective-permute-start.12) | collective-permute-done | bytes 524320 | tf_op jit(solution)/shard_map/ppermute | solution.py:403
  265.5 0.9 copy.69
  266.4 5.8 %all-to-all-start.3 = ((bf16[16,64,256]{2,1,0:T(8,128)(2,1)}), bf16[16,64,256]{2,1,0:T(8,128)(2,1)S(1)}, u32[]{:S(2)}, u32[]{:S(2)}) async-start(bf16[16,64,256]{2,1,0:T(8,128)(2,1)} %bitcast.19), calls=%async_computation.3 | async-start | bytes 1048576 | tf_op jit(solution)/shard_map/all_to_all | solution.py:488
  272.4 1.5 fusion.4
  273.9 12.8 %all-to-all-done.3 = bf16[16,64,256]{2,1,0:T(8,128)(2,1)S(1)} async-done(((bf16[16,64,256]{2,1,0:T(8,128)(2,1)}), bf16[16,64,256]{2,1,0:T(8,128)(2,1)S(1)}, u32[]{:S(2)}, u32[]{:S(2)}) %all-to-all-start.3) | async-done | bytes 524320 | tf_op jit(solution)/shard_map/all_to_all | solution.py:488
  287.2 1.0 copy.72
  (51 shorter events, 4.8 us)
Async XLA Ops:
  7.2 3.7 %copy-start = (bf16[128,2048]{1,0:T(8,128)(2,1)S(1)}, bf16[128,2048]{1,0:T(8,128)(2,1)}, u32[]{:S(2)}) copy-start(bf16[128,2048]{1,0:T(8,128)(2,1)} %param.10) | copy-start | bytes 1572868
  7.2 3.3 %copy-start.7 = (s32[128,1]{0,1:T(1,128)S(1)}, s32[128,1]{0,1:T(1,128)}, u32[]{:S(2)}) copy-start(s32[128,1]{0,1:T(1,128)} %param.11) | copy-start | bytes 1540
  7.2 125.2 %all-gather.5.cloned.1.call-start = ((), (), s32[]{:S(2)}) async-start(), calls=%async_computation.5 | async-start | bytes 11796480 | tf_op jit(solution)/shard_map/all_gather | solution.py:416
  10.4 187.5 %all-gather.3.cloned.1.call-start = ((), (), s32[]{:S(2)}) async-start(), calls=%async_computation.4 | async-start | bytes 7077888 | tf_op jit(solution)/shard_map/all_gather | solution.py:416
  62.7 3.4 %copy-start.6 = (bf16[16,128,256]{2,1,0:T(8,128)(2,1)S(1)}, bf16[16,128,256]{2,1,0:T(8,128)(2,1)}, u32[]{:S(2)}) copy-start(bf16[16,128,256]{2,1,0:T(8,128)(2,1)} %all_to_all.25.rest_1_) | copy-start | bytes 3145732
  66.2 23.9 %collective-permute-start = (bf16[2,2,2,256,256]{4,3,2,1,0:T(8,128)(2,1)S(1)}, bf16[2,2,2,256,256]{4,3,2,1,0:T(8,128)(2,1)S(1)}, u32[]{:S(2)}, u32[]{:S(2)}) collective-permute-start(bf16[2,2,2,256,256]{4,3,2,1,0:T(8,128)(2,1)S(1)} %bitcast.49), channel_id=1, source_target_pairs={{0,1},{1,0},{2,3},{3,2},{4,5},{5,4},{6,7},{7,6},{8,9},{9,8},{10,11... | collective-permute-start | bytes 3145736 | tf_op jit(solution)/shard_map/ppermute | solution.py:403
  68.6 21.3 %all-to-all-start = ((bf16[16,16,1]{1,2,0:T(2,128)(2,1)}), bf16[16,16,1]{1,2,0:T(2,128)(2,1)S(1)}, u32[]{:S(2)}, u32[]{:S(2)}) async-start(bf16[16,16,1]{1,2,0:T(2,128)(2,1)} %all_to_all.20), calls=%async_computation | async-start | bytes 16384 | tf_op jit(solution)/shard_map/all_to_all | solution.py:420
  137.1 14.8 %collective-permute-start.3 = (bf16[256,1024]{1,0:T(8,128)(2,1)S(1)}, bf16[256,1024]{1,0:T(8,128)(2,1)S(1)}, u32[]{:S(2)}, u32[]{:S(2)}) collective-permute-start(bf16[256,1024]{1,0:T(8,128)(2,1)S(1)} %get-tuple-element.35), channel_id=1, source_target_pairs={{0,4},{2,6},{4,0},{6,2},{8,12},{10,14},{12,8},{14,10},{16,20},{18,... | collective-permute-start | bytes 1572872 | tf_op jit(solution)/shard_map/ppermute | solution.py:444
  143.8 19.4 %collective-permute-start.2 = (bf16[256,1024]{1,0:T(8,128)(2,1)S(1)}, bf16[256,1024]{1,0:T(8,128)(2,1)S(1)}, u32[]{:S(2)}, u32[]{:S(2)}) collective-permute-start(bf16[256,1024]{1,0:T(8,128)(2,1)S(1)} %get-tuple-element.33), channel_id=1, source_target_pairs={{0,4},{2,6},{4,0},{6,2},{8,12},{10,14},{12,8},{14,10},{16,20},{18,... | collective-permute-start | bytes 1572872 | tf_op jit(solution)/shard_map/ppermute | solution.py:444
  156.8 4.2 %copy-start.4 = (bf16[256,1024]{1,0:T(8,128)(2,1)}, bf16[256,1024]{1,0:T(8,128)(2,1)S(1)}, u32[]{:S(2)}) copy-start(bf16[256,1024]{1,0:T(8,128)(2,1)S(1)} %get-tuple-element.38.refs_0_) | copy-start | bytes 1572868
  156.8 23.3 %collective-permute-start.4 = (bf16[256,1024]{1,0:T(8,128)(2,1)S(1)}, bf16[256,1024]{1,0:T(8,128)(2,1)S(1)}, u32[]{:S(2)}, u32[]{:S(2)}) collective-permute-start(bf16[256,1024]{1,0:T(8,128)(2,1)S(1)} %get-tuple-element.38.refs_0_), channel_id=1, source_target_pairs={{0,4},{2,6},{4,0},{6,2},{8,12},{10,14},{12,8},{14,10},{16,20},{18,... | collective-permute-start | bytes 1572872 | tf_op jit(solution)/shard_map/ppermute | solution.py:458
  161.0 19.1 %collective-permute-start.1 = (bf16[256,512]{1,0:T(8,128)(2,1)S(1)}, bf16[256,512]{1,0:T(8,128)(2,1)S(1)}, u32[]{:S(2)}, u32[]{:S(2)}) collective-permute-start(bf16[256,512]{1,0:T(8,128)(2,1)S(1)} %get-tuple-element.31), channel_id=1, source_target_pairs={{0,4},{2,6},{4,0},{6,2},{8,12},{10,14},{12,8},{14,10},{16,20},{18,... | collective-permute-start | bytes 786440 | tf_op jit(solution)/shard_map/ppermute | solution.py:444
  163.2 16.9 %copy-start.2 = (bf16[1024,2048]{1,0:T(8,128)(2,1)S(1)}, bf16[1024,2048]{1,0:T(8,128)(2,1)}, u32[]{:S(2)}) copy-start(bf16[1024,2048]{1,0:T(8,128)(2,1)} %queries.9) | copy-start | bytes 12582916
  168.3 39.3 %collective-permute-start.7 = (bf16[256,1024]{1,0:T(8,128)(2,1)}, bf16[256,1024]{1,0:T(8,128)(2,1)S(1)}, u32[]{:S(2)}, u32[]{:S(2)}) collective-permute-start(bf16[256,1024]{1,0:T(8,128)(2,1)} %get-tuple-element.45.refs_3_), channel_id=1, source_target_pairs={{0,4},{2,6},{4,0},{6,2},{8,12},{10,14},{12,8},{14,10},{16,20},{18,... | collective-permute-start | bytes 1572872 | tf_op jit(solution)/shard_map/ppermute | solution.py:458
  183.2 24.4 %collective-permute-start.8 = (bf16[256,512]{1,0:T(8,128)(2,1)S(1)}, bf16[256,512]{1,0:T(8,128)(2,1)}, u32[]{:S(2)}, u32[]{:S(2)}) collective-permute-start(bf16[256,512]{1,0:T(8,128)(2,1)S(1)} %get-tuple-element.39.rest_0_.refs_6_), channel_id=1, source_target_pairs={{0,4},{2,6},{4,0},{6,2},{8,12},{10,14},{12,8},{14,10},{16,20},{18,... | collective-permute-start | bytes 786440 | tf_op jit(solution)/shard_map/ppermute | solution.py:458
  200.7 6.9 %copy-start.5 = (bf16[256,1024]{1,0:T(8,128)(2,1)S(1)}, bf16[256,1024]{1,0:T(8,128)(2,1)}, u32[]{:S(2)}) copy-start(bf16[256,1024]{1,0:T(8,128)(2,1)} %copy-done.4) | copy-start | bytes 1572868
  200.7 16.4 %collective-permute-start.6 = (bf16[256,512]{1,0:T(8,128)(2,1)S(1)}, bf16[256,512]{1,0:T(8,128)(2,1)S(1)}, u32[]{:S(2)}, u32[]{:S(2)}) collective-permute-start(bf16[256,512]{1,0:T(8,128)(2,1)S(1)} %get-tuple-element.43), channel_id=1, source_target_pairs={{0,4},{2,6},{4,0},{6,2},{8,12},{10,14},{12,8},{14,10},{16,20},{18,... | collective-permute-start | bytes 786440 | tf_op jit(solution)/shard_map/ppermute | solution.py:444
  206.9 10.2 %copy-start.3 = (bf16[1024,2048]{1,0:T(8,128)(2,1)S(1)}, bf16[1024,2048]{1,0:T(8,128)(2,1)}, u32[]{:S(2)}) copy-start(bf16[1024,2048]{1,0:T(8,128)(2,1)} %queries.9) | copy-start | bytes 12582916
  207.0 13.9 %collective-permute-start.5 = (bf16[256,1024]{1,0:T(8,128)(2,1)S(1)}, bf16[256,1024]{1,0:T(8,128)(2,1)S(1)}, u32[]{:S(2)}, u32[]{:S(2)}) collective-permute-start(bf16[256,1024]{1,0:T(8,128)(2,1)S(1)} %get-tuple-element.41), channel_id=1, source_target_pairs={{0,4},{2,6},{4,0},{6,2},{8,12},{10,14},{12,8},{14,10},{16,20},{18,... | collective-permute-start | bytes 1572872 | tf_op jit(solution)/shard_map/ppermute | solution.py:444
  229.0 13.7 %collective-permute-start.9 = (bf16[2,2,1,256,256]{4,3,2,1,0:T(8,128)(2,1)S(1)}, bf16[2,2,1,256,256]{4,3,2,1,0:T(8,128)(2,1)S(1)}, u32[]{:S(2)}, u32[]{:S(2)}) collective-permute-start(bf16[2,2,1,256,256]{4,3,2,1,0:T(8,128)(2,1)S(1)} %get-tuple-element.54), channel_id=1, source_target_pairs={{0,1},{1,0},{2,3},{3,2},{4,5},{5,4},{6,7},{7,6},{8,9},{9,8},{10,11... | collective-permute-start | bytes 1572872 | tf_op jit(solution)/shard_map/ppermute | solution.py:403
  230.5 18.9 %collective-permute-start.11 = (bf16[256,1024]{1,0:T(8,128)(2,1)S(1)}, bf16[256,1024]{1,0:T(8,128)(2,1)S(1)}, u32[]{:S(2)}, u32[]{:S(2)}) collective-permute-start(bf16[256,1024]{1,0:T(8,128)(2,1)S(1)} %get-tuple-element.50.refs_2_), channel_id=1, source_target_pairs={{0,4},{2,6},{4,0},{6,2},{8,12},{10,14},{12,8},{14,10},{16,20},{18,... | collective-permute-start | bytes 1572872 | tf_op jit(solution)/shard_map/ppermute | solution.py:458
  231.7 17.7 %collective-permute-start.10 = (bf16[256,512]{1,0:T(8,128)(2,1)}, bf16[256,512]{1,0:T(8,128)(2,1)S(1)}, u32[]{:S(2)}, u32[]{:S(2)}) collective-permute-start(bf16[256,512]{1,0:T(8,128)(2,1)} %get-tuple-element.49.refs_0_), channel_id=1, source_target_pairs={{0,4},{2,6},{4,0},{6,2},{8,12},{10,14},{12,8},{14,10},{16,20},{18,... | collective-permute-start | bytes 786440 | tf_op jit(solution)/shard_map/ppermute | solution.py:458
  243.7 22.7 %all-to-all-start.2 = ((bf16[16,64,256]{2,1,0:T(8,128)(2,1)}), bf16[16,64,256]{2,1,0:T(8,128)(2,1)}, u32[]{:S(2)}, u32[]{:S(2)}) async-start(bf16[16,64,256]{2,1,0:T(8,128)(2,1)} %bitcast.51), calls=%async_computation.2 | async-start | bytes 1048576 | tf_op jit(solution)/shard_map/all_to_all | solution.py:488
  252.7 12.6 %collective-permute-start.12 = (bf16[2,2,1,256,256]{4,3,2,1,0:T(8,128)(2,1)S(1)}, bf16[2,2,1,256,256]{4,3,2,1,0:T(8,128)(2,1)S(1)}, u32[]{:S(2)}, u32[]{:S(2)}) collective-permute-start(bf16[2,2,1,256,256]{4,3,2,1,0:T(8,128)(2,1)S(1)} %get-tuple-element.57), channel_id=1, source_target_pairs={{0,1},{1,0},{2,3},{3,2},{4,5},{5,4},{6,7},{7,6},{8,9},{9,8},{10,11... | collective-permute-start | bytes 1572872 | tf_op jit(solution)/shard_map/ppermute | solution.py:403
  266.4 20.3 %all-to-all-start.3 = ((bf16[16,64,256]{2,1,0:T(8,128)(2,1)}), bf16[16,64,256]{2,1,0:T(8,128)(2,1)S(1)}, u32[]{:S(2)}, u32[]{:S(2)}) async-start(bf16[16,64,256]{2,1,0:T(8,128)(2,1)} %bitcast.19), calls=%async_computation.3 | async-start | bytes 1048576 | tf_op jit(solution)/shard_map/all_to_all | solution.py:488
  272.4 15.9 %copy-start.1 = (bf16[128,2048]{1,0:T(8,128)(2,1)S(1)}, bf16[128,2048]{1,0:T(8,128)(2,1)}, u32[]{:S(2)}) copy-start(bf16[128,2048]{1,0:T(8,128)(2,1)} %param.10) | copy-start | bytes 1572868
Sparse Core Ops, SparseCore 0:
  10.5 121.8 all-gather.4
  134.0 63.8 all-gather.2
